TPU v7x, 32 devices: a whole 2x2x4 slice. The times are simulated.
32 devices in a mesh: dp: 8 (over y, x, core), blk: 4 (over z).
Axes of the slice: x: 2, y: 2, z: 4, core: 2. Of those that a mesh axis runs over, the one named last changes fastest.
Arguments:
- tokens: bfloat16 [24, 1536, 768], P('dp', 'blk'), may hold values from -6 to 6
- counts: int32 [24], P('dp'), may hold values from 864 to 1536, as said below
- ln1_gain: bfloat16 [768], replicated, may hold values from 0.5 to 1.5
- ln1_shift: bfloat16 [768], replicated, may hold values from -0.59765625 to 0.59765625
- w_qkv: bfloat16 [768, 2304], replicated, may hold values from -0.21875 to 0.21875
- bias_q: bfloat16 [768], replicated, may hold values from -0.59765625 to 0.59765625
- bias_v: bfloat16 [768], replicated, may hold values from -0.23925781 to 0.23925781
- w_out: bfloat16 [768, 768], replicated, may hold values from -4 to 4
- bias_out: bfloat16 [768], replicated, may hold values from -0.59765625 to 0.59765625
- ln2_gain: bfloat16 [768], replicated, may hold values from 0.5 to 1.5
- ln2_shift: bfloat16 [768], replicated, may hold values from -0.59765625 to 0.59765625
- w_fc1: bfloat16 [768, 3072], replicated, may hold values from -0.21875 to 0.21875
- bias_fc1: bfloat16 [3072], replicated, may hold values from -0.59765625 to 0.59765625
- w_fc2: bfloat16 [3072, 768], replicated, may hold values from -0.109375 to 0.109375
- bias_fc2: bfloat16 [768], replicated, may hold values from -0.59765625 to 0.59765625
- cotangent: bfloat16 [24, 1536, 768], P('dp', 'blk'), may hold values from -6 to 6
Outputs:
- output: bfloat16 [24, 1536, 768], P('dp', 'blk')
- input_grad: float32 [24, 1536, 768], P('dp', 'blk')
- grad_ln1_gain: float32 [768], replicated
- grad_ln1_shift: float32 [768], replicated
- grad_w_qkv: float32 [768, 2304], replicated
- grad_bias_q: float32 [768], replicated
- grad_bias_v: float32 [768], replicated
- grad_w_out: float32 [768, 768], replicated
- grad_bias_out: float32 [768], replicated
- grad_ln2_gain: float32 [768], replicated
- grad_ln2_shift: float32 [768], replicated
- grad_w_fc1: float32 [768, 3072], replicated
- grad_bias_fc1: float32 [3072], replicated
- grad_w_fc2: float32 [3072, 768], replicated
- grad_bias_fc2: float32 [768], replicated
Inputs may be any that keep to these rules, and one draw needn't show every extreme that they name: `counts`: each cube holds its valid tokens first; in each index of dp exactly the ceiling of half of its 3 cubes hold 1536, the others 864.
All inputs are finite; a program needn't handle non-finite values.
Results may differ from a plain program's by a relative error of at most 0.02.
Values may be sent and summed in bfloat16 or wider, within the bound.
No kernel may reach another device: no remote copies, remote signals or barrier semaphores. Data moves between devices by JAX's collectives and lax.ppermute only.
A program may use at most 256 MiB of HBM per device.

v0:
```python
import functools
import math

import jax
import jax.numpy as jnp
from jax import lax
from jax.experimental import pallas as pl
from jax.experimental.pallas import tpu as pltpu
from jax.sharding import PartitionSpec as P

HEADS = 12
HD = 64
SHORT = 864


NORM_EPS = 1e-06
MASK_LOW = -1e30


def norm_rows(values, gain, shift):
    centre = values - jnp.mean(values, axis=-1, keepdims=True)
    spread = jnp.mean(centre * centre, axis=-1, keepdims=True)
    return centre * lax.rsqrt(spread + NORM_EPS) * gain + shift


def gelu_exact(values):
    return jax.nn.gelu(values, approximate=False)


def cube_valid(counts, offset, length):
    places = offset + jnp.arange(length, dtype=jnp.int32)
    return places[None, :] < counts[:, None]


def total_every(parts):
    split = (
        lax.psum_scatter(
            parts[0].astype(jnp.bfloat16), "blk", scatter_dimension=0, tiled=True
        ).astype(jnp.float32),
        lax.psum_scatter(
            parts[1].astype(jnp.bfloat16), "blk", scatter_dimension=0, tiled=True
        ).astype(jnp.float32),
        lax.psum_scatter(
            parts[2].astype(jnp.bfloat16), "blk", scatter_dimension=0, tiled=True
        ).astype(jnp.float32),
        lax.psum_scatter(
            parts[3].astype(jnp.bfloat16), "blk", scatter_dimension=0, tiled=True
        ).astype(jnp.float32),
        lax.psum_scatter(
            parts[4].astype(jnp.bfloat16), "blk", scatter_dimension=0, tiled=True
        ).astype(jnp.float32),
        lax.psum_scatter(
            parts[5].astype(jnp.bfloat16), "blk", scatter_dimension=0, tiled=True
        ).astype(jnp.float32),
        lax.psum_scatter(
            parts[6].astype(jnp.bfloat16), "blk", scatter_dimension=0, tiled=True
        ).astype(jnp.float32),
        lax.psum_scatter(
            parts[7].astype(jnp.bfloat16), "blk", scatter_dimension=0, tiled=True
        ).astype(jnp.float32),
        lax.psum_scatter(
            parts[8].astype(jnp.bfloat16), "blk", scatter_dimension=0, tiled=True
        ).astype(jnp.float32),
        lax.psum_scatter(
            parts[9].astype(jnp.bfloat16), "blk", scatter_dimension=0, tiled=True
        ).astype(jnp.float32),
        lax.psum_scatter(
            parts[10].astype(jnp.bfloat16), "blk", scatter_dimension=0, tiled=True
        ).astype(jnp.float32),
        lax.psum_scatter(
            parts[11].astype(jnp.bfloat16), "blk", scatter_dimension=0, tiled=True
        ).astype(jnp.float32),
        lax.psum_scatter(
            parts[12].astype(jnp.bfloat16), "blk", scatter_dimension=0, tiled=True
        ).astype(jnp.float32),
    )
    summed = (
        lax.psum(split[0].astype(jnp.bfloat16), "dp").astype(jnp.float32),
        lax.psum(split[1].astype(jnp.bfloat16), "dp").astype(jnp.float32),
        lax.psum(split[2].astype(jnp.bfloat16), "dp").astype(jnp.float32),
        lax.psum(split[3].astype(jnp.bfloat16), "dp").astype(jnp.float32),
        lax.psum(split[4].astype(jnp.bfloat16), "dp").astype(jnp.float32),
        lax.psum(split[5].astype(jnp.bfloat16), "dp").astype(jnp.float32),
        lax.psum(split[6].astype(jnp.bfloat16), "dp").astype(jnp.float32),
        lax.psum(split[7].astype(jnp.bfloat16), "dp").astype(jnp.float32),
        lax.psum(split[8].astype(jnp.bfloat16), "dp").astype(jnp.float32),
        lax.psum(split[9].astype(jnp.bfloat16), "dp").astype(jnp.float32),
        lax.psum(split[10].astype(jnp.bfloat16), "dp").astype(jnp.float32),
        lax.psum(split[11].astype(jnp.bfloat16), "dp").astype(jnp.float32),
        lax.psum(split[12].astype(jnp.bfloat16), "dp").astype(jnp.float32),
    )
    return (
        lax.all_gather(summed[0].astype(jnp.bfloat16), "blk", axis=0, tiled=True).astype(
            jnp.float32
        ),
        lax.all_gather(summed[1].astype(jnp.bfloat16), "blk", axis=0, tiled=True).astype(
            jnp.float32
        ),
        lax.all_gather(summed[2].astype(jnp.bfloat16), "blk", axis=0, tiled=True).astype(
            jnp.float32
        ),
        lax.all_gather(summed[3].astype(jnp.bfloat16), "blk", axis=0, tiled=True).astype(
            jnp.float32
        ),
        lax.all_gather(summed[4].astype(jnp.bfloat16), "blk", axis=0, tiled=True).astype(
            jnp.float32
        ),
        lax.all_gather(summed[5].astype(jnp.bfloat16), "blk", axis=0, tiled=True).astype(
            jnp.float32
        ),
        lax.all_gather(summed[6].astype(jnp.bfloat16), "blk", axis=0, tiled=True).astype(
            jnp.float32
        ),
        lax.all_gather(summed[7].astype(jnp.bfloat16), "blk", axis=0, tiled=True).astype(
            jnp.float32
        ),
        lax.all_gather(summed[8].astype(jnp.bfloat16), "blk", axis=0, tiled=True).astype(
            jnp.float32
        ),
        lax.all_gather(summed[9].astype(jnp.bfloat16), "blk", axis=0, tiled=True).astype(
            jnp.float32
        ),
        lax.all_gather(summed[10].astype(jnp.bfloat16), "blk", axis=0, tiled=True).astype(
            jnp.float32
        ),
        lax.all_gather(summed[11].astype(jnp.bfloat16), "blk", axis=0, tiled=True).astype(
            jnp.float32
        ),
        lax.all_gather(summed[12].astype(jnp.bfloat16), "blk", axis=0, tiled=True).astype(
            jnp.float32
        ),
    )


def local(
    tokens,
    counts,
    ln1_gain,
    ln1_shift,
    w_qkv,
    bias_q,
    bias_v,
    w_out,
    bias_out,
    ln2_gain,
    ln2_shift,
    w_fc1,
    bias_fc1,
    w_fc2,
    bias_fc2,
    cotangent,
):
    cube_count, row_count, width = tokens.shape
    head_count = HEADS
    depth = HD
    score_scale = HD ** (-0.5)
    inputs = tokens.astype(jnp.float32)
    gain_one = ln1_gain.astype(jnp.float32)
    shift_one = ln1_shift.astype(jnp.float32)
    gain_two = ln2_gain.astype(jnp.float32)
    shift_two = ln2_shift.astype(jnp.float32)
    normed = norm_rows(inputs, gain_one, shift_one).astype(jnp.bfloat16)
    project = jnp.dot(normed, w_qkv, preferred_element_type=jnp.float32)
    queries = (project[..., :width] + bias_q.astype(jnp.float32)).astype(jnp.bfloat16)
    key_local = project[..., width : 2 * width].astype(jnp.bfloat16)
    value_local = (project[..., 2 * width :] + bias_v.astype(jnp.float32)).astype(jnp.bfloat16)
    key_all, value_all = (
        lax.all_gather(key_local, "blk", axis=1, tiled=True),
        lax.all_gather(value_local, "blk", axis=1, tiled=True),
    )
    seq_rows = key_all.shape[1]
    block_rows = math.gcd(seq_rows, 512)
    block_count = seq_rows // block_rows
    block_steps = jnp.arange(block_count, dtype=jnp.int32)
    query_heads = queries.reshape(cube_count, row_count, head_count, depth)

    def key_slices(offset):
        key_part = lax.dynamic_slice_in_dim(key_all, offset, block_rows, 1).reshape(
            cube_count, block_rows, head_count, depth
        )
        value_part = lax.dynamic_slice_in_dim(value_all, offset, block_rows, 1).reshape(
            cube_count, block_rows, head_count, depth
        )
        usable = cube_valid(counts, offset, block_rows)[:, None, None, :]
        return (key_part, value_part, usable)

    def forward_block(carry, step_index):
        row_top, row_total, accum = carry
        key_part, value_part, usable = key_slices(step_index * block_rows)
        scores = (
            jnp.einsum("cqhd,ckhd->chqk", query_heads, key_part, preferred_element_type=jnp.float32)
            * score_scale
        )
        masked = jnp.where(usable, scores, MASK_LOW)
        new_top = jnp.maximum(row_top, jnp.max(masked, axis=-1))
        factor = jnp.exp(row_top - new_top)
        weights = jnp.where(usable, jnp.exp(masked - new_top[..., None]), 0.0)
        row_total = row_total * factor + jnp.sum(weights, axis=-1)
        accum = accum * jnp.transpose(factor, (0, 2, 1))[..., None] + jnp.einsum(
            "chqk,ckhd->cqhd",
            weights.astype(jnp.bfloat16),
            value_part,
            preferred_element_type=jnp.float32,
        )
        return ((new_top, row_total, accum), None)

    start_carry = (
        jnp.full((cube_count, head_count, row_count), MASK_LOW, jnp.float32),
        jnp.zeros((cube_count, head_count, row_count), jnp.float32),
        jnp.zeros((cube_count, row_count, head_count, depth), jnp.float32),
    )
    (row_top, row_total, accum), _ = lax.scan(forward_block, start_carry, block_steps)
    attended_f = (accum / jnp.transpose(row_total, (0, 2, 1))[..., None]).reshape(
        cube_count, row_count, width
    )
    log_total = row_top + jnp.log(row_total)
    attended = attended_f.astype(jnp.bfloat16)
    middle = (
        inputs
        + jnp.dot(attended, w_out, preferred_element_type=jnp.float32)
        + bias_out.astype(jnp.float32)
    )
    normed_two = norm_rows(middle, gain_two, shift_two).astype(jnp.bfloat16)
    hidden = jnp.dot(normed_two, w_fc1, preferred_element_type=jnp.float32) + bias_fc1.astype(
        jnp.float32
    )
    active = gelu_exact(hidden).astype(jnp.bfloat16)
    output = (
        middle
        + jnp.dot(active, w_fc2, preferred_element_type=jnp.float32)
        + bias_fc2.astype(jnp.float32)
    ).astype(jnp.bfloat16)
    grad_bias_fc2 = jnp.sum(cotangent.astype(jnp.float32), axis=(0, 1))
    grad_w_fc2 = jnp.einsum("ctf,ctd->fd", active, cotangent, preferred_element_type=jnp.float32)
    back_active = jnp.einsum("ctd,fd->ctf", cotangent, w_fc2, preferred_element_type=jnp.float32)
    _, gelu_pull = jax.vjp(gelu_exact, hidden)
    back_hidden = gelu_pull(back_active)[0]
    grad_bias_fc1 = jnp.sum(back_hidden, axis=(0, 1))
    hidden_low = back_hidden.astype(jnp.bfloat16)
    grad_w_fc1 = jnp.einsum(
        "ctd,ctf->df", normed_two, hidden_low, preferred_element_type=jnp.float32
    )
    back_normed_two = jnp.einsum(
        "ctf,df->ctd", hidden_low, w_fc1, preferred_element_type=jnp.float32
    )
    _, norm_pull_two = jax.vjp(norm_rows, middle, gain_two, shift_two)
    back_middle_norm, grad_ln2_gain, grad_ln2_shift = norm_pull_two(back_normed_two)
    back_middle = cotangent.astype(jnp.float32) + back_middle_norm
    mlp_grads = (
        grad_ln2_gain,
        grad_ln2_shift,
        grad_w_fc1,
        grad_bias_fc1,
        grad_w_fc2,
        grad_bias_fc2,
    )
    grad_bias_out = jnp.sum(back_middle, axis=(0, 1))
    middle_low = back_middle.astype(jnp.bfloat16)
    grad_w_out = jnp.einsum("ctd,cte->de", attended, middle_low, preferred_element_type=jnp.float32)
    back_attended = jnp.einsum(
        "cte,de->ctd", middle_low, w_out, preferred_element_type=jnp.float32
    ).astype(jnp.bfloat16)
    back_heads = back_attended.reshape(cube_count, row_count, head_count, depth)
    delta = jnp.transpose(
        jnp.sum(
            (back_attended.astype(jnp.float32) * attended_f).reshape(
                cube_count, row_count, head_count, depth
            ),
            axis=-1,
        ),
        (0, 2, 1),
    )

    def block_grads(key_part, value_part, usable):
        scores = (
            jnp.einsum("cqhd,ckhd->chqk", query_heads, key_part, preferred_element_type=jnp.float32)
            * score_scale
        )
        probs = jnp.where(usable, jnp.exp(scores - log_total[..., None]), 0.0)
        back_probs = jnp.einsum(
            "cqhd,ckhd->chqk", back_heads, value_part, preferred_element_type=jnp.float32
        )
        back_scores = (probs * (back_probs - delta[..., None])).astype(jnp.bfloat16)
        return (probs, back_scores)

    query_zero = jnp.zeros((cube_count, row_count, head_count, depth), jnp.float32)

    def back_block(carry, step_index):
        back_query, key_grads, value_grads = carry
        offset = step_index * block_rows
        key_part, value_part, usable = key_slices(offset)
        probs, back_scores = block_grads(key_part, value_part, usable)
        back_query = (
            back_query
            + jnp.einsum(
                "chqk,ckhd->cqhd", back_scores, key_part, preferred_element_type=jnp.float32
            )
            * score_scale
        )
        key_block = (
            jnp.einsum(
                "chqk,cqhd->ckhd", back_scores, query_heads, preferred_element_type=jnp.float32
            )
            * score_scale
        )
        value_block = jnp.einsum(
            "chqk,cqhd->ckhd",
            probs.astype(jnp.bfloat16),
            back_heads,
            preferred_element_type=jnp.float32,
        )
        key_grads = lax.dynamic_update_slice_in_dim(
            key_grads, key_block.reshape(cube_count, block_rows, width), offset, 1
        )
        value_grads = lax.dynamic_update_slice_in_dim(
            value_grads, value_block.reshape(cube_count, block_rows, width), offset, 1
        )
        return ((back_query, key_grads, value_grads), None)

    full_zero = jnp.zeros((cube_count, seq_rows, width), jnp.float32)
    (back_query, key_grads, value_grads), _ = lax.scan(
        back_block, (query_zero, full_zero, full_zero), block_steps
    )
    key_back, value_back = (
        lax.psum_scatter(
            key_grads.astype(jnp.bfloat16), "blk", scatter_dimension=1, tiled=True
        ).astype(jnp.float32),
        lax.psum_scatter(
            value_grads.astype(jnp.bfloat16), "blk", scatter_dimension=1, tiled=True
        ).astype(jnp.float32),
    )
    query_low = back_query.reshape(cube_count, row_count, width).astype(jnp.bfloat16)
    key_low = key_back.astype(jnp.bfloat16)
    value_low = value_back.astype(jnp.bfloat16)
    grad_bias_q = jnp.sum(query_low.astype(jnp.float32), axis=(0, 1))
    grad_bias_v = jnp.sum(value_low.astype(jnp.float32), axis=(0, 1))
    back_project = jnp.concatenate([query_low, key_low, value_low], axis=-1)
    grad_w_qkv = jnp.einsum("ctd,cte->de", normed, back_project, preferred_element_type=jnp.float32)
    back_normed = jnp.einsum("cte,de->ctd", back_project, w_qkv, preferred_element_type=jnp.float32)
    _, norm_pull_one = jax.vjp(norm_rows, inputs, gain_one, shift_one)
    back_inputs, grad_ln1_gain, grad_ln1_shift = norm_pull_one(back_normed)
    input_grad = back_middle + back_inputs
    attn_grads = (
        grad_ln1_gain,
        grad_ln1_shift,
        grad_w_qkv,
        grad_bias_q,
        grad_bias_v,
        grad_w_out,
        grad_bias_out,
    )
    every_grad = total_every(attn_grads + mlp_grads)
    attn_grads = every_grad[:7]
    mlp_grads = every_grad[7:]
    return (
        output,
        input_grad,
        attn_grads[0],
        attn_grads[1],
        attn_grads[2],
        attn_grads[3],
        attn_grads[4],
        attn_grads[5],
        attn_grads[6],
        mlp_grads[0],
        mlp_grads[1],
        mlp_grads[2],
        mlp_grads[3],
        mlp_grads[4],
        mlp_grads[5],
    )


F32 = jnp.float32
BF16 = jnp.bfloat16
EXP_SCALE = math.log2(math.e) / 8
LANES = 128
VMEM = pl.BlockSpec(memory_space=pltpu.VMEM)
SMEM = pl.BlockSpec(memory_space=pltpu.SMEM)
ANY = pl.BlockSpec(memory_space=pl.ANY)


def lasting(micros):
    return pl.CostEstimate(flops=micros * 10**9, bytes_accessed=2**20, transcendentals=0)


def shape_of(shape, dtype):
    return jax.ShapeDtypeStruct(shape, dtype)


def limits(mib):
    return pltpu.CompilerParams(vmem_limit_bytes=mib * 2**20)


def dot_nt(a, b):
    return lax.dot_general(a, b, (((1,), (1,)), ((), ())), preferred_element_type=F32)


def dot_nn(a, b):
    return lax.dot_general(a, b, (((1,), (0,)), ((), ())), preferred_element_type=F32)


def dot_tn(a, b):
    return lax.dot_general(a, b, (((0,), (0,)), ((), ())), preferred_element_type=F32)


def centred(values):
    centre = values - jnp.mean(values, axis=1, keepdims=True)
    spread = jnp.mean(centre * centre, axis=1, keepdims=True)
    return centre, lax.rsqrt(spread + NORM_EPS)


def norm_back(centre, recip, back, gain):
    unit = centre * recip
    grad = back * gain
    inner = jnp.mean(grad * unit, axis=1, keepdims=True)
    return unit, recip * (grad - jnp.mean(grad, axis=1, keepdims=True) - unit * inner)


def prepare_kernel(a, b, out_a, out_b, *, counts):
    out_a[...] = a[...].astype(F32)
    out_b[...] = b[...].astype(F32)


def prepare(a, b):
    return pl.pallas_call(
        functools.partial(prepare_kernel, counts=None),
        in_specs=[VMEM] * 2,
        out_specs=[VMEM] * 2,
        out_shape=[shape_of(a.shape, F32), shape_of(b.shape, F32)],
        cost_estimate=lasting(1),
        name="prepare",
    )(a, b)


def project_rows(x, vecs, w, q_ref, kv_ref, at, q_at=None):
    gain, shift, bias_q, bias_v = (vecs[i : i + 1, :] for i in range(4))
    centre, recip = centred(x.astype(F32))
    normed = (centre * recip * gain + shift).astype(BF16)
    kv_ref[0, at, :] = dot_nn(normed, w[:, 768:1536]).astype(BF16)
    kv_ref[1, at, :] = (dot_nn(normed, w[:, 1536:]) + bias_v).astype(BF16)
    if q_at is not None:
        q_ref[q_at, :] = (dot_nn(normed, w[:, :768]) + bias_q).astype(BF16)


def project_kernel(x13_in, x2_in, vecs, w_in, q_ref, kv_ref, held, w, sems):
    copies = start_copies([x13_in.at[0], x2_in, w_in], [held.at[0], held.at[1], w], sems)
    for copy in copies:
        copy.wait()
    rows = held.shape[1]
    for i in range(2):
        at = pl.ds(i * rows, rows)
        project_rows(held[i], vecs, w, q_ref, kv_ref, at, at)


def project(x13, x2, vecs, w):
    n = 2 * x2.shape[0]
    return pl.pallas_call(
        project_kernel,
        in_specs=[ANY, ANY, VMEM, ANY],
        out_specs=[VMEM] * 2,
        out_shape=[shape_of((n, 768), BF16), shape_of((2, n, 768), BF16)],
        scratch_shapes=[
            pltpu.VMEM((2,) + x2.shape, BF16),
            pltpu.VMEM(w.shape, w.dtype),
            pltpu.SemaphoreType.DMA((3,)),
        ],
        compiler_params=limits(40),
        cost_estimate=lasting(4),
        name="project",
    )(x13, x2, vecs, w)


def project_short_kernel(
    where, x13, near, other, far, vecs, w_in, q_ref, head_ref, tail_ref, w, held, sems, *, spare
):
    (copy,) = start_copies([w_in], [w], sems)
    rows = near.shape[0]
    mine = where[2]
    for k, block in enumerate((x13[1], near[...], other[...], far[...])):
        held[k ^ mine] = block
    copy.wait()
    for i in range(2):
        project_rows(held[i], vecs, w, None, head_ref, pl.ds(i * rows, rows))
    project_rows(held[2][:spare], vecs, w, None, tail_ref, pl.ds(0, spare))
    centre, recip = centred(x13[1].astype(F32))
    normed = (centre * recip * vecs[0:1, :] + vecs[1:2, :]).astype(BF16)
    q_ref[...] = (dot_nn(normed, w[:, :768]) + vecs[2:3, :]).astype(BF16)


def project_short(where, x13, near, other, far, vecs, w, spare):
    rows = near.shape[0]
    return pl.pallas_call(
        functools.partial(project_short_kernel, spare=spare),
        in_specs=[SMEM] + [VMEM] * 5 + [ANY],
        out_specs=[VMEM] * 3,
        out_shape=[
            shape_of((rows, 768), BF16),
            shape_of((2, 2 * rows, 768), BF16),
            shape_of((2, spare, 768), BF16),
        ],
        scratch_shapes=[
            pltpu.VMEM(w.shape, w.dtype),
            pltpu.VMEM((4, rows, 768), BF16),
            pltpu.SemaphoreType.DMA((1,)),
        ],
        compiler_params=limits(40),
        cost_estimate=lasting(4),
        name="project_short",
    )(where, x13, near, other, far, vecs, w)


def start_copies(sources, targets, sems):
    copies = [
        pltpu.make_async_copy(source, target, sems.at[i])
        for i, (source, target) in enumerate(zip(sources, targets))
    ]
    for copy in copies:
        copy.start()
    return copies


def three_parts(values, lane):
    high = values.astype(BF16)
    rest = values - high.astype(F32)
    middle = rest.astype(BF16)
    least = (rest - middle.astype(F32)).astype(BF16)
    zero = jnp.zeros((), BF16)
    return jnp.where(
        lane == 0, high, jnp.where(lane == 1, middle, jnp.where(lane == 2, least, zero))
    )


def lane_index(rows=1):
    return lax.broadcasted_iota(jnp.int32, (rows, LANES), 1)


def attend_kernel(*refs, pieces, valid, step):
    q_ref = refs[0]
    kvs = refs[1 : 1 + pieces]
    o_ref, t_ref = refs[1 + pieces :]
    lane = lane_index()
    low = lane < 64
    half = lane % 64
    total = sum(kv.shape[1] for kv in kvs)
    keys, values = [], []
    for h in range(2):
        own = low if h == 0 else ~low
        key_parts, value_parts, at = [], [], 0
        for kv in kvs:
            n = kv.shape[1]
            beside = jnp.zeros((n, LANES), BF16)
            if at + n > valid:
                place = lax.broadcasted_iota(jnp.int32, (n, LANES), 0) + at
                beside = jnp.where(
                    (place >= valid) & (lane_index(n) % 64 == 0), MASK_LOW, 0.0
                ).astype(BF16)
            key_parts.append(jnp.where(own, kv[0], beside))
            value_parts.append(jnp.where(own, kv[1], jnp.ones((), BF16)))
            at += n
        keys.append(key_parts)
        values.append(value_parts)
    for s in range(q_ref.shape[0] // step):
        at = pl.ds(s * step, step)
        q = q_ref[at, :]
        sums, tops = [], []
        for h in range(2):
            own = low if h == 0 else ~low
            q_own = q
            if total > valid:
                q_own = jnp.where(own, q, jnp.where(half == 0, 1.0, 0.0).astype(BF16))
            scores = [dot_nt(q_own, k) for k in keys[h]]
            top = functools.reduce(
                jnp.maximum, [jnp.max(x, axis=1, keepdims=True) for x in scores]
            )
            scaled_top = top * EXP_SCALE
            weights = [jnp.exp2(x * EXP_SCALE - scaled_top).astype(BF16) for x in scores]
            sums.append(
                functools.reduce(jnp.add, [dot_nn(p, v) for p, v in zip(weights, values[h])])
            )
            tops.append(top)
        above = jnp.where(low, sums[0], sums[1])
        below = jnp.where(low, sums[1], sums[0])
        o_ref[at, :] = above / pltpu.roll(below, 64, 1)
        log_total = -(jnp.where(low, tops[1], tops[0]) + 8.0 * jnp.log(below))
        t_ref[at, :] = jnp.where(half == 3, jnp.ones((), BF16), three_parts(log_total, half))


def attend(q, kvs, valid, rows, step, first=0, count=6):
    n = q.shape[0]
    keys = sum(kv.shape[1] for kv in kvs)
    block = pl.BlockSpec((rows, LANES), lambda p, i: (i, p))
    return pl.pallas_call(
        functools.partial(attend_kernel, pieces=len(kvs), valid=valid, step=step),
        out_shape=[shape_of((n, LANES * count), F32), shape_of((n, LANES * count), BF16)],
        grid=(count, n // rows),
        in_specs=[pl.BlockSpec((rows, LANES), lambda p, i: (i, first + p))]
        + [pl.BlockSpec((2, kv.shape[1], LANES), lambda p, i: (0, 0, first + p)) for kv in kvs],
        out_specs=[block, block],
        compiler_params=limits(56),
        cost_estimate=lasting(n * keys * count // 280000),
        name="attend",
    )(q, *kvs)


def attend_back_kernel(*refs, pieces, valid, step, split):
    where = refs[0]
    q_ref, do_ref, o_ref, t_ref = refs[1:5]
    kvs = refs[5 : 5 + pieces]
    dq_ref = refs[5 + pieces]
    outs = refs[6 + pieces :]
    n = q_ref.shape[0]
    lane = lane_index()
    low = lane < 64
    half = lane % 64
    q, do, t = q_ref[...], do_ref[...], t_ref[...]
    product = do.astype(F32) * o_ref[...]
    delta = [
        jnp.sum(jnp.where(low, product, 0.0), axis=1, keepdims=True),
        jnp.sum(jnp.where(low, 0.0, product), axis=1, keepdims=True),
    ]
    d = three_parts(-jnp.where(low, delta[1], delta[0]), half)
    queries = [jnp.where(low, q, t), jnp.where(low, t, q)]
    backs = [jnp.where(low, do, d), jnp.where(low, d, do)]
    ones = jnp.where(half < 3, 1.0, 0.0).astype(BF16)
    sums = [jnp.zeros((LANES, n), F32), jnp.zeros((LANES, n), F32)]
    starts = [sum(kv.shape[1] for kv in kvs[:i]) for i in range(pieces)]
    small = None
    for i in reversed(range(pieces)):
        kv = kvs[i]
        for first in range(0, kv.shape[1], step):
            size = min(step, kv.shape[1] - first)
            at = pl.ds(first, size)
            key_sums, value_sums = [], []
            for h in range(2):
                own = low if h == 0 else ~low
                beside = ones
                if starts[i] + first + size > valid:
                    place = lax.broadcasted_iota(jnp.int32, (size, LANES), 0) + (starts[i] + first)
                    wide = lane_index(size) % 64
                    beside = jnp.where(
                        wide < 3, 1.0, jnp.where((place >= valid) & (wide == 3), MASK_LOW, 0.0)
                    ).astype(BF16)
                key = jnp.where(own, kv[0, at, :], beside)
                value = jnp.where(own, kv[1, at, :], ones)
                probs = jnp.exp2(dot_nt(key, queries[h]) * EXP_SCALE)
                back_scores = (probs * dot_nt(value, backs[h])).astype(BF16)
                value_sums.append(dot_nn(probs.astype(BF16), backs[h]))
                key_sums.append(dot_nn(back_scores, queries[h]))
                sums[h] = sums[h] + dot_tn(key, back_scores)
            both = (
                (jnp.where(low, key_sums[0], key_sums[1]) * 0.125).astype(BF16),
                jnp.where(low, value_sums[0], value_sums[1]).astype(BF16),
            )
            for k in range(2):
                if not split:
                    outs[i][k, at, :] = both[k]
                elif i == 0:
                    other = jnp.zeros_like(both[k])
                    if first == 0:
                        rest = jnp.zeros((size - small[k].shape[0], LANES), BF16)
                        other = jnp.concatenate([small[k], rest], axis=0)
                    stays = where[0] == 0
                    outs[0][k, at, :] = jnp.where(stays, both[k], other)
                    outs[1][k, at, :] = jnp.where(stays, other, both[k])
            small = both
    both = jnp.concatenate([sums[0][:64], sums[1][64:]], axis=0)
    dq_ref[...] = (both.T * 0.125).astype(BF16)


def attend_back(where, q, do, first_row, o, t, kvs, valid, step, first, count, split=False):
    n = q.shape[0]
    keys = sum(kv.shape[1] for kv in kvs)
    row = first_row // n
    block = pl.BlockSpec((n, LANES), lambda p: (0, first + p))
    back_block = pl.BlockSpec((n, LANES), lambda p: (row, first + p))
    wide = [pl.BlockSpec((2, kv.shape[1], LANES), lambda p: (0, 0, first + p)) for kv in kvs]
    out = pl.BlockSpec((n, LANES), lambda p: (0, p))
    outs = [kvs[0], kvs[0]] if split else kvs
    out_wide = [pl.BlockSpec((2, kv.shape[1], LANES), lambda p: (0, 0, p)) for kv in outs]
    return pl.pallas_call(
        functools.partial(
            attend_back_kernel, pieces=len(kvs), valid=valid, step=step, split=split
        ),
        out_shape=[shape_of((n, LANES * count), BF16)]
        + [shape_of((2, kv.shape[1], LANES * count), BF16) for kv in outs],
        grid=(count,),
        in_specs=[SMEM, block, back_block, block, block] + wide,
        out_specs=[out] + out_wide,
        compiler_params=limits(56),
        cost_estimate=lasting(n * keys * count // 180000),
        name="attend_back",
    )(where, q, do, o, t, *kvs)


def fill_part(where, send, keep, j, block):
    left, right = block[:, :384], block[:, 384:]
    first = where[0] == 0
    for ref, half in (
        (keep, jnp.where(first, left, right)),
        (send, jnp.where(first, right, left)),
    ):
        for p in range(16):
            ref[p ^ where[1], pl.ds(j * 48, 48), :] = half[p * 48 : (p + 1) * 48]


def attended_rows(att_full, att_short, i, rows):
    if i == 2:
        return att_short[...].astype(BF16)
    at = pl.ds(i * rows, rows)
    return att_full[at, :].astype(BF16)


def feed_kernel(
    where, att_full_in, att_short_in, x13_in, x2_in, c13, c2, w_out_in, vecs, w1, b1, w2,
    o13, o2, mid_out, normed_out, hidden_low, send, keep, gb1,
    att_full, att_short, x13, x2, w_out, mid, normed, out_sum, cot, active, sems,
    *, steps, tile,
):
    j = pl.program_id(0)
    xs, outs = (x13.at[0], x2, x13.at[1]), (o13.at[0], o2, o13.at[1])
    rows = x2.shape[0]
    bias_out, gain, shift, b2 = (vecs[i : i + 1, :] for i in range(4))

    def at(i):
        return pl.ds(i * rows, rows)

    def leaving():
        return [
            pltpu.make_async_copy(mid, mid_out, sems.at[0]),
            pltpu.make_async_copy(normed, normed_out, sems.at[1]),
        ]

    @pl.when(j == 0)
    def _():
        copies = start_copies(
            [w_out_in, att_full_in, x13_in, x2_in, att_short_in, c13.at[0], c2, c13.at[1]],
            [w_out, att_full, x13, x2, att_short] + [cot.at[at(i), :] for i in range(3)],
            sems,
        )
        for copy in copies[:4]:
            copy.wait()
        for i in range(3):
            if i == 2:
                copies[4].wait()
            att = attended_rows(att_full, att_short, i, rows)
            m = xs[i][...].astype(F32) + dot_nn(att, w_out[...]) + bias_out
            mid[at(i), :] = m
            centre, recip = centred(m)
            normed[at(i), :] = (centre * recip * gain + shift).astype(BF16)
            out_sum[at(i), :] = m + b2
        for copy in copies[5:]:
            copy.wait()
        for copy in leaving():
            copy.start()

    w1_tile, w2_tile = w1[...], w2[...]
    bias = b1[...]
    bias_sum = jnp.zeros((1, tile), F32)
    for i in range(3):
        h = dot_nn(normed[at(i), :], w1_tile) + bias
        back_active = dot_nt(cot[at(i), :], w2_tile)
        share = 0.5 + 0.5 * lax.erf(h * math.sqrt(0.5))
        act = (h * share).astype(BF16)
        slope = share + h * (math.sqrt(0.5 / math.pi) * jnp.exp(h * h * (-0.5)))
        back_hidden = back_active * slope
        bias_sum = bias_sum + jnp.sum(back_hidden, axis=0, keepdims=True)
        active[at(i), :] = act
        hidden_low[at(i), :] = back_hidden.astype(BF16)
        out_sum[at(i), :] += dot_nn(act, w2_tile)
    gb1[...] = bias_sum
    grad = dot_tn(active[...], cot[...]).astype(BF16)
    fill_part(where, send, keep, 0, grad)

    @pl.when(j == steps - 1)
    def _():
        for copy in leaving():
            copy.wait()
        for i in range(3):
            outs[i][...] = out_sum[at(i), :].astype(BF16)


def feed(where, att_full, att_short, xs, cots, w_out, vecs, w1, b1, w2):
    rows = xs[1].shape[0]
    n = rows * 3
    wide = w1.shape[1]
    tile = 768
    steps = wide // tile
    across = pl.BlockSpec((768, tile), lambda j: (0, j))
    down = pl.BlockSpec((tile, 768), lambda j: (j, 0))
    line = pl.BlockSpec((1, tile), lambda j: (0, j))
    return pl.pallas_call(
        functools.partial(feed_kernel, steps=steps, tile=tile),
        grid=(steps,),
        in_specs=[SMEM] + [ANY] * 7 + [VMEM, across, line, down],
        out_specs=[VMEM] * 2
        + [ANY] * 2
        + [pl.BlockSpec((n, tile), lambda j: (0, j))]
        + [pl.BlockSpec((16, 48, 384), lambda j: (0, j, 0))] * 2
        + [line],
        out_shape=[shape_of((2, rows, 768), BF16), shape_of((rows, 768), BF16)]
        + [
            shape_of((n, 768), F32),
            shape_of((n, 768), BF16),
            shape_of((n, wide), BF16),
            shape_of((16, 48 * steps, 384), BF16),
            shape_of((16, 48 * steps, 384), BF16),
            shape_of((1, wide), F32),
        ],
        scratch_shapes=[
            pltpu.VMEM(v.shape, v.dtype) for v in (att_full, att_short, *xs, w_out)
        ]
        + [
            pltpu.VMEM((n, 768), F32),
            pltpu.VMEM((n, 768), BF16),
            pltpu.VMEM((n, 768), F32),
            pltpu.VMEM((n, 768), BF16),
            pltpu.VMEM((n, tile), BF16),
            pltpu.SemaphoreType.DMA((8,)),
        ],
        compiler_params=limits(60),
        cost_estimate=lasting(36),
        name="feed",
    )(where, att_full, att_short, *xs, *cots, w_out, vecs, w1, b1, w2)


def feed_back_kernel(
    where, att_full_in, att_short_in, c13_in, c2_in, w_out, vecs, mid_in, normed,
    hidden_low, w1,
    back_att, back_mid, send, keep, sums,
    back_sum, flipped, low_mid, att, att_full, att_short, c13, c2, mid, sems,
    *, steps,
):
    j = pl.program_id(0)
    late = (att_full, att_short, c13, c2, mid)
    sources = (att_full_in, att_short_in, c13_in, c2_in, mid_in)
    cots = (c13.at[0], c2, c13.at[1])
    rows = c2.shape[0]
    gain = vecs[1:2, :]

    def at(i):
        return pl.ds(i * rows, rows)

    @pl.when(j == 0)
    def _():
        start_copies(sources, late, sems)
        flipped[...] = normed[...].T
        for i in range(3):
            back_sum[at(i), :] = jnp.zeros((rows, 768), F32)

    @pl.when(j < steps)
    def _():
        for i in range(3):
            back_sum[at(i), :] += dot_nt(hidden_low[at(i), :], w1[...])
        fill_part(where, send, keep, 0, dot_nn(flipped[...], hidden_low[...]).astype(BF16))

    @pl.when(j == steps)
    def _():
        for i in range(len(late)):
            pltpu.make_async_copy(sources[i], late[i], sems.at[i]).wait()
        zero = jnp.zeros((1, 768), F32)
        grad_out, grad_gain, grad_shift, grad_b2 = zero, zero, zero, zero
        for i in range(3):
            centre, recip = centred(mid[at(i), :])
            back = back_sum[at(i), :]
            unit, through = norm_back(centre, recip, back, gain)
            c = cots[i][...].astype(F32)
            m = c + through
            grad_gain = grad_gain + jnp.sum(back * unit, axis=0, keepdims=True)
            grad_shift = grad_shift + jnp.sum(back, axis=0, keepdims=True)
            grad_out = grad_out + jnp.sum(m, axis=0, keepdims=True)
            grad_b2 = grad_b2 + jnp.sum(c, axis=0, keepdims=True)
            back_mid[at(i), :] = m
            low = m.astype(BF16)
            low_mid[at(i), :] = low
            back_att[at(i), :] = dot_nt(low, w_out[...]).astype(BF16)
            att[at(i), :] = attended_rows(att_full, att_short, i, rows)
        fill_part(where, send, keep, 0, dot_tn(att[...], low_mid[...]).astype(BF16))
        sums[...] = jnp.concatenate(
            [grad_out, grad_gain, grad_shift, grad_b2, zero, zero, zero, zero], axis=0
        )


def feed_back(where, att_full, att_short, cots, w_out, vecs, mid, normed, hidden_low, w1):
    rows = cots[1].shape[0]
    n = rows * 3
    wide = w1.shape[1]
    tile = 768
    steps = wide // tile
    part = pl.BlockSpec((16, 48, 384), lambda j: (0, j, 0))
    return pl.pallas_call(
        functools.partial(feed_back_kernel, steps=steps),
        grid=(steps + 1,),
        in_specs=[SMEM]
        + [ANY] * 4
        + [VMEM, VMEM, ANY, VMEM]
        + [
            pl.BlockSpec((n, tile), lambda j: (0, jnp.minimum(j, steps - 1))),
            pl.BlockSpec((768, tile), lambda j: (0, jnp.minimum(j, steps - 1))),
        ],
        out_specs=[VMEM, VMEM, part, part, VMEM],
        out_shape=[
            shape_of((n, 768), BF16),
            shape_of((n, 768), F32),
            shape_of((16, 48 * (steps + 1), 384), BF16),
            shape_of((16, 48 * (steps + 1), 384), BF16),
            shape_of((8, 768), F32),
        ],
        scratch_shapes=[
            pltpu.VMEM((n, 768), F32),
            pltpu.VMEM((768, n), BF16),
            pltpu.VMEM((n, 768), BF16),
            pltpu.VMEM((n, 768), BF16),
        ]
        + [
            pltpu.VMEM(v.shape, v.dtype) for v in (att_full, att_short, *cots, mid)
        ]
        + [pltpu.SemaphoreType.DMA((5,))],
        compiler_params=limits(60),
        cost_estimate=lasting(26),
        name="feed_back",
    )(where, att_full, att_short, *cots, w_out, vecs, mid, normed, hidden_low, w1)


def project_back_kernel(
    where, x13_in, x2_in, vecs, dq_full_in, dq_short_in, own_full_in, got_full_in,
    keep_short_in, got_pair_in, got_near_in, send, keep, back_out,
    x13, x2, dq_full, dq_short, own_full, got_full, keep_short, got_pair, got_near, back, flipped,
    sems,
):
    rows = x2.shape[0]
    full = dq_full.shape[0]
    gain, shift = vecs[0:1, :], vecs[1:2, :]
    odd = where[1] % 2
    own_rows = pl.ds(pl.multiple_of(odd * rows, rows), rows)
    sources = [
        x13_in, x2_in, dq_full_in, dq_short_in, own_full_in, got_full_in,
        keep_short_in.at[:, own_rows, :], got_pair_in.at[:, own_rows, :], got_near_in,
    ]
    targets = [x13, x2, dq_full, dq_short, own_full, got_full, keep_short, got_pair, got_near]
    copies = start_copies(sources, targets, sems)
    for copy in copies[:2]:
        copy.wait()
    for i, x in enumerate((x13.at[0], x2, x13.at[1])):
        centre, recip = centred(x[...].astype(F32))
        flipped[:, pl.ds(i * rows, rows)] = (centre * recip * gain + shift).astype(BF16).T
    for copy in copies[2:4]:
        copy.wait()
    back[0, :full, :] = dq_full[...]
    back[0, full:, :] = dq_short[...]
    outs = [pltpu.make_async_copy(back.at[k], back_out.at[k], sems.at[k]) for k in range(3)]
    outs[0].start()
    fill_part(where, send, keep, 0, dot_nn(flipped[...], back[0]).astype(BF16))
    for copy in copies[4:]:
        copy.wait()
    for k in range(2):
        total = own_full[k].astype(F32) + got_full[k].astype(F32)
        back[k + 1, :full, :] = total.astype(BF16)
        total = keep_short[k].astype(F32) + got_pair[k].astype(F32) + got_near[k].astype(F32)
        back[k + 1, full:, :] = total.astype(BF16)
        outs[k + 1].start()
        fill_part(where, send, keep, k + 1, dot_nn(flipped[...], back[k + 1]).astype(BF16))
    for copy in outs:
        copy.wait()


def project_back(where, xs, vecs, *backs):
    rows = xs[1].shape[0]
    n = rows * 3
    short = (2, rows, 768)
    held = [(v.shape, v.dtype) for v in (*xs, *backs[:4])] + [(short, BF16)] * 3
    return pl.pallas_call(
        project_back_kernel,
        in_specs=[SMEM, ANY, ANY, VMEM] + [ANY] * 7,
        out_specs=[VMEM] * 2 + [ANY],
        out_shape=[shape_of((16, 144, 384), BF16)] * 2 + [shape_of((3, n, 768), BF16)],
        scratch_shapes=[pltpu.VMEM(*each) for each in held]
        + [pltpu.VMEM((3, n, 768), BF16), pltpu.VMEM((768, n), BF16)]
        + [pltpu.SemaphoreType.DMA((9,))],
        compiler_params=limits(60),
        cost_estimate=lasting(11),
        name="project_back",
    )(where, *xs, vecs, *backs)


def input_back_kernel(
    where, x13, x2, vecs, w_in, back_mid, back, sums, gb1, o13, o2, lines, total, w, sems
):
    i = pl.program_id(0)
    rows = x2.shape[0]
    gain = vecs[0:1, :]

    @pl.when(i == 0)
    def _():
        (copy,) = start_copies([w_in], [w], sems)
        total[...] = jnp.zeros(total.shape, F32)
        copy.wait()

    x = jnp.where(i == 1, x2[...], x13[0])
    centre, recip = centred(x.astype(F32))
    back_normed = dot_nt(back[0], w[:, :768])
    for k in (1, 2):
        back_normed = back_normed + dot_nt(back[k], w[:, 768 * k : 768 * (k + 1)])
    unit, through = norm_back(centre, recip, back_normed, gain)
    out = (back_mid[...] + through).astype(BF16)

    @pl.when(i == 1)
    def _():
        o2[...] = out

    @pl.when(i != 1)
    def _():
        o13[0] = out

    ones = jnp.ones((8, rows), BF16)
    total[...] += jnp.concatenate(
        [
            jnp.sum(back_normed * unit, axis=0, keepdims=True),
            jnp.sum(back_normed, axis=0, keepdims=True),
            dot_nn(ones, back[0])[0:1],
            dot_nn(ones, back[2])[0:1],
            jnp.zeros((4, 768), F32),
        ],
        axis=0,
    )

    @pl.when(i == 2)
    def _():
        each = [sums[k : k + 1, :] for k in range(4)] + [total[k : k + 1, :] for k in range(4)]
        each += [gb1[:, k * 768 : (k + 1) * 768] for k in range(gb1.shape[1] // 768)]
        for k in range(16):
            block = jnp.zeros((16, 384), F32)
            if k < len(each):
                block = jnp.concatenate(
                    [each[k][:, :384], each[k][:, 384:], block[:14]], axis=0
                )
            lines[k ^ where[1]] = block.astype(BF16)


def input_back(where, xs, vecs, w, back_mid, back, sums, gb1):
    rows = xs[1].shape[0]
    return pl.pallas_call(
        input_back_kernel,
        grid=(3,),
        in_specs=[
            SMEM,
            pl.BlockSpec((1, rows, 768), lambda i: (i // 2, 0, 0)),
            VMEM,
            VMEM,
            ANY,
            pl.BlockSpec((rows, 768), lambda i: (i, 0)),
            pl.BlockSpec((3, rows, 768), lambda i: (0, i, 0)),
            VMEM,
            VMEM,
        ],
        out_specs=[pl.BlockSpec((1, rows, 768), lambda i: (i // 2, 0, 0)), VMEM, VMEM],
        out_shape=[
            shape_of((2, rows, 768), BF16),
            shape_of((rows, 768), BF16),
            shape_of((16, 16, 384), BF16),
        ],
        scratch_shapes=[
            pltpu.VMEM((8, 768), F32),
            pltpu.VMEM(w.shape, w.dtype),
            pltpu.SemaphoreType.DMA((1,)),
        ],
        compiler_params=limits(40),
        cost_estimate=lasting(9),
        name="input_back",
    )(where, *xs, vecs, w, back_mid, back, sums, gb1)


def finish_kernel(where, mine, other, *refs, with_lines):
    if with_lines:
        mine_rows, other_rows, out, *vectors, rows = refs
    else:
        (out,) = refs
    first = where[0] == 0
    for q in range(16):
        a, b = mine[q // 4, q % 4].astype(F32), other[q // 4, q % 4].astype(F32)
        at = pl.ds(pl.multiple_of((q ^ where[1]) * 48, 48), 48)
        out[at, :384] = jnp.where(first, a, b)
        out[at, 384:] = jnp.where(first, b, a)
    if not with_lines:
        return

    @pl.when(pl.program_id(0) == 0)
    def _():
        for q in range(16):
            both = mine_rows[q // 4, q % 4].astype(F32) + other_rows[q // 4, q % 4].astype(F32)
            rows[pl.ds(q ^ where[1], 1), :] = jnp.concatenate([both[0:1], both[1:2]], axis=1)
        for k in range(len(vectors) - 1):
            vectors[k][...] = rows[k, :]
        size = rows.shape[1]
        for k in range(vectors[-1].shape[0] // size):
            vectors[-1][pl.ds(k * size, size)] = rows[len(vectors) - 1 + k, :]


def finish(where, mine, other, start, count, across, with_lines=False):
    block = pl.BlockSpec((4, 4, 48, 384), lambda j: (0, 0, start + j, 0))
    spare = pl.BlockSpec((4, 4, 16, 384), lambda j: (0, 0, 3 * count, 0))
    shape = (768, 768 * count) if across else (768 * count, 768)
    result = [shape_of(shape, F32)]
    specs = [pl.BlockSpec((768, 768), (lambda j: (0, j)) if across else (lambda j: (j, 0)))]
    scratch = []
    if with_lines:
        result += [shape_of((768,), F32)] * 8 + [shape_of((3072,), F32)]
        specs += [VMEM] * 9
        scratch = [pltpu.VMEM((16, 768), F32)]
    out = pl.pallas_call(
        functools.partial(finish_kernel, with_lines=with_lines),
        grid=(count,),
        in_specs=[SMEM, block, block] + [spare, spare] * with_lines,
        out_specs=specs,
        out_shape=result,
        scratch_shapes=scratch,
        compiler_params=limits(40),
        cost_estimate=lasting(4),
        name="finish",
    )(where, mine, other, *[mine, other] * with_lines)
    return out if with_lines else out[0]


FIRST_TO = {
    (0, 0): (0, 0), (0, 1): (0, 1), (0, 2): (1, 0), (0, 3): (1, 1),
    (1, 0): (0, 2), (1, 1): (0, 3), (1, 2): (1, 2), (1, 3): (1, 3),
}
SECOND_TO = {
    (0, 0): (0, 1), (0, 1): (0, 0), (0, 2): (1, 1), (0, 3): (1, 0),
    (1, 0): (0, 3), (1, 1): (0, 2), (1, 2): (1, 3), (1, 3): (1, 2),
}


def column_pairs(table):
    pairs = []
    for chip in range(4):
        for (core, z), (core_to, z_to) in table.items():
            pairs.append(((chip * 2 + core) * 4 + z, (chip * 2 + core_to) * 4 + z_to))
    return pairs


def exchange_short(block):
    pairs = ([], [], [])
    for chip in range(4):
        for core in range(2):
            for z in range(4):
                if core == 1 and z % 2 == 1:
                    continue
                me = (chip * 2 + core) * 4 + z
                to = (chip * 2 + 1 - core) * 4
                pairs[0].append((me, (chip * 2 + core) * 4 + (z ^ 1)))
                pairs[1].append((me, to + z))
                pairs[2].append((me, to + (z ^ 1)))
    return tuple(lax.ppermute(block, ("dp", "blk"), p) for p in pairs)


CHIPS = [[0, 2, 4, 6], [1, 3, 5, 7]]


def flip_pairs(size, mask):
    return [(i, i ^ mask) for i in range(size)]


def swap(array, axis, mask):
    return lax.ppermute(array, axis, flip_pairs(8 if axis == "dp" else 4, mask))


def add_low(*terms):
    return sum(term.astype(F32) for term in terms).astype(BF16)


class Place:
    def __init__(self):
        dp = lax.axis_index("dp")
        self.z = lax.axis_index("blk")
        self.core = dp % 2
        self.chip = dp // 2


def after(value, *others):
    return lax.optimization_barrier((value,) + others)[0]


def by_chip(keep, got):
    return [add_low(keep[4 * k : 4 * k + 4], got[4 * k : 4 * k + 4]) for k in range(4)]


def over_chips(sums):
    return [swap(sums[k], "dp", 2 * k) for k in (1, 2, 3)]


def over_line(quarter):
    return [swap(quarter[k], "blk", k) for k in (1, 2, 3)]


def gather_all(part):
    every = lax.all_gather(part, ("dp", "blk"), axis=0)
    return every.reshape((4, 2, 4) + every.shape[1:])


def local_paired(
    tokens,
    counts,
    ln1_gain,
    ln1_shift,
    w_qkv,
    bias_q,
    bias_v,
    w_out,
    bias_out,
    ln2_gain,
    ln2_shift,
    w_fc1,
    bias_fc1,
    w_fc2,
    bias_fc2,
    cotangent,
):
    place = Place()
    odd = place.z % 2
    short = jnp.argmin(counts).astype(jnp.int32)
    full_one = jnp.where(short == 0, 1, 0)
    full_two = jnp.where(short == 2, 1, 2)
    slots = (jnp.where(odd == 0, full_one, full_two), jnp.where(odd == 0, full_two, full_one), short)
    tables = (FIRST_TO, SECOND_TO, FIRST_TO)

    def arrange(pieces):
        (one, three), two = pieces
        return jnp.stack(
            [
                jnp.where(slots[0] == i, one, jnp.where(slots[1] == i, two, three))
                for i in range(3)
            ]
        )

    where = jnp.stack(
        [place.core, place.chip * 4 + place.z, 2 * place.core + odd]
    ).astype(jnp.int32)

    def leaving(array):
        pieces = [lax.dynamic_index_in_dim(array, slot, 0, keepdims=False) for slot in slots]
        return jnp.stack([pieces[0], pieces[2]]), pieces[1]

    def move(pieces):
        return tuple(
            lax.ppermute(piece, ("dp", "blk"), column_pairs(table))
            for piece, table in zip(pieces, (FIRST_TO, SECOND_TO))
        )

    def give(pieces):
        return tuple(
            None
            if piece is None
            else lax.ppermute(piece, ("dp", "blk"), [pair[::-1] for pair in column_pairs(table)])
            for piece, table in zip(pieces, (FIRST_TO, SECOND_TO))
        )

    wide = w_fc1.shape[1] // 768
    rows = tokens.shape[1]
    vectors = [ln1_gain, ln1_shift, bias_q, bias_v, bias_out, ln2_gain, ln2_shift, bias_fc2]
    vecs, b1 = prepare(jnp.stack(vectors), bias_fc1.reshape(1, -1))
    vecs_one, vecs_two = vecs[:4], vecs[4:]
    token_sends = leaving(tokens)
    x13, x2 = move(token_sends)
    xs = (x13, x2)
    cot_sends = leaving(after(cotangent, *token_sends))
    x3 = after(x13[1], x2, vecs, *cot_sends)
    short_blocks = exchange_short(x3)
    q_full, kv_full = project(x13, after(x2, x3), vecs_one, w_qkv)
    kv_other = swap(kv_full, "dp", 1)
    cots = move(after(cot_sends, x3))
    seq = 2 * kv_full.shape[1]
    kv_both = [kv_full, kv_other]
    att_full, t_full = attend(q_full, kv_both, seq, 768, 384)
    spare = -(-(SHORT - 2 * rows) // LANES) * LANES
    q_short, kv_head, kv_tail = project_short(
        where, x13, *after(short_blocks, att_full), vecs_one, w_qkv, spare
    )
    kv_short = [kv_head, kv_tail]
    att_short, t_short = attend(q_short, kv_short, SHORT, 384, 384)
    cots = after(cots, att_short)
    o13, o2, mid, normed_two, hidden_low, send_a, keep_a, gb1 = feed(
        where, att_full, att_short, xs, cots, w_out, vecs_two, w_fc1, b1, w_fc2
    )
    got_a = swap(send_a, "dp", 1)
    home_one = give((o13, o2))
    sums_a = by_chip(keep_a, got_a)
    chips_a = over_chips(sums_a)
    back_att, back_mid, send_b, keep_b, feed_sums = feed_back(
        where, att_full, att_short, cots, w_out, vecs_two, after(mid, *sums_a), normed_two,
        hidden_low, w_fc1,
    )
    home = (after(home_one[0], back_mid), home_one[1])
    quarter_a = add_low(after(sums_a[0], back_mid, home[0]), *chips_a)
    line_a = over_line(quarter_a)
    got_b = swap(after(send_b, quarter_a), "dp", 1)

    n_full = q_full.shape[0]
    dq_short, keep_short, send_pair = attend_back(
        where, after(q_short, quarter_a), back_att, n_full, att_short, t_short, kv_short, SHORT,
        448, 0, 6, True,
    )
    home = (home[0], after(home[1], dq_short))
    part_a = add_low(after(quarter_a[0], dq_short, home[1]), *line_a)
    all_a = gather_all(part_a)
    got_pair = swap(after(send_pair, part_a), "dp", 1)
    sums_b = by_chip(after(keep_b, dq_short, part_a), got_b)
    chips_b = over_chips(sums_b)
    away = (1 - odd) * rows
    send_short = add_low(
        lax.dynamic_slice_in_dim(keep_short, away, rows, 1),
        lax.dynamic_slice_in_dim(after(got_pair, *sums_b), away, rows, 1),
    )
    got_near = swap(send_short, "blk", 1)
    dq_full, own_full, sent_full = attend_back(
        where, after(q_full, send_short), back_att, 0, att_full, t_full, kv_both, seq, 768, 0, 6
    )
    got_near = after(got_near, dq_full)
    quarter_b = add_low(after(sums_b[0], dq_full, got_near), *chips_b)
    got_full = swap(after(sent_full, quarter_b), "dp", 1)
    line_b = over_line(quarter_b)
    send_c, keep_c, back = project_back(
        where, xs, vecs_one, dq_full, dq_short, own_full, got_full, keep_short, got_pair, got_near
    )
    part_b = add_low(after(quarter_b[0], keep_c), *line_b)
    got_c = swap(after(send_c, part_b), "dp", 1)
    near_b = over_line([part_b] * 4)
    i13, i2, line_sums = input_back(
        where, xs, vecs_one, w_qkv, back_mid, after(back, part_b), feed_sums, gb1
    )
    near_b = jnp.stack([after(part_b, i2)] + near_b)
    half_b = lax.all_gather(near_b, "dp", axis=0, axis_index_groups=CHIPS)
    sums_c = [
        jnp.concatenate([total, line_sums[4 * k : 4 * k + 4]], axis=1)
        for k, total in enumerate(by_chip(after(keep_c, i2, near_b), got_c))
    ]
    chips_c = over_chips(sums_c)
    (i13_home,) = give((after(i13, *sums_c), None))[:1]
    output = arrange(after(home, *sums_c))
    all_a = after(all_a, *sums_c)
    halves_a = [all_a[:, c] for c in range(2)]
    grad_w_fc2 = finish(jnp.zeros((3,), jnp.int32), *halves_a, 0, wide, False)
    i13_home = after(i13_home, grad_w_fc2, output)
    quarter_c = add_low(after(sums_c[0], i13_home), *chips_c)
    line_c = over_line(quarter_c)
    part_c = add_low(quarter_c[0], *line_c)
    near_c = jnp.stack([part_c] + over_line([part_c] * 4))
    far_c = over_chips([near_c] * 4)
    i2_home = give((None, after(i2, near_c)))[1]
    half_b = after(half_b, near_c)
    other_b = swap(half_b, "dp", 1)
    inside = where * jnp.array([1, 0, 0], jnp.int32) + jnp.array([0, 1, 0], jnp.int32) * place.z
    grad_w_fc1 = finish(inside, half_b, other_b, 0, wide, True)
    grad_w_out = finish(inside, half_b, other_b, wide, 1, True)
    i2_home = after(i2_home, grad_w_fc1, grad_w_out)
    whole_c = jnp.stack([after(near_c, i2_home)] + far_c)
    other_c = swap(whole_c, "dp", 1)
    input_grad = arrange(after((i13_home, i2_home), whole_c)).astype(F32)
    grad_w_qkv, *lines = finish(where, whole_c, other_c, 0, 3, True, True)
    return (
        output,
        input_grad,
        lines[4],
        lines[5],
        grad_w_qkv,
        lines[6],
        lines[7],
        grad_w_out,
        lines[0],
        lines[1],
        lines[2],
        grad_w_fc1,
        lines[8],
        grad_w_fc2,
        lines[3],
    )


def solution(mesh):
    paired = mesh.shape["dp"] == 8 and mesh.shape["blk"] == 4
    chosen = local_paired if paired else local
    return jax.shard_map(
        chosen,
        mesh=mesh,
        in_specs=(
            P("dp", "blk", None),
            P("dp"),
            P(),
            P(),
            P(),
            P(),
            P(),
            P(),
            P(),
            P(),
            P(),
            P(),
            P(),
            P(),
            P(),
            P("dp", "blk", None),
        ),
        out_specs=(
            P("dp", "blk", None),
            P("dp", "blk", None),
            P(),
            P(),
            P(),
            P(),
            P(),
            P(),
            P(),
            P(),
            P(),
            P(),
            P(),
            P(),
            P(),
        ),
        check_vma=False,
    )
```

profile of v0, /device:TPU:0, one launch (start us, length us, event | category | flops | bytes accessed | tf_op | source)
XLA Modules:
  0.0 437.3 jit_solution(14188021971600880682)
XLA Ops:
  11.7 2.4 dynamic-slice_bitcast_fusion.1
  15.2 1.9 collective-permute-start
  17.1 3.0 collective-permute-start.1
  25.1 1.4 fusion.16
  26.5 7.9 %collective-permute-done.1.x2_in.x2 = bf16[384,768]{1,0:T(8,128)(2,1)S(1)} collective-permute-done((bf16[384,768]{1,0:T(8,128)(2,1)}, bf16[384,768]{1,0:T(8,128)(2,1)S(1)}, u32[]{:S(2)}, u32[]{:S(2)}) %collective-permute-start.1) | collective-permute-done | bytes 589856 | tf_op jit(solution)/shard_map/ppermute | solution.py:1246
  34.4 2.2 copy-done.9
  36.7 5.0 %project.1 = (bf16[768,768]{1,0:T(8,128)(2,1)S(1)}, bf16[2,768,768]{2,1,0:T(8,128)(2,1)}) custom-call(bf16[2,384,768]{2,1,0:T(8,128)(2,1)S(1)} %collective-permute-done.x13_in.x13, bf16[384,768]{1,0:T(8,128)(2,1)S(1)} %collective-permute-done.1.x2_in.x2, f32[4,768]{1,0:T(4,128)S(1)} %get-tuple-element.235.vecs, bf16[768,2304]{1,0:T(8,128)(2,1)S(1)} %copy-done.9), custom_call_target="tpu_custom_call" | custom-call | flops 4000000000 | bytes 1048576 | tf_op jit(solution)/shard_map/project/pallas_call | solution.py:458
  42.8 20.4 %collective-permute-start.2 = (bf16[2,768,768]{2,1,0:T(8,128)(2,1)}, bf16[2,768,768]{2,1,0:T(8,128)(2,1)}, u32[]{:S(2)}, u32[]{:S(2)}) collective-permute-start(bf16[2,768,768]{2,1,0:T(8,128)(2,1)} %get-tuple-element.109.refs_1_.refs_5_), channel_id=1, source_target_pairs={{0,4},{4,0},{8,12},{12,8},{16,20},{20,16},{24,28},{28,24},{1,5},{5... | collective-permute-start | bytes 7077896 | tf_op jit(solution)/shard_map/ppermute | solution.py:1165
  63.9 8.6 %collective-permute-start.3 = (bf16[384,768]{1,0:T(8,128)(2,1)S(1)}, bf16[384,768]{1,0:T(8,128)(2,1)S(1)}, u32[]{:S(2)}, u32[]{:S(2)}) collective-permute-start(bf16[384,768]{1,0:T(8,128)(2,1)S(1)} %slice_bitcast_fusion.2), channel_id=1, source_target_pairs={{0,1},{1,0},{2,3},{3,2},{4,5},{6,7},{8,9},{9,8},{10,11},{11,10},{1... | collective-permute-start | bytes 1769480 | tf_op jit(solution)/shard_map/ppermute | solution.py:1154
  72.4 1.9 collective-permute-start.4
  75.7 10.8 %collective-permute-start.6 = (bf16[2,384,768]{2,1,0:T(8,128)(2,1)}, bf16[2,384,768]{2,1,0:T(8,128)(2,1)}, u32[]{:S(2)}, u32[]{:S(2)}) collective-permute-start(bf16[2,384,768]{2,1,0:T(8,128)(2,1)} %pad_maximum_fusion.3), channel_id=1, source_target_pairs={{0,0},{1,1},{2,4},{3,5},{4,2},{5,3},{6,6},{7,7},{8,8},{9,9},{10,12... | collective-permute-start | bytes 3538952 | tf_op jit(solution)/shard_map/ppermute | solution.py:1246
  86.6 2.8 collective-permute-start.7
  89.3 24.8 %attend.2 = (f32[768,768]{1,0:T(8,128)}, bf16[768,768]{1,0:T(8,128)(2,1)}) custom-call(bf16[768,768]{1,0:T(8,128)(2,1)} %copy-done.15, bf16[2,768,768]{2,1,0:T(8,128)(2,1)} %get-tuple-element.109.refs_1_.refs_5_, bf16[2,768,768]{2,1,0:T(8,128)(2,1)} %collective-permute-done.2.refs_2_.refs_6_), custom_call_target="tpu_custom_call" | custom-call | flops 24999999488 | bytes 1048576 | tf_op jit(solution)/shard_map/attend/pallas_call | solution.py:593
  114.2 4.2 project_short.1
  121.4 11.3 %attend.3 = (f32[384,768]{1,0:T(8,128)}, bf16[384,768]{1,0:T(8,128)(2,1)}) custom-call(bf16[384,768]{1,0:T(8,128)(2,1)} %copy-done.17, bf16[2,768,768]{2,1,0:T(8,128)(2,1)} %copy-done.14, bf16[2,128,768]{2,1,0:T(8,128)(2,1)} %copy-done.18), custom_call_target="tpu_custom_call" | custom-call | flops 7000000000 | bytes 1048576 | tf_op jit(solution)/shard_map/attend/pallas_call | solution.py:593
  133.5 34.8 %feed.1 = (bf16[2,384,768]{2,1,0:T(8,128)(2,1)}, bf16[384,768]{1,0:T(8,128)(2,1)}, f32[1152,768]{1,0:T(8,128)}, bf16[1152,768]{1,0:T(8,128)(2,1)}, bf16[1152,307...) custom-call(s32[3]{0:T(128)} %copy-done.7, ...), custom_call_target="tpu_custom_call" | custom-call | flops 35999997952 | bytes 1048576 | tf_op jit(solution)/shard_map/feed/pallas_call | solution.py:792
  168.4 1.9 collective-permute-start.8
  170.4 2.8 collective-permute-done.9
  173.1 2.3 add_convert_fusion.7
  176.5 2.0 collective-permute-start.12
  179.0 24.3 %feed_back.1 = (bf16[1152,768]{1,0:T(8,128)(2,1)}, f32[1152,768]{1,0:T(8,128)}, bf16[16,240,384]{2,1,0:T(8,128)(2,1)}, bf16[16,240,384]{2,1,0:T(8,128)(2,1)}, f32[8,768]{1,0:T(8,128)}) custom-call(s32[3]{0:T(128)} %copy-done.7, f32[768,768]{1,0:T(8,128)} %get-tuple-element.110.att_full_in.refs_3_, f32[384,768]{1,0:T(8,128)} %get-tuple-element.117.att_short_in.refs_3_, ...), custom_call_target="tpu_custom_call" | custom-call | flops 25999998976 | bytes 1048576 | tf_op jit(solution)/shard_map/feed_back/pallas_call | solution.py:891
  204.6 1.7 add_convert_fusion.6
  207.3 3.7 collective-permute-start.15
  212.0 16.5 %attend_back.2 = (bf16[384,768]{1,0:T(8,128)(2,1)}, bf16[2,768,768]{2,1,0:T(8,128)(2,1)}, bf16[2,768,768]{2,1,0:T(8,128)(2,1)}) custom-call(s32[3]{0:T(128)} %copy-done.7, bf16[384,768]{1,0:T(8,128)(2,1)} %copy-done.17, bf16[1152,768]{1,0:T(8,128)(2,1)} %get-tuple-element.135.refs_2_, f32[384,768]{1,0:T(8,128)} %get-tuple-element.117.att_short_in.refs_3_, ...), custom_call_target="tpu_custom_call" | custom-call | flops 11000000512 | bytes 1048576 | tf_op jit(solution)/shard_map/attend_back/pallas_call | solution.py:681
  229.8 3.5 add_convert_fusion.2
  234.2 1.6 add_convert_fusion
  236.9 2.0 collective-permute-start.21
  239.4 37.7 %attend_back.3 = (bf16[768,768]{1,0:T(8,128)(2,1)}, bf16[2,768,768]{2,1,0:T(8,128)(2,1)}, bf16[2,768,768]{2,1,0:T(8,128)(2,1)}) custom-call(s32[3]{0:T(128)} %copy-done.7, bf16[768,768]{1,0:T(8,128)(2,1)} %copy-done.15, bf16[1152,768]{1,0:T(8,128)(2,1)} %get-tuple-element.135.refs_2_, f32[768,768]{1,0:T(8,128)} %get-tuple-element.110.att_full_in.refs_3_, ...), custom_call_target="tpu_custom_call" | custom-call | flops 38999998464 | bytes 1048576 | tf_op jit(solution)/shard_map/attend_back/pallas_call | solution.py:681
  279.5 2.1 collective-permute-start.24
  281.5 1.8 collective-permute-start.25
  284.7 1.4 copy-done.36
  286.1 11.9 %project_back.1 = (bf16[16,144,384]{2,1,0:T(8,128)(2,1)}, bf16[16,144,384]{2,1,0:T(8,128)(2,1)}, bf16[3,1152,768]{2,1,0:T(8,128)(2,1)}) custom-call(s32[3]{0:T(128)} %copy-done.7, bf16[2,384,768]{2,1,0:T(8,128)(2,1)} %copy-done.3, bf16[384,768]{1,0:T(8,128)(2,1)} %copy-done.12, f32[4,768]{1,0:T(4,128)} %copy-done.5, ...), custom_call_target="tpu_custom_call" | custom-call | flops 11000000512 | bytes 1048576 | tf_op jit(solution)/shard_map/project_back/pallas_call | solution.py:972
  299.0 8.2 %collective-permute-done.26 = bf16[240,384]{1,0:T(8,128)(2,1)S(1)} collective-permute-done((bf16[240,384]{1,0:T(8,128)(2,1)S(1)}, bf16[240,384]{1,0:T(8,128)(2,1)S(1)}, u32[]{:S(2)}, u32[]{:S(2)}) %collective-permute-start.26) | collective-permute-done | bytes 184352 | tf_op jit(solution)/shard_map/ppermute | solution.py:1165
  307.3 3.7 collective-permute-start.27
  311.4 2.1 collective-permute-start.29
  313.5 2.0 copy-done.11
  315.5 2.0 copy-done.16
  317.5 9.6 %input_back.1 = (bf16[2,384,768]{2,1,0:T(8,128)(2,1)S(1)}, bf16[384,768]{1,0:T(8,128)(2,1)S(1)}, bf16[16,16,384]{2,1,0:T(8,128)(2,1)S(1)}) custom-call(s32[3]{0:T(128)S(1)} %copy-done.8, bf16[2,384,768]{2,1,0:T(8,128)(2,1)S(1)} %copy-done.4, bf16[384,768]{1,0:T(8,128)(2,1)S(1)} %copy-done.13, f32[4,768]{1,0:T(4,128)S(1)} %copy-done.6, ...), custom_call_target="tpu_custom_call" | custom-call | flops 8999999488 | bytes 1048576 | tf_op jit(solution)/shard_map/input_back/pallas_call | solution.py:1042
  328.4 2.4 add_convert_fusion.12
  331.6 2.4 collective-permute-start.34
  336.8 1.7 collective-permute-start.31
  339.8 1.4 pad_maximum_fusion.1
  341.2 2.9 slice_bitcast_fusion
  344.0 4.9 %finish.4 = f32[3072,768]{1,0:T(8,128)} custom-call(s32[3]{0:T(128)S(1)} %broadcast_1_where.2.where, bf16[4,4,192,384]{3,2,1,0:T(8,128)(2,1)S(1)} %get-tuple-element.198.mine, bf16[4,4,192,384]{3,2,1,0:T(8,128)(2,1)S(1)} %get-tuple-element.197.other), custom_call_target="tpu_custom_call" | custom-call | flops 4000000000 | bytes 1048576 | tf_op jit(solution)/shard_map/finish/pallas_call | solution.py:1110
  348.9 4.8 %collective-permute-done.34 = bf16[4,160,384]{2,1,0:T(8,128)(2,1)} collective-permute-done((bf16[4,160,384]{2,1,0:T(8,128)(2,1)}, bf16[4,160,384]{2,1,0:T(8,128)(2,1)}, u32[]{:S(2)}, u32[]{:S(2)}) %collective-permute-start.34) | collective-permute-done | bytes 491552 | tf_op jit(solution)/shard_map/ppermute | solution.py:1165
  353.7 10.9 %collective-permute-done.33 = bf16[4,160,384]{2,1,0:T(8,128)(2,1)} collective-permute-done((bf16[4,160,384]{2,1,0:T(8,128)(2,1)}, bf16[4,160,384]{2,1,0:T(8,128)(2,1)}, u32[]{:S(2)}, u32[]{:S(2)}) %collective-permute-start.33) | collective-permute-done | bytes 491552 | tf_op jit(solution)/shard_map/ppermute | solution.py:1165
  364.7 1.6 add_convert_fusion.11
  366.3 2.1 collective-permute-start.35
  368.4 3.6 collective-permute-start.36
  372.0 8.9 %collective-permute-done.36 = bf16[160,384]{1,0:T(8,128)(2,1)S(1)} collective-permute-done((bf16[160,384]{1,0:T(8,128)(2,1)S(1)}, bf16[160,384]{1,0:T(8,128)(2,1)S(1)}, u32[]{:S(2)}, u32[]{:S(2)}) %collective-permute-start.36) | collective-permute-done | bytes 122912 | tf_op jit(solution)/shard_map/ppermute | solution.py:1165
  381.0 3.3 collective-permute-start.38
  386.8 1.9 collective-permute-done.38
  388.7 7.8 %collective-permute-done.39 = bf16[160,384]{1,0:T(8,128)(2,1)S(1)} collective-permute-done((bf16[160,384]{1,0:T(8,128)(2,1)S(1)}, bf16[160,384]{1,0:T(8,128)(2,1)S(1)}, u32[]{:S(2)}, u32[]{:S(2)}) %collective-permute-start.39) | collective-permute-done | bytes 122912 | tf_op jit(solution)/shard_map/ppermute | solution.py:1165
  396.7 1.4 collective-permute-start.43
  398.1 1.6 collective-permute-start.44
  400.2 2.9 collective-permute-start.41
  403.1 1.8 copy-done.2
  404.9 2.1 finish.6
  407.0 4.7 %finish.5 = f32[768,3072]{1,0:T(8,128)} custom-call(s32[3]{0:T(128)S(1)} %get-tuple-element.191.where, bf16[4,4,240,384]{3,2,1,0:T(8,128)(2,1)S(1)} %bitcast.108, bf16[4,4,240,384]{3,2,1,0:T(8,128)(2,1)S(1)} %collective-permute-done.42.other), custom_call_target="tpu_custom_call" | custom-call | flops 4000000000 | bytes 1048576 | tf_op jit(solution)/shard_map/finish/pallas_call | solution.py:1110
  411.7 5.4 %collective-permute-done.41 = bf16[384,768]{1,0:T(8,128)(2,1)S(1)} collective-permute-done((bf16[384,768]{1,0:T(8,128)(2,1)S(1)}, bf16[384,768]{1,0:T(8,128)(2,1)S(1)}, u32[]{:S(2)}, u32[]{:S(2)}) %collective-permute-start.41) | collective-permute-done | bytes 589856 | tf_op jit(solution)/shard_map/ppermute | solution.py:1254
  417.1 3.9 collective-permute-done.44
  422.3 1.4 fusion.1
  423.7 2.1 maximum_convert_fusion
  426.2 4.0 finish.7
  (174 shorter events, 39.6 us)
Async XLA Ops:
  7.2 334.0 %all-gather.5.cloned.1.call-start = ((), (), s32[]{:S(2)}) async-start(), calls=%async_computation | async-start | bytes 4866048 | tf_op jit(solution)/shard_map/all_gather | solution.py:1197
  14.1 6.1 %copy-start.21 = (bf16[3,384,768]{2,1,0:T(8,128)(2,1)S(1)}, bf16[3,384,768]{2,1,0:T(8,128)(2,1)}, u32[]{:S(2)}) copy-start(bf16[3,384,768]{2,1,0:T(8,128)(2,1)} %param.33) | copy-start | bytes 5308420
  15.2 11.3 %collective-permute-start = (bf16[2,384,768]{2,1,0:T(8,128)(2,1)}, bf16[2,384,768]{2,1,0:T(8,128)(2,1)S(1)}, u32[]{:S(2)}, u32[]{:S(2)}) collective-permute-start(bf16[2,384,768]{2,1,0:T(8,128)(2,1)} %pad_maximum_fusion.2), channel_id=1, source_target_pairs={{0,0},{1,1},{2,4},{3,5},{4,2},{5,3},{6,6},{7,7},{8,8},{9,9},{10,12... | collective-permute-start | bytes 3538952 | tf_op jit(solution)/shard_map/ppermute | solution.py:1246
  17.1 17.3 %collective-permute-start.1 = (bf16[384,768]{1,0:T(8,128)(2,1)}, bf16[384,768]{1,0:T(8,128)(2,1)S(1)}, u32[]{:S(2)}, u32[]{:S(2)}) collective-permute-start(bf16[384,768]{1,0:T(8,128)(2,1)} %get-tuple-element.216), channel_id=1, source_target_pairs={{0,1},{1,0},{2,5},{3,4},{4,3},{5,2},{6,7},{7,6},{8,9},{9,8},{10,13... | collective-permute-start | bytes 1769480 | tf_op jit(solution)/shard_map/ppermute | solution.py:1246
  26.5 87.6 %copy-start.5 = (f32[4,768]{1,0:T(4,128)}, f32[4,768]{1,0:T(4,128)S(1)}, u32[]{:S(2)}) copy-start(f32[4,768]{1,0:T(4,128)S(1)} %get-tuple-element.235.vecs) | copy-start | bytes 36868
  26.5 87.7 %copy-start.3 = (bf16[2,384,768]{2,1,0:T(8,128)(2,1)}, bf16[2,384,768]{2,1,0:T(8,128)(2,1)S(1)}, u32[]{:S(2)}) copy-start(bf16[2,384,768]{2,1,0:T(8,128)(2,1)S(1)} %collective-permute-done.x13_in.x13) | copy-start | bytes 3538948
  34.4 7.2 %copy-start.12 = (bf16[384,768]{1,0:T(8,128)(2,1)}, bf16[384,768]{1,0:T(8,128)(2,1)S(1)}, u32[]{:S(2)}) copy-start(bf16[384,768]{1,0:T(8,128)(2,1)S(1)} %collective-permute-done.1.x2_in.x2) | copy-start | bytes 1769476
  36.7 26.5 %copy-start.34 = (s32[3]{0:T(128)S(1)}, s32[3]{0:T(128)}, u32[]{:S(2)}) copy-start(s32[3]{0:T(128)} %constant.74.clone) | copy-start | bytes 40
  42.8 43.8 %collective-permute-start.2 = (bf16[2,768,768]{2,1,0:T(8,128)(2,1)}, bf16[2,768,768]{2,1,0:T(8,128)(2,1)}, u32[]{:S(2)}, u32[]{:S(2)}) collective-permute-start(bf16[2,768,768]{2,1,0:T(8,128)(2,1)} %get-tuple-element.109.refs_1_.refs_5_), channel_id=1, source_target_pairs={{0,4},{4,0},{8,12},{12,8},{16,20},{20,16},{24,28},{28,24},{1,5},{5... | collective-permute-start | bytes 7077896 | tf_op jit(solution)/shard_map/ppermute | solution.py:1165
  63.9 50.3 %copy-start.7 = (s32[3]{0:T(128)}, s32[3]{0:T(128)S(1)}, u32[]{:S(2)}) copy-start(s32[3]{0:T(128)S(1)} %get-tuple-element.192.where.refs_0_) | copy-start | bytes 40
  63.9 50.2 %collective-permute-start.3 = (bf16[384,768]{1,0:T(8,128)(2,1)S(1)}, bf16[384,768]{1,0:T(8,128)(2,1)S(1)}, u32[]{:S(2)}, u32[]{:S(2)}) collective-permute-start(bf16[384,768]{1,0:T(8,128)(2,1)S(1)} %slice_bitcast_fusion.2), channel_id=1, source_target_pairs={{0,1},{1,0},{2,3},{3,2},{4,5},{6,7},{8,9},{9,8},{10,11},{11,10},{1... | collective-permute-start | bytes 1769480 | tf_op jit(solution)/shard_map/ppermute | solution.py:1154
  72.4 41.7 %collective-permute-start.4 = (bf16[384,768]{1,0:T(8,128)(2,1)S(1)}, bf16[384,768]{1,0:T(8,128)(2,1)S(1)}, u32[]{:S(2)}, u32[]{:S(2)}) collective-permute-start(bf16[384,768]{1,0:T(8,128)(2,1)S(1)} %slice_bitcast_fusion.2), channel_id=1, source_target_pairs={{0,4},{1,5},{2,6},{3,7},{4,0},{6,2},{8,12},{9,13},{10,14},{11,15},... | collective-permute-start | bytes 1769480 | tf_op jit(solution)/shard_map/ppermute | solution.py:1154
  74.4 39.8 %collective-permute-start.5 = (bf16[384,768]{1,0:T(8,128)(2,1)S(1)}, bf16[384,768]{1,0:T(8,128)(2,1)S(1)}, u32[]{:S(2)}, u32[]{:S(2)}) collective-permute-start(bf16[384,768]{1,0:T(8,128)(2,1)S(1)} %slice_bitcast_fusion.2), channel_id=1, source_target_pairs={{0,5},{1,4},{2,7},{3,6},{4,1},{6,3},{8,13},{9,12},{10,15},{11,14},... | collective-permute-start | bytes 1769480 | tf_op jit(solution)/shard_map/ppermute | solution.py:1154
  75.7 57.0 %collective-permute-start.6 = (bf16[2,384,768]{2,1,0:T(8,128)(2,1)}, bf16[2,384,768]{2,1,0:T(8,128)(2,1)}, u32[]{:S(2)}, u32[]{:S(2)}) collective-permute-start(bf16[2,384,768]{2,1,0:T(8,128)(2,1)} %pad_maximum_fusion.3), channel_id=1, source_target_pairs={{0,0},{1,1},{2,4},{3,5},{4,2},{5,3},{6,6},{7,7},{8,8},{9,9},{10,12... | collective-permute-start | bytes 3538952 | tf_op jit(solution)/shard_map/ppermute | solution.py:1246
  86.6 46.1 %collective-permute-start.7 = (bf16[384,768]{1,0:T(8,128)(2,1)}, bf16[384,768]{1,0:T(8,128)(2,1)S(1)}, u32[]{:S(2)}, u32[]{:S(2)}) collective-permute-start(bf16[384,768]{1,0:T(8,128)(2,1)} %get-tuple-element.119), channel_id=1, source_target_pairs={{0,1},{1,0},{2,5},{3,4},{4,3},{5,2},{6,7},{7,6},{8,9},{9,8},{10,13... | collective-permute-start | bytes 1769480 | tf_op jit(solution)/shard_map/ppermute | solution.py:1246
  89.3 24.8 %copy-start.10 = (bf16[768,2304]{1,0:T(8,128)(2,1)S(1)}, bf16[768,2304]{1,0:T(8,128)(2,1)}, u32[]{:S(2)}) copy-start(bf16[768,2304]{1,0:T(8,128)(2,1)} %w_in.5) | copy-start | bytes 10616836
  168.3 4.8 %collective-permute-start.9 = (bf16[16,192,384]{2,1,0:T(8,128)(2,1)}, bf16[16,192,384]{2,1,0:T(8,128)(2,1)S(1)}, u32[]{:S(2)}, u32[]{:S(2)}) collective-permute-start(bf16[16,192,384]{2,1,0:T(8,128)(2,1)} %get-tuple-element.126), channel_id=1, source_target_pairs={{0,4},{4,0},{8,12},{12,8},{16,20},{20,16},{24,28},{28,24},{1,5},{5... | collective-permute-start | bytes 7077896 | tf_op jit(solution)/shard_map/ppermute | solution.py:1165
  168.4 34.9 %collective-permute-start.8 = (bf16[2,384,768]{2,1,0:T(8,128)(2,1)}, bf16[2,384,768]{2,1,0:T(8,128)(2,1)S(1)}, u32[]{:S(2)}, u32[]{:S(2)}) collective-permute-start(bf16[2,384,768]{2,1,0:T(8,128)(2,1)} %get-tuple-element.123), channel_id=1, source_target_pairs={{0,0},{1,1},{4,2},{5,3},{2,4},{3,5},{6,6},{7,7},{8,8},{9,9},{12,10... | collective-permute-start | bytes 3538952 | tf_op jit(solution)/shard_map/ppermute | solution.py:1254
  170.3 58.2 %collective-permute-start.10 = (bf16[384,768]{1,0:T(8,128)(2,1)}, bf16[384,768]{1,0:T(8,128)(2,1)}, u32[]{:S(2)}, u32[]{:S(2)}) collective-permute-start(bf16[384,768]{1,0:T(8,128)(2,1)} %get-tuple-element.132), channel_id=1, source_target_pairs={{1,0},{0,1},{5,2},{4,3},{3,4},{2,5},{7,6},{6,7},{9,8},{8,9},{13,10... | collective-permute-start | bytes 1769480 | tf_op jit(solution)/shard_map/ppermute | solution.py:1254
  175.4 27.9 %collective-permute-start.11 = (bf16[4,192,384]{2,1,0:T(8,128)(2,1)S(1)}, bf16[4,192,384]{2,1,0:T(8,128)(2,1)}, u32[]{:S(2)}, u32[]{:S(2)}) collective-permute-start(bf16[4,192,384]{2,1,0:T(8,128)(2,1)S(1)} %get-tuple-element.201), channel_id=1, source_target_pairs={{0,8},{4,12},{8,0},{12,4},{16,24},{20,28},{24,16},{28,20},{1,9},{5... | collective-permute-start | bytes 1769480 | tf_op jit(solution)/shard_map/ppermute | solution.py:1165
  176.5 27.2 %collective-permute-start.12 = (bf16[4,192,384]{2,1,0:T(8,128)(2,1)S(1)}, bf16[4,192,384]{2,1,0:T(8,128)(2,1)}, u32[]{:S(2)}, u32[]{:S(2)}) collective-permute-start(bf16[4,192,384]{2,1,0:T(8,128)(2,1)S(1)} %get-tuple-element.200), channel_id=1, source_target_pairs={{0,16},{4,20},{8,24},{12,28},{16,0},{20,4},{24,8},{28,12},{1,17},{... | collective-permute-start | bytes 1769480 | tf_op jit(solution)/shard_map/ppermute | solution.py:1165
  178.5 26.1 %collective-permute-start.13 = (bf16[4,192,384]{2,1,0:T(8,128)(2,1)S(1)}, bf16[4,192,384]{2,1,0:T(8,128)(2,1)}, u32[]{:S(2)}, u32[]{:S(2)}) collective-permute-start(bf16[4,192,384]{2,1,0:T(8,128)(2,1)S(1)} %get-tuple-element.199), channel_id=1, source_target_pairs={{0,24},{4,28},{8,16},{12,20},{16,8},{20,12},{24,0},{28,4},{1,25},{... | collective-permute-start | bytes 1769480 | tf_op jit(solution)/shard_map/ppermute | solution.py:1165
  206.4 22.1 %collective-permute-start.14 = (bf16[192,384]{1,0:T(8,128)(2,1)S(1)}, bf16[192,384]{1,0:T(8,128)(2,1)S(1)}, u32[]{:S(2)}, u32[]{:S(2)}) collective-permute-start(bf16[192,384]{1,0:T(8,128)(2,1)S(1)} %get-tuple-element.226), channel_id=1, source_target_pairs={{0,1},{1,0},{2,3},{3,2},{4,5},{5,4},{6,7},{7,6},{8,9},{9,8},{10,11... | collective-permute-start | bytes 442376 | tf_op jit(solution)/shard_map/ppermute | solution.py:1165
  207.3 21.3 %collective-permute-start.15 = (bf16[192,384]{1,0:T(8,128)(2,1)S(1)}, bf16[192,384]{1,0:T(8,128)(2,1)S(1)}, u32[]{:S(2)}, u32[]{:S(2)}) collective-permute-start(bf16[192,384]{1,0:T(8,128)(2,1)S(1)} %get-tuple-element.225), channel_id=1, source_target_pairs={{0,2},{1,3},{2,0},{3,1},{4,6},{5,7},{6,4},{7,5},{8,10},{9,11},{10,... | collective-permute-start | bytes 442376 | tf_op jit(solution)/shard_map/ppermute | solution.py:1165
  211.0 17.6 %collective-permute-start.16 = (bf16[192,384]{1,0:T(8,128)(2,1)S(1)}, bf16[192,384]{1,0:T(8,128)(2,1)S(1)}, u32[]{:S(2)}, u32[]{:S(2)}) collective-permute-start(bf16[192,384]{1,0:T(8,128)(2,1)S(1)} %get-tuple-element.224), channel_id=1, source_target_pairs={{0,3},{1,2},{2,1},{3,0},{4,7},{5,6},{6,5},{7,4},{8,11},{9,10},{10,... | collective-permute-start | bytes 442376 | tf_op jit(solution)/shard_map/ppermute | solution.py:1165
  211.0 18.8 %collective-permute-start.18 = (bf16[16,240,384]{2,1,0:T(8,128)(2,1)}, bf16[16,240,384]{2,1,0:T(8,128)(2,1)}, u32[]{:S(2)}, u32[]{:S(2)}) collective-permute-start(bf16[16,240,384]{2,1,0:T(8,128)(2,1)} %get-tuple-element.146), channel_id=1, source_target_pairs={{0,4},{4,0},{8,12},{12,8},{16,20},{20,16},{24,28},{28,24},{1,5},{5... | collective-permute-start | bytes 8847368 | tf_op jit(solution)/shard_map/ppermute | solution.py:1165
  229.3 4.9 %collective-permute-start.17 = (bf16[2,768,768]{2,1,0:T(8,128)(2,1)}, bf16[2,768,768]{2,1,0:T(8,128)(2,1)}, u32[]{:S(2)}, u32[]{:S(2)}) collective-permute-start(bf16[2,768,768]{2,1,0:T(8,128)(2,1)} %get-tuple-element.142), channel_id=1, source_target_pairs={{0,4},{4,0},{8,12},{12,8},{16,20},{20,16},{24,28},{28,24},{1,5},{5... | collective-permute-start | bytes 7077896 | tf_op jit(solution)/shard_map/ppermute | solution.py:1165
  229.3 167.2 %all-gather.7.cloned.1.call-start = ((), (), s32[]{:S(2)}) async-start(), calls=%async_computation.1 | async-start | bytes 3686400 | tf_op jit(solution)/shard_map/all_gather | solution.py:1332
  229.8 4.4 %copy-start.24 = (bf16[2,768,768]{2,1,0:T(8,128)(2,1)S(1)}, bf16[2,768,768]{2,1,0:T(8,128)(2,1)}, u32[]{:S(2)}) copy-start(bf16[2,768,768]{2,1,0:T(8,128)(2,1)} %get-tuple-element.139.keep_short_in) | copy-start | bytes 7077892
  235.8 41.3 %collective-permute-start.19 = (bf16[2,384,768]{2,1,0:T(8,128)(2,1)S(1)}, bf16[2,384,768]{2,1,0:T(8,128)(2,1)S(1)}, u32[]{:S(2)}, u32[]{:S(2)}) collective-permute-start(bf16[2,384,768]{2,1,0:T(8,128)(2,1)S(1)} %add_convert_fusion), channel_id=1, source_target_pairs={{0,1},{1,0},{2,3},{3,2},{4,5},{5,4},{6,7},{7,6},{8,9},{9,8},{10,11... | collective-permute-start | bytes 3538952 | tf_op jit(solution)/shard_map/ppermute | solution.py:1165
  235.8 41.2 %collective-permute-start.20 = (bf16[4,240,384]{2,1,0:T(8,128)(2,1)S(1)}, bf16[4,240,384]{2,1,0:T(8,128)(2,1)S(1)}, u32[]{:S(2)}, u32[]{:S(2)}) collective-permute-start(bf16[4,240,384]{2,1,0:T(8,128)(2,1)S(1)} %get-tuple-element.195), channel_id=1, source_target_pairs={{0,8},{4,12},{8,0},{12,4},{16,24},{20,28},{24,16},{28,20},{1,9},{5... | collective-permute-start | bytes 2211848 | tf_op jit(solution)/shard_map/ppermute | solution.py:1165
  236.9 40.2 %collective-permute-start.21 = (bf16[4,240,384]{2,1,0:T(8,128)(2,1)S(1)}, bf16[4,240,384]{2,1,0:T(8,128)(2,1)S(1)}, u32[]{:S(2)}, u32[]{:S(2)}) collective-permute-start(bf16[4,240,384]{2,1,0:T(8,128)(2,1)S(1)} %get-tuple-element.194), channel_id=1, source_target_pairs={{0,16},{4,20},{8,24},{12,28},{16,0},{20,4},{24,8},{28,12},{1,17},{... | collective-permute-start | bytes 2211848 | tf_op jit(solution)/shard_map/ppermute | solution.py:1165
  238.9 38.2 %collective-permute-start.22 = (bf16[4,240,384]{2,1,0:T(8,128)(2,1)S(1)}, bf16[4,240,384]{2,1,0:T(8,128)(2,1)S(1)}, u32[]{:S(2)}, u32[]{:S(2)}) collective-permute-start(bf16[4,240,384]{2,1,0:T(8,128)(2,1)S(1)} %get-tuple-element.193), channel_id=1, source_target_pairs={{0,24},{4,28},{8,16},{12,20},{16,8},{20,12},{24,0},{28,4},{1,25},{... | collective-permute-start | bytes 2211848 | tf_op jit(solution)/shard_map/ppermute | solution.py:1165
  279.4 5.3 %collective-permute-start.23 = (bf16[2,768,768]{2,1,0:T(8,128)(2,1)S(1)}, bf16[2,768,768]{2,1,0:T(8,128)(2,1)S(1)}, u32[]{:S(2)}, u32[]{:S(2)}) collective-permute-start(bf16[2,768,768]{2,1,0:T(8,128)(2,1)S(1)} %copy-done.35), channel_id=1, source_target_pairs={{0,4},{4,0},{8,12},{12,8},{16,20},{20,16},{24,28},{28,24},{1,5},{5... | collective-permute-start | bytes 7077896 | tf_op jit(solution)/shard_map/ppermute | solution.py:1165
  279.5 19.6 %collective-permute-start.24 = (bf16[240,384]{1,0:T(8,128)(2,1)S(1)}, bf16[240,384]{1,0:T(8,128)(2,1)S(1)}, u32[]{:S(2)}, u32[]{:S(2)}) collective-permute-start(bf16[240,384]{1,0:T(8,128)(2,1)S(1)} %get-tuple-element.222), channel_id=1, source_target_pairs={{0,1},{1,0},{2,3},{3,2},{4,5},{5,4},{6,7},{7,6},{8,9},{9,8},{10,11... | collective-permute-start | bytes 552968 | tf_op jit(solution)/shard_map/ppermute | solution.py:1165
  281.5 17.5 %collective-permute-start.25 = (bf16[240,384]{1,0:T(8,128)(2,1)S(1)}, bf16[240,384]{1,0:T(8,128)(2,1)S(1)}, u32[]{:S(2)}, u32[]{:S(2)}) collective-permute-start(bf16[240,384]{1,0:T(8,128)(2,1)S(1)} %get-tuple-element.221), channel_id=1, source_target_pairs={{0,2},{1,3},{2,0},{3,1},{4,6},{5,7},{6,4},{7,5},{8,10},{9,11},{10,... | collective-permute-start | bytes 552968 | tf_op jit(solution)/shard_map/ppermute | solution.py:1165
  283.3 23.9 %collective-permute-start.26 = (bf16[240,384]{1,0:T(8,128)(2,1)S(1)}, bf16[240,384]{1,0:T(8,128)(2,1)S(1)}, u32[]{:S(2)}, u32[]{:S(2)}) collective-permute-start(bf16[240,384]{1,0:T(8,128)(2,1)S(1)} %get-tuple-element.220), channel_id=1, source_target_pairs={{0,3},{1,2},{2,1},{3,0},{4,7},{5,6},{6,5},{7,4},{8,11},{9,10},{10,... | collective-permute-start | bytes 552968 | tf_op jit(solution)/shard_map/ppermute | solution.py:1165
  286.1 27.4 %copy-start.4 = (bf16[2,384,768]{2,1,0:T(8,128)(2,1)S(1)}, bf16[2,384,768]{2,1,0:T(8,128)(2,1)}, u32[]{:S(2)}) copy-start(bf16[2,384,768]{2,1,0:T(8,128)(2,1)} %copy-done.3) | copy-start | bytes 3538948
  286.1 27.4 %copy-start.6 = (f32[4,768]{1,0:T(4,128)S(1)}, f32[4,768]{1,0:T(4,128)}, u32[]{:S(2)}) copy-start(f32[4,768]{1,0:T(4,128)} %copy-done.5) | copy-start | bytes 36868
  286.1 27.4 %copy-start.8 = (s32[3]{0:T(128)S(1)}, s32[3]{0:T(128)}, u32[]{:S(2)}) copy-start(s32[3]{0:T(128)} %copy-done.7) | copy-start | bytes 40
  286.1 27.4 %copy-start.13 = (bf16[384,768]{1,0:T(8,128)(2,1)S(1)}, bf16[384,768]{1,0:T(8,128)(2,1)}, u32[]{:S(2)}) copy-start(bf16[384,768]{1,0:T(8,128)(2,1)} %copy-done.12) | copy-start | bytes 1769476
  286.1 27.4 %copy-start.19 = (f32[8,768]{1,0:T(8,128)S(1)}, f32[8,768]{1,0:T(8,128)}, u32[]{:S(2)}) copy-start(f32[8,768]{1,0:T(8,128)} %get-tuple-element.160.sums) | copy-start | bytes 73732
  286.1 27.4 %copy-start.20 = (f32[1,3072]{1,0:T(1,128)S(1)}, f32[1,3072]{1,0:T(1,128)}, u32[]{:S(2)}) copy-start(f32[1,3072]{1,0:T(1,128)} %get-tuple-element.161.gb1) | copy-start | bytes 36868
  307.3 19.7 %collective-permute-start.27 = (bf16[240,384]{1,0:T(8,128)(2,1)S(1)}, bf16[240,384]{1,0:T(8,128)(2,1)S(1)}, u32[]{:S(2)}, u32[]{:S(2)}) collective-permute-start(bf16[240,384]{1,0:T(8,128)(2,1)S(1)} %add_convert_fusion.16), channel_id=1, source_target_pairs={{0,1},{1,0},{2,3},{3,2},{4,5},{5,4},{6,7},{7,6},{8,9},{9,8},{10,11... | collective-permute-start | bytes 552968 | tf_op jit(solution)/shard_map/ppermute | solution.py:1165
  311.0 16.3 %collective-permute-start.28 = (bf16[240,384]{1,0:T(8,128)(2,1)S(1)}, bf16[240,384]{1,0:T(8,128)(2,1)S(1)}, u32[]{:S(2)}, u32[]{:S(2)}) collective-permute-start(bf16[240,384]{1,0:T(8,128)(2,1)S(1)} %add_convert_fusion.16), channel_id=1, source_target_pairs={{0,2},{1,3},{2,0},{3,1},{4,6},{5,7},{6,4},{7,5},{8,10},{9,11},{10,... | collective-permute-start | bytes 552968 | tf_op jit(solution)/shard_map/ppermute | solution.py:1165
  311.4 16.0 %collective-permute-start.29 = (bf16[240,384]{1,0:T(8,128)(2,1)S(1)}, bf16[240,384]{1,0:T(8,128)(2,1)S(1)}, u32[]{:S(2)}, u32[]{:S(2)}) collective-permute-start(bf16[240,384]{1,0:T(8,128)(2,1)S(1)} %add_convert_fusion.16), channel_id=1, source_target_pairs={{0,3},{1,2},{2,1},{3,0},{4,7},{5,6},{6,5},{7,4},{8,11},{9,10},{10,... | collective-permute-start | bytes 552968 | tf_op jit(solution)/shard_map/ppermute | solution.py:1165
  313.4 15.0 %collective-permute-start.30 = (bf16[16,144,384]{2,1,0:T(8,128)(2,1)}, bf16[16,144,384]{2,1,0:T(8,128)(2,1)}, u32[]{:S(2)}, u32[]{:S(2)}) collective-permute-start(bf16[16,144,384]{2,1,0:T(8,128)(2,1)} %get-tuple-element.166), channel_id=1, source_target_pairs={{0,4},{4,0},{8,12},{12,8},{16,20},{20,16},{24,28},{28,24},{1,5},{5... | collective-permute-start | bytes 5308424 | tf_op jit(solution)/shard_map/ppermute | solution.py:1165
  330.8 7.7 %copy-start.23 = (bf16[2,384,768]{2,1,0:T(8,128)(2,1)S(1)}, bf16[2,384,768]{2,1,0:T(8,128)(2,1)}, u32[]{:S(2)}) copy-start(bf16[2,384,768]{2,1,0:T(8,128)(2,1)} %copy-done.22) | copy-start | bytes 3538948
  331.6 22.1 %collective-permute-start.34 = (bf16[4,160,384]{2,1,0:T(8,128)(2,1)}, bf16[4,160,384]{2,1,0:T(8,128)(2,1)}, u32[]{:S(2)}, u32[]{:S(2)}) collective-permute-start(bf16[4,160,384]{2,1,0:T(8,128)(2,1)} %pad_maximum_fusion.8), channel_id=1, source_target_pairs={{0,24},{4,28},{8,16},{12,20},{16,8},{20,12},{24,0},{28,4},{1,25},{... | collective-permute-start | bytes 1474568 | tf_op jit(solution)/shard_map/ppermute | solution.py:1165
  334.8 29.8 %collective-permute-start.33 = (bf16[4,160,384]{2,1,0:T(8,128)(2,1)}, bf16[4,160,384]{2,1,0:T(8,128)(2,1)}, u32[]{:S(2)}, u32[]{:S(2)}) collective-permute-start(bf16[4,160,384]{2,1,0:T(8,128)(2,1)} %pad_maximum_fusion.7), channel_id=1, source_target_pairs={{0,16},{4,20},{8,24},{12,28},{16,0},{20,4},{24,8},{28,12},{1,17},{... | collective-permute-start | bytes 1474568 | tf_op jit(solution)/shard_map/ppermute | solution.py:1165
  336.2 28.5 %collective-permute-start.32 = (bf16[4,160,384]{2,1,0:T(8,128)(2,1)}, bf16[4,160,384]{2,1,0:T(8,128)(2,1)}, u32[]{:S(2)}, u32[]{:S(2)}) collective-permute-start(bf16[4,160,384]{2,1,0:T(8,128)(2,1)} %pad_maximum_fusion.6), channel_id=1, source_target_pairs={{0,8},{4,12},{8,0},{12,4},{16,24},{20,28},{24,16},{28,20},{1,9},{5... | collective-permute-start | bytes 1474568 | tf_op jit(solution)/shard_map/ppermute | solution.py:1165
  336.8 12.1 %collective-permute-start.31 = (bf16[2,384,768]{2,1,0:T(8,128)(2,1)S(1)}, bf16[2,384,768]{2,1,0:T(8,128)(2,1)}, u32[]{:S(2)}, u32[]{:S(2)}) collective-permute-start(bf16[2,384,768]{2,1,0:T(8,128)(2,1)S(1)} %get-tuple-element.171), channel_id=1, source_target_pairs={{0,0},{1,1},{4,2},{5,3},{2,4},{3,5},{6,6},{7,7},{8,8},{9,9},{12,10... | collective-permute-start | bytes 3538952 | tf_op jit(solution)/shard_map/ppermute | solution.py:1254
  366.3 5.7 %collective-permute-start.35 = (bf16[160,384]{1,0:T(8,128)(2,1)S(1)}, bf16[160,384]{1,0:T(8,128)(2,1)S(1)}, u32[]{:S(2)}, u32[]{:S(2)}) collective-permute-start(bf16[160,384]{1,0:T(8,128)(2,1)S(1)} %get-tuple-element.227), channel_id=1, source_target_pairs={{0,1},{1,0},{2,3},{3,2},{4,5},{5,4},{6,7},{7,6},{8,9},{9,8},{10,11... | collective-permute-start | bytes 368648 | tf_op jit(solution)/shard_map/ppermute | solution.py:1165
  368.4 12.5 %collective-permute-start.36 = (bf16[160,384]{1,0:T(8,128)(2,1)S(1)}, bf16[160,384]{1,0:T(8,128)(2,1)S(1)}, u32[]{:S(2)}, u32[]{:S(2)}) collective-permute-start(bf16[160,384]{1,0:T(8,128)(2,1)S(1)} %get-tuple-element.229), channel_id=1, source_target_pairs={{0,2},{1,3},{2,0},{3,1},{4,6},{5,7},{6,4},{7,5},{8,10},{9,11},{10,... | collective-permute-start | bytes 368648 | tf_op jit(solution)/shard_map/ppermute | solution.py:1165
  372.0 8.9 %collective-permute-start.37 = (bf16[160,384]{1,0:T(8,128)(2,1)S(1)}, bf16[160,384]{1,0:T(8,128)(2,1)S(1)}, u32[]{:S(2)}, u32[]{:S(2)}) collective-permute-start(bf16[160,384]{1,0:T(8,128)(2,1)S(1)} %get-tuple-element.228), channel_id=1, source_target_pairs={{0,3},{1,2},{2,1},{3,0},{4,7},{5,6},{6,5},{7,4},{8,11},{9,10},{10,... | collective-permute-start | bytes 368648 | tf_op jit(solution)/shard_map/ppermute | solution.py:1165
  381.0 7.7 %collective-permute-start.38 = (bf16[160,384]{1,0:T(8,128)(2,1)S(1)}, bf16[160,384]{1,0:T(8,128)(2,1)S(1)}, u32[]{:S(2)}, u32[]{:S(2)}) collective-permute-start(bf16[160,384]{1,0:T(8,128)(2,1)S(1)} %fusion.14), channel_id=1, source_target_pairs={{0,1},{1,0},{2,3},{3,2},{4,5},{5,4},{6,7},{7,6},{8,9},{9,8},{10,11... | collective-permute-start | bytes 368648 | tf_op jit(solution)/shard_map/ppermute | solution.py:1165
  384.3 12.2 %collective-permute-start.39 = (bf16[160,384]{1,0:T(8,128)(2,1)S(1)}, bf16[160,384]{1,0:T(8,128)(2,1)S(1)}, u32[]{:S(2)}, u32[]{:S(2)}) collective-permute-start(bf16[160,384]{1,0:T(8,128)(2,1)S(1)} %fusion.14), channel_id=1, source_target_pairs={{0,2},{1,3},{2,0},{3,1},{4,6},{5,7},{6,4},{7,5},{8,10},{9,11},{10,... | collective-permute-start | bytes 368648 | tf_op jit(solution)/shard_map/ppermute | solution.py:1165
  385.4 11.0 %collective-permute-start.40 = (bf16[160,384]{1,0:T(8,128)(2,1)S(1)}, bf16[160,384]{1,0:T(8,128)(2,1)S(1)}, u32[]{:S(2)}, u32[]{:S(2)}) collective-permute-start(bf16[160,384]{1,0:T(8,128)(2,1)S(1)} %fusion.14), channel_id=1, source_target_pairs={{0,3},{1,2},{2,1},{3,0},{4,7},{5,6},{6,5},{7,4},{8,11},{9,10},{10,... | collective-permute-start | bytes 368648 | tf_op jit(solution)/shard_map/ppermute | solution.py:1165
  396.6 6.5 %collective-permute-start.42 = (bf16[4,4,240,384]{3,2,1,0:T(8,128)(2,1)}, bf16[4,4,240,384]{3,2,1,0:T(8,128)(2,1)S(1)}, u32[]{:S(2)}, u32[]{:S(2)}) collective-permute-start(bf16[4,4,240,384]{3,2,1,0:T(8,128)(2,1)} %bitcast.106), channel_id=1, source_target_pairs={{0,4},{4,0},{8,12},{12,8},{16,20},{20,16},{24,28},{28,24},{1,5},{5... | collective-permute-start | bytes 8847368 | tf_op jit(solution)/shard_map/ppermute | solution.py:1165
  396.7 20.4 %collective-permute-start.43 = (bf16[4,160,384]{2,1,0:T(8,128)(2,1)S(1)}, bf16[4,160,384]{2,1,0:T(8,128)(2,1)S(1)}, u32[]{:S(2)}, u32[]{:S(2)}) collective-permute-start(bf16[4,160,384]{2,1,0:T(8,128)(2,1)S(1)} %pad_maximum_fusion.9), channel_id=1, source_target_pairs={{0,8},{4,12},{8,0},{12,4},{16,24},{20,28},{24,16},{28,20},{1,9},{5... | collective-permute-start | bytes 1474568 | tf_op jit(solution)/shard_map/ppermute | solution.py:1165
  398.1 22.9 %collective-permute-start.44 = (bf16[4,160,384]{2,1,0:T(8,128)(2,1)S(1)}, bf16[4,160,384]{2,1,0:T(8,128)(2,1)S(1)}, u32[]{:S(2)}, u32[]{:S(2)}) collective-permute-start(bf16[4,160,384]{2,1,0:T(8,128)(2,1)S(1)} %pad_maximum_fusion.9), channel_id=1, source_target_pairs={{0,16},{4,20},{8,24},{12,28},{16,0},{20,4},{24,8},{28,12},{1,17},{... | collective-permute-start | bytes 1474568 | tf_op jit(solution)/shard_map/ppermute | solution.py:1165
  399.6 22.3 %collective-permute-start.45 = (bf16[4,160,384]{2,1,0:T(8,128)(2,1)S(1)}, bf16[4,160,384]{2,1,0:T(8,128)(2,1)S(1)}, u32[]{:S(2)}, u32[]{:S(2)}) collective-permute-start(bf16[4,160,384]{2,1,0:T(8,128)(2,1)S(1)} %pad_maximum_fusion.9), channel_id=1, source_target_pairs={{0,24},{4,28},{8,16},{12,20},{16,8},{20,12},{24,0},{28,4},{1,25},{... | collective-permute-start | bytes 1474568 | tf_op jit(solution)/shard_map/ppermute | solution.py:1165
  400.2 16.9 %collective-permute-start.41 = (bf16[384,768]{1,0:T(8,128)(2,1)S(1)}, bf16[384,768]{1,0:T(8,128)(2,1)S(1)}, u32[]{:S(2)}, u32[]{:S(2)}) collective-permute-start(bf16[384,768]{1,0:T(8,128)(2,1)S(1)} %get-tuple-element.175), channel_id=1, source_target_pairs={{1,0},{0,1},{5,2},{4,3},{3,4},{2,5},{7,6},{6,7},{9,8},{8,9},{13,10... | collective-permute-start | bytes 1769480 | tf_op jit(solution)/shard_map/ppermute | solution.py:1254
  422.2 4.0 collective-permute-start.46
  (24 other events, 36.6 us)
Sparse Core Ops, SparseCore 0:
  229.5 80.3 all-gather.4
  328.5 57.2 all-gather.6
where the time goes:
time: 443 us; the launch traced here: 437 us
  Pallas kernels  197 us (44%)
  starting transfers between devices  101 us (23%)
  waiting for transfers between devices  67.4 us (15%)
  other arithmetic  28 us (6%)
  local copies, waits for them, and re-layouts  26 us (6%)
  between operations  18.3 us (4%)
    ppermute x36, starting transfers between devices, swap(): return lax.ppermute(array, axis, flip_pairs(8 if axis == 'dp' else 4, mask))  63.3 us
    pallas_call x2, Pallas kernels, attend_back(): pl.pallas_call(functools.partial(attend_back_kernel, pieces=len(kvs), val...  54.1 us
    ppermute x36, waiting for transfers between devices, swap(): return lax.ppermute(array, axis, flip_pairs(8 if axis == 'dp' else 4, mask))  54 us
    pallas_call x2, Pallas kernels, attend(): pl.pallas_call(functools.partial(attend_kernel, pieces=len(kvs), valid=va...  36.1 us
    pallas_call x1, Pallas kernels, feed(): pl.pallas_call(functools.partial(feed_kernel, steps=steps, tile=tile), gr...  34.8 us
    pallas_call x1, Pallas kernels, feed_back(): pl.pallas_call(functools.partial(feed_back_kernel, steps=steps), grid=(st...  24.3 us
    ppermute x4, starting transfers between devices, move(): lax.ppermute(piece, ('dp', 'blk'), column_pairs(table))  18.6 us
    unnamed x78, local copies, waits for them, and re-layouts  16.9 us
  transfers between devices with their start and end apart: 49, of which 17 were waited for; matrix products, arithmetic and copies ran while one was open for 7% of the time, Pallas kernels for 35%

commit v1 on v0

--- a/solution.py
+++ b/solution.py
@@ -375,6 +375,7 @@
 BF16 = jnp.bfloat16
 EXP_SCALE = math.log2(math.e) / 8
 LANES = 128
+CUT = 256
 VMEM = pl.BlockSpec(memory_space=pltpu.VMEM)
 SMEM = pl.BlockSpec(memory_space=pltpu.SMEM)
 ANY = pl.BlockSpec(memory_space=pl.ANY)
@@ -417,20 +418,22 @@
     return unit, recip * (grad - jnp.mean(grad, axis=1, keepdims=True) - unit * inner)
 
 
-def prepare_kernel(a, b, out_a, out_b, *, counts):
+def prepare_kernel(a, b, w, out_a, out_b, out_w):
     out_a[...] = a[...].astype(F32)
     out_b[...] = b[...].astype(F32)
-
-
-def prepare(a, b):
+    out_w[...] = w[...]
+
+
+def prepare(a, b, w):
     return pl.pallas_call(
-        functools.partial(prepare_kernel, counts=None),
-        in_specs=[VMEM] * 2,
-        out_specs=[VMEM] * 2,
-        out_shape=[shape_of(a.shape, F32), shape_of(b.shape, F32)],
-        cost_estimate=lasting(1),
+        prepare_kernel,
+        in_specs=[VMEM] * 3,
+        out_specs=[VMEM] * 3,
+        out_shape=[shape_of(a.shape, F32), shape_of(b.shape, F32), shape_of(w.shape, w.dtype)],
+        compiler_params=limits(16),
+        cost_estimate=lasting(2),
         name="prepare",
-    )(a, b)
+    )(a, b, w)
 
 
 def project_rows(x, vecs, w, q_ref, kv_ref, at, q_at=None):
@@ -465,7 +468,7 @@
             pltpu.VMEM(w.shape, w.dtype),
             pltpu.SemaphoreType.DMA((3,)),
         ],
-        compiler_params=limits(40),
+        compiler_params=limits(24),
         cost_estimate=lasting(4),
         name="project",
     )(x13, x2, vecs, w)
@@ -504,7 +507,7 @@
             pltpu.VMEM((4, rows, 768), BF16),
             pltpu.SemaphoreType.DMA((1,)),
         ],
-        compiler_params=limits(40),
+        compiler_params=limits(24),
         cost_estimate=lasting(4),
         name="project_short",
     )(where, x13, near, other, far, vecs, w)
@@ -560,6 +563,11 @@
             at += n
         keys.append(key_parts)
         values.append(value_parts)
+    cuts = [
+        (i, first, min(CUT, kv.shape[1] - first))
+        for i, kv in enumerate(kvs)
+        for first in range(0, kv.shape[1], CUT)
+    ]
     for s in range(q_ref.shape[0] // step):
         at = pl.ds(s * step, step)
         q = q_ref[at, :]
@@ -569,21 +577,25 @@
             q_own = q
             if total > valid:
                 q_own = jnp.where(own, q, jnp.where(half == 0, 1.0, 0.0).astype(BF16))
-            scores = [dot_nt(q_own, k) for k in keys[h]]
-            top = functools.reduce(
-                jnp.maximum, [jnp.max(x, axis=1, keepdims=True) for x in scores]
-            )
-            scaled_top = top * EXP_SCALE
-            weights = [jnp.exp2(x * EXP_SCALE - scaled_top).astype(BF16) for x in scores]
-            sums.append(
-                functools.reduce(jnp.add, [dot_nn(p, v) for p, v in zip(weights, values[h])])
-            )
+            top, kept = None, None
+            for i, first, size in cuts:
+                scores = dot_nt(q_own, keys[h][i][first : first + size]) * EXP_SCALE
+                new_top = jnp.max(scores, axis=1, keepdims=True)
+                if top is not None:
+                    new_top = jnp.maximum(top, new_top)
+                weights = jnp.exp2(scores - new_top).astype(BF16)
+                part = dot_nn(weights, values[h][i][first : first + size])
+                kept = part if top is None else kept * jnp.exp2(top - new_top) + part
+                top = new_top
+            sums.append(kept)
             tops.append(top)
         above = jnp.where(low, sums[0], sums[1])
         below = jnp.where(low, sums[1], sums[0])
         o_ref[at, :] = above / pltpu.roll(below, 64, 1)
-        log_total = -(jnp.where(low, tops[1], tops[0]) + 8.0 * jnp.log(below))
-        t_ref[at, :] = jnp.where(half == 3, jnp.ones((), BF16), three_parts(log_total, half))
+        top = jnp.where(low, tops[1], tops[0]) * (1.0 / EXP_SCALE)
+        t_ref[at, :] = jnp.where(
+            half == 3, jnp.ones((), BF16), three_parts(-(top + 8.0 * jnp.log(below)), half)
+        )
 
 
 def attend(q, kvs, valid, rows, step, first=0, count=6):
@@ -597,7 +609,7 @@
         in_specs=[pl.BlockSpec((rows, LANES), lambda p, i: (i, first + p))]
         + [pl.BlockSpec((2, kv.shape[1], LANES), lambda p, i: (0, 0, first + p)) for kv in kvs],
         out_specs=[block, block],
-        compiler_params=limits(56),
+        compiler_params=limits(24),
         cost_estimate=lasting(n * keys * count // 280000),
         name="attend",
     )(q, *kvs)
@@ -687,7 +699,7 @@
         grid=(count,),
         in_specs=[SMEM, block, back_block, block, block] + wide,
         out_specs=[out] + out_wide,
-        compiler_params=limits(56),
+        compiler_params=limits(28),
         cost_estimate=lasting(n * keys * count // 180000),
         name="attend_back",
     )(where, q, do, o, t, *kvs)
@@ -818,7 +830,7 @@
             pltpu.VMEM((n, tile), BF16),
             pltpu.SemaphoreType.DMA((8,)),
         ],
-        compiler_params=limits(60),
+        compiler_params=limits(48),
         cost_estimate=lasting(36),
         name="feed",
     )(where, att_full, att_short, *xs, *cots, w_out, vecs, w1, b1, w2)
@@ -916,7 +928,7 @@
             pltpu.VMEM(v.shape, v.dtype) for v in (att_full, att_short, *cots, mid)
         ]
         + [pltpu.SemaphoreType.DMA((5,))],
-        compiler_params=limits(60),
+        compiler_params=limits(44),
         cost_estimate=lasting(26),
         name="feed_back",
     )(where, att_full, att_short, *cots, w_out, vecs, mid, normed, hidden_low, w1)
@@ -977,7 +989,7 @@
         scratch_shapes=[pltpu.VMEM(*each) for each in held]
         + [pltpu.VMEM((3, n, 768), BF16), pltpu.VMEM((768, n), BF16)]
         + [pltpu.SemaphoreType.DMA((9,))],
-        compiler_params=limits(60),
+        compiler_params=limits(40),
         cost_estimate=lasting(11),
         name="project_back",
     )(where, *xs, vecs, *backs)
@@ -1064,7 +1076,7 @@
             pltpu.VMEM(w.shape, w.dtype),
             pltpu.SemaphoreType.DMA((1,)),
         ],
-        compiler_params=limits(40),
+        compiler_params=limits(32),
         cost_estimate=lasting(9),
         name="input_back",
     )(where, *xs, vecs, w, back_mid, back, sums, gb1)
@@ -1114,7 +1126,7 @@
         out_specs=specs,
         out_shape=result,
         scratch_shapes=scratch,
-        compiler_params=limits(40),
+        compiler_params=limits(20),
         cost_estimate=lasting(4),
         name="finish",
     )(where, mine, other, *[mine, other] * with_lines)
@@ -1167,6 +1179,37 @@
 
 def add_low(*terms):
     return sum(term.astype(F32) for term in terms).astype(BF16)
+
+
+def find_slots(counts, odd):
+    short = jnp.where(counts[1] < counts[0], 1, jnp.where(counts[2] < counts[0], 2, 0))
+    one = jnp.where(short == 0, 1, 0)
+    two = jnp.where(short == 2, 1, 2)
+    return jnp.where(odd == 0, one, two), jnp.where(odd == 0, two, one), short
+
+
+def leave_kernel(counts, odd, source, pair, single, sems):
+    slots = find_slots(counts, odd[0])
+    copies = start_copies(
+        [source.at[slots[0]], source.at[slots[2]], source.at[slots[1]]],
+        [pair.at[0], pair.at[1], single],
+        sems,
+    )
+    for copy in copies:
+        copy.wait()
+
+
+def leave(counts, odd, array):
+    rows = array.shape[1]
+    return pl.pallas_call(
+        leave_kernel,
+        in_specs=[SMEM, SMEM, ANY],
+        out_specs=[VMEM, VMEM],
+        out_shape=[shape_of((2, rows, 768), BF16), shape_of((rows, 768), BF16)],
+        scratch_shapes=[pltpu.SemaphoreType.DMA((3,))],
+        cost_estimate=lasting(2),
+        name="leave",
+    )(counts, odd.reshape(1).astype(jnp.int32), array)
 
 
 class Place:
@@ -1218,11 +1261,7 @@
 ):
     place = Place()
     odd = place.z % 2
-    short = jnp.argmin(counts).astype(jnp.int32)
-    full_one = jnp.where(short == 0, 1, 0)
-    full_two = jnp.where(short == 2, 1, 2)
-    slots = (jnp.where(odd == 0, full_one, full_two), jnp.where(odd == 0, full_two, full_one), short)
-    tables = (FIRST_TO, SECOND_TO, FIRST_TO)
+    slots = find_slots(counts, odd)
 
     def arrange(pieces):
         (one, three), two = pieces
@@ -1237,10 +1276,6 @@
         [place.core, place.chip * 4 + place.z, 2 * place.core + odd]
     ).astype(jnp.int32)
 
-    def leaving(array):
-        pieces = [lax.dynamic_index_in_dim(array, slot, 0, keepdims=False) for slot in slots]
-        return jnp.stack([pieces[0], pieces[2]]), pieces[1]
-
     def move(pieces):
         return tuple(
             lax.ppermute(piece, ("dp", "blk"), column_pairs(table))
@@ -1258,15 +1293,15 @@
     wide = w_fc1.shape[1] // 768
     rows = tokens.shape[1]
     vectors = [ln1_gain, ln1_shift, bias_q, bias_v, bias_out, ln2_gain, ln2_shift, bias_fc2]
-    vecs, b1 = prepare(jnp.stack(vectors), bias_fc1.reshape(1, -1))
+    vecs, b1, w_near = prepare(jnp.stack(vectors), bias_fc1.reshape(1, -1), w_qkv)
     vecs_one, vecs_two = vecs[:4], vecs[4:]
-    token_sends = leaving(tokens)
+    token_sends = leave(counts, odd, tokens)
     x13, x2 = move(token_sends)
     xs = (x13, x2)
-    cot_sends = leaving(after(cotangent, *token_sends))
+    cot_sends = leave(counts, odd, after(cotangent, *token_sends))
     x3 = after(x13[1], x2, vecs, *cot_sends)
     short_blocks = exchange_short(x3)
-    q_full, kv_full = project(x13, after(x2, x3), vecs_one, w_qkv)
+    q_full, kv_full = project(x13, after(x2, x3), vecs_one, w_near)
     kv_other = swap(kv_full, "dp", 1)
     cots = move(after(cot_sends, x3))
     seq = 2 * kv_full.shape[1]
@@ -1274,7 +1309,7 @@
     att_full, t_full = attend(q_full, kv_both, seq, 768, 384)
     spare = -(-(SHORT - 2 * rows) // LANES) * LANES
     q_short, kv_head, kv_tail = project_short(
-        where, x13, *after(short_blocks, att_full), vecs_one, w_qkv, spare
+        where, x13, *after(short_blocks, att_full), vecs_one, w_near, spare
     )
     kv_short = [kv_head, kv_tail]
     att_short, t_short = attend(q_short, kv_short, SHORT, 384, 384)
@@ -1298,7 +1333,7 @@
     n_full = q_full.shape[0]
     dq_short, keep_short, send_pair = attend_back(
         where, after(q_short, quarter_a), back_att, n_full, att_short, t_short, kv_short, SHORT,
-        448, 0, 6, True,
+        768, 0, 6, True,
     )
     home = (home[0], after(home[1], dq_short))
     part_a = add_low(after(quarter_a[0], dq_short, home[1]), *line_a)
@@ -1335,7 +1370,7 @@
         for k, total in enumerate(by_chip(after(keep_c, i2, near_b), got_c))
     ]
     chips_c = over_chips(sums_c)
-    (i13_home,) = give((after(i13, *sums_c), None))[:1]
+    (i13_home,) = give((i13, None))[:1]
     output = arrange(after(home, *sums_c))
     all_a = after(all_a, *sums_c)
     halves_a = [all_a[:, c] for c in range(2)]

time: 443 us -> 430 us (0.971)
  other arithmetic: 28 us -> 20.7 us
    ppermute x4, starting transfers between devices: 18.6 us -> 10.2 us  [move(): lax.ppermute(piece, ('dp', 'blk'), column_pairs(table))]
    ppermute x4, starting transfers between devices: 6.49 us -> 13.1 us  [give(): lax.ppermute(piece, ('dp', 'blk'), [pair[::-1] for pair in column_pairs(t...]
    pallas_call x2, Pallas kernels: 36.1 us -> 29.6 us  [attend(): pl.pallas_call(functools.partial(attend_kernel, pieces=len(kvs), valid=va...]
    ppermute x36, starting transfers between devices: 63.3 us -> 69.7 us  [swap(): return lax.ppermute(array, axis, flip_pairs(8 if axis == 'dp' else 4, mask))]
    pallas_call x1 -> x3, Pallas kernels: 1.34 us -> 7.01 us  [the longest x2 6.78 us: leave(): pl.pallas_call(leave_kernel, in_specs=[SMEM, SMEM, ANY], out_specs=[VMEM,...]
    unnamed x78 -> x120, local copies, waits for them, and re-layouts: 16.9 us -> 20.1 us
  transfers between devices with their start and end apart: 49 -> 49, of which waited for: 17 -> 17; matrix products, arithmetic and copies ran while one was open for 7% -> 6% of each run, Pallas kernels for 35% -> 35%
where the time goes in v1:
time: 430 us; the launch traced here: 425 us
  Pallas kernels  193 us (45%)
  starting transfers between devices  105 us (24%)
  waiting for transfers between devices  63.5 us (15%)
  local copies, waits for them, and re-layouts  24.9 us (6%)
  other arithmetic  20.7 us (5%)
  between operations  18 us (4%)
    ppermute x36, starting transfers between devices, swap(): return lax.ppermute(array, axis, flip_pairs(8 if axis == 'dp' else 4, mask))  69.7 us
    pallas_call x2, Pallas kernels, attend_back(): pl.pallas_call(functools.partial(attend_back_kernel, pieces=len(kvs), val...  54 us
    ppermute x36, waiting for transfers between devices, swap(): return lax.ppermute(array, axis, flip_pairs(8 if axis == 'dp' else 4, mask))  51.4 us
    pallas_call x1, Pallas kernels, feed(): pl.pallas_call(functools.partial(feed_kernel, steps=steps, tile=tile), gr...  33.4 us
    pallas_call x2, Pallas kernels, attend(): pl.pallas_call(functools.partial(attend_kernel, pieces=len(kvs), valid=va...  29.6 us
    pallas_call x1, Pallas kernels, feed_back(): pl.pallas_call(functools.partial(feed_back_kernel, steps=steps), grid=(st...  23.8 us
    unnamed x120, local copies, waits for them, and re-layouts  20.1 us
    pallas_call x4, Pallas kernels, finish(): pl.pallas_call(functools.partial(finish_kernel, with_lines=with_lines), g...  15.7 us
  transfers between devices with their start and end apart: 49, of which 17 were waited for; matrix products, arithmetic and copies ran while one was open for 6% of the time, Pallas kernels for 35%

profile of v1, /device:TPU:0, one launch (start us, length us, event | category | flops | bytes accessed | tf_op | source)
XLA Modules:
  0.0 425.1 jit_solution(2927631522956437737)
XLA Ops:
  7.3 3.5 leave.2
  10.8 1.9 collective-permute-start
  12.7 3.0 collective-permute-start.1
  16.0 3.3 leave.3
  19.3 2.0 copy-done.5
  22.5 7.5 %collective-permute-done.1.x2_in.x2 = bf16[384,768]{1,0:T(8,128)(2,1)S(1)} collective-permute-done((bf16[384,768]{1,0:T(8,128)(2,1)}, bf16[384,768]{1,0:T(8,128)(2,1)S(1)}, u32[]{:S(2)}, u32[]{:S(2)}) %collective-permute-start.1) | collective-permute-done | bytes 589856 | tf_op jit(solution)/shard_map/ppermute | solution.py:1281
  30.0 5.0 %project.1 = (bf16[768,768]{1,0:T(8,128)(2,1)S(1)}, bf16[2,768,768]{2,1,0:T(8,128)(2,1)}) custom-call(bf16[2,384,768]{2,1,0:T(8,128)(2,1)S(1)} %collective-permute-done.x13_in.x13, bf16[384,768]{1,0:T(8,128)(2,1)S(1)} %collective-permute-done.1.x2_in.x2, f32[4,768]{1,0:T(4,128)S(1)} %get-tuple-element.235.vecs, bf16[768,2304]{1,0:T(8,128)(2,1)S(1)} %get-tuple-element.114.w_in), custom_call_target="tpu_custom_call" | custom-call | flops 4000000000 | bytes 1048576 | tf_op jit(solution)/shard_map/project/pallas_call | solution.py:461
  35.0 20.9 %collective-permute-start.2 = (bf16[2,768,768]{2,1,0:T(8,128)(2,1)}, bf16[2,768,768]{2,1,0:T(8,128)(2,1)}, u32[]{:S(2)}, u32[]{:S(2)}) collective-permute-start(bf16[2,768,768]{2,1,0:T(8,128)(2,1)} %get-tuple-element.116.refs_1_.refs_5_), channel_id=1, source_target_pairs={{0,4},{4,0},{8,12},{12,8},{16,20},{20,16},{24,28},{28,24},{1,5},{5... | collective-permute-start | bytes 7077896 | tf_op jit(solution)/shard_map/ppermute | solution.py:1177
  56.0 8.1 %collective-permute-start.3 = (bf16[384,768]{1,0:T(8,128)(2,1)}, bf16[384,768]{1,0:T(8,128)(2,1)S(1)}, u32[]{:S(2)}, u32[]{:S(2)}) collective-permute-start(bf16[384,768]{1,0:T(8,128)(2,1)} %slice_bitcast_fusion.2), channel_id=1, source_target_pairs={{0,1},{1,0},{2,3},{3,2},{4,5},{6,7},{8,9},{9,8},{10,11},{11,10},{1... | collective-permute-start | bytes 1769480 | tf_op jit(solution)/shard_map/ppermute | solution.py:1166
  64.1 1.9 collective-permute-start.4
  67.4 2.4 collective-permute-start.6
  69.8 2.8 collective-permute-start.7
  72.6 21.1 %attend.2 = (f32[768,768]{1,0:T(8,128)S(1)}, bf16[768,768]{1,0:T(8,128)(2,1)S(1)}) custom-call(bf16[768,768]{1,0:T(8,128)(2,1)S(1)} %get-tuple-element.155.refs_0_.refs_1_, bf16[2,768,768]{2,1,0:T(8,128)(2,1)} %get-tuple-element.116.refs_1_.refs_5_, bf16[2,768,768]{2,1,0:T(8,128)(2,1)} %collective-permute-done.2.refs_2_.refs_6_), custom_call_target="tpu_custom_call" | custom-call | flops 24999999488 | bytes 1048576 | tf_op jit(solution)/shard_map/attend/pallas_call | solution.py:605
  95.1 4.3 %project_short.1 = (bf16[384,768]{1,0:T(8,128)(2,1)S(1)}, bf16[2,768,768]{2,1,0:T(8,128)(2,1)S(1)}, bf16[2,128,768]{2,1,0:T(8,128)(2,1)S(1)}) custom-call(s32[3]{0:T(128)S(1)} %get-tuple-element.198.where.refs_0_, bf16[2,384,768]{2,1,0:T(8,128)(2,1)S(1)} %collective-permute-done.x13_in.x13, bf16[384,768]{1,0:T(8,128)(2,1)S(1)} %collective-permute-done.3.near, ...), custom_call_target="tpu_custom_call" | custom-call | flops 4000000000 | bytes 1048576 | tf_op jit(solution)/shard_map/project_short/pallas_call | solution.py:496
  99.4 8.5 %attend.3 = (f32[384,768]{1,0:T(8,128)S(1)}, bf16[384,768]{1,0:T(8,128)(2,1)S(1)}) custom-call(bf16[384,768]{1,0:T(8,128)(2,1)S(1)} %get-tuple-element.141.refs_0_.refs_1_, bf16[2,768,768]{2,1,0:T(8,128)(2,1)S(1)} %get-tuple-element.122.refs_1_.refs_5_, bf16[2,128,768]{2,1,0:T(8,128)(2,1)S(1)} %get-tuple-element.123.refs_2_.refs_6_), custom_call_target="tpu_custom_call" | custom-call | flops 7000000000 | bytes 1048576 | tf_op jit(solution)/shard_map/attend/pallas_call | solution.py:605
  109.0 33.4 %feed.1 = (bf16[2,384,768]{2,1,0:T(8,128)(2,1)S(1)}, bf16[384,768]{1,0:T(8,128)(2,1)S(1)}, f32[1152,768]{1,0:T(8,128)}, bf16[1152,768]{1,0:T(8,128)(2,1)}, bf16[...) custom-call(s32[3]{0:T(128)S(1)} %get-tuple-element.198.where.refs_0, ...), custom_call_target="tpu_custom_call" | custom-call | flops 35999997952 | bytes 1048576 | tf_op jit(solution)/shard_map/feed/pallas_call | solution.py:804
  142.3 7.4 %collective-permute-start.9 = (bf16[16,192,384]{2,1,0:T(8,128)(2,1)}, bf16[16,192,384]{2,1,0:T(8,128)(2,1)S(1)}, u32[]{:S(2)}, u32[]{:S(2)}) collective-permute-start(bf16[16,192,384]{2,1,0:T(8,128)(2,1)} %get-tuple-element.133), channel_id=1, source_target_pairs={{0,4},{4,0},{8,12},{12,8},{16,20},{20,16},{24,28},{28,24},{1,5},{5... | collective-permute-start | bytes 7077896 | tf_op jit(solution)/shard_map/ppermute | solution.py:1177
  150.5 3.6 collective-permute-done.9
  154.1 2.3 add_convert_fusion.7
  156.4 1.6 collective-permute-start.11
  158.0 1.5 collective-permute-start.12
  160.0 23.8 %feed_back.1 = (bf16[1152,768]{1,0:T(8,128)(2,1)S(1)}, f32[1152,768]{1,0:T(8,128)}, bf16[16,240,384]{2,1,0:T(8,128)(2,1)}, bf16[16,240,384]{2,1,0:T(8,128)(2,1)}, f32[8,768]{1,0:T(8,128)S(1)}) custom-call(s32[3]{0:T(128)S(1)} %get-tuple-element.198.where.refs_0_, f32[768,768]{1,0:T(8,128)S(1)} %copy-done.37, ...), custom_call_target="tpu_custom_call" | custom-call | flops 25999998976 | bytes 1048576 | tf_op jit(solution)/shard_map/feed_back/pallas_call | solution.py:903
  187.1 5.6 %collective-permute-start.15 = (bf16[192,384]{1,0:T(8,128)(2,1)S(1)}, bf16[192,384]{1,0:T(8,128)(2,1)S(1)}, u32[]{:S(2)}, u32[]{:S(2)}) collective-permute-start(bf16[192,384]{1,0:T(8,128)(2,1)S(1)} %get-tuple-element.225), channel_id=1, source_target_pairs={{0,2},{1,3},{2,0},{3,1},{4,6},{5,7},{6,4},{7,5},{8,10},{9,11},{10,... | collective-permute-start | bytes 442376 | tf_op jit(solution)/shard_map/ppermute | solution.py:1177
  194.0 1.5 copy-done.32
  195.5 16.1 %attend_back.2 = (bf16[384,768]{1,0:T(8,128)(2,1)S(1)}, bf16[2,768,768]{2,1,0:T(8,128)(2,1)S(1)}, bf16[2,768,768]{2,1,0:T(8,128)(2,1)S(1)}) custom-call(s32[3]{0:T(128)S(1)} %get-tuple-element.198.where.refs_0_, bf16[384,768]{1,0:T(8,128)(2,1)S(1)} %copy-done.24, bf16[1152,768]{1,0:T(8,128)(2,1)S(1)} %copy-done.32, f32[384,768]{1,0:T(8,128)S(1)} %copy-done.30, ...), custom_call_target="tpu_custom_call" | custom-call | flops 11000000512 | bytes 1048576 | tf_op jit(solution)/shard_map/attend_back/pallas_call | solution.py:693
  211.7 1.4 copy-done.7
  215.8 3.5 add_convert_fusion.2
  219.8 1.7 add_convert_fusion
  222.2 1.5 collective-permute-start.20
  223.6 1.5 collective-permute-start.21
  225.7 37.9 %attend_back.3 = (bf16[768,768]{1,0:T(8,128)(2,1)S(1)}, bf16[2,768,768]{2,1,0:T(8,128)(2,1)S(1)}, bf16[2,768,768]{2,1,0:T(8,128)(2,1)S(1)}) custom-call(s32[3]{0:T(128)S(1)} %copy-done.3, bf16[768,768]{1,0:T(8,128)(2,1)S(1)} %copy-done.21, bf16[1152,768]{1,0:T(8,128)(2,1)S(1)} %copy-done.33, f32[768,768]{1,0:T(8,128)S(1)} %copy-done.38, ...), custom_call_target="tpu_custom_call" | custom-call | flops 38999998464 | bytes 1048576 | tf_op jit(solution)/shard_map/attend_back/pallas_call | solution.py:693
  265.1 1.5 collective-permute-start.24
  266.6 2.4 collective-permute-start.25
  270.5 1.7 copy-done.28
  272.1 10.8 %project_back.1 = (bf16[16,144,384]{2,1,0:T(8,128)(2,1)}, bf16[16,144,384]{2,1,0:T(8,128)(2,1)S(1)}, bf16[3,1152,768]{2,1,0:T(8,128)(2,1)}) custom-call(s32[3]{0:T(128)S(1)} %copy-done.3, bf16[2,384,768]{2,1,0:T(8,128)(2,1)S(1)} %collective-permute-done.x13_in.x13, bf16[384,768]{1,0:T(8,128)(2,1)S(1)} %copy-done.12, f32[4,768]{1,0:T(4,128)S(1)} %get-tuple-element.235.vecs, ...), custom_call_target="tpu_custom_call" | custom-call | flops 11000000512 | bytes 1048576 | tf_op jit(solution)/shard_map/project_back/pallas_call | solution.py:984
  282.9 1.7 collective-permute-done.24
  284.7 9.2 %collective-permute-done.26 = bf16[240,384]{1,0:T(8,128)(2,1)S(1)} collective-permute-done((bf16[240,384]{1,0:T(8,128)(2,1)S(1)}, bf16[240,384]{1,0:T(8,128)(2,1)S(1)}, u32[]{:S(2)}, u32[]{:S(2)}) %collective-permute-start.26) | collective-permute-done | bytes 184352 | tf_op jit(solution)/shard_map/ppermute | solution.py:1177
  294.0 3.7 collective-permute-start.27
  297.9 2.2 collective-permute-start.29
  300.2 2.5 copy-done.19
  302.7 9.8 %input_back.1 = (bf16[2,384,768]{2,1,0:T(8,128)(2,1)}, bf16[384,768]{1,0:T(8,128)(2,1)S(1)}, bf16[16,16,384]{2,1,0:T(8,128)(2,1)S(1)}) custom-call(s32[3]{0:T(128)S(1)} %copy-done.3, bf16[2,384,768]{2,1,0:T(8,128)(2,1)S(1)} %collective-permute-done.x13_in.x13, bf16[384,768]{1,0:T(8,128)(2,1)S(1)} %copy-done.12, f32[4,768]{1,0:T(4,128)S(1)} %get-tuple-element.235.vecs, ...), custom_call_target="tpu_custom_call" | custom-call | flops 8999999488 | bytes 1048576 | tf_op jit(solution)/shard_map/input_back/pallas_call | solution.py:1054
  318.3 10.4 %collective-permute-start.31 = (bf16[2,384,768]{2,1,0:T(8,128)(2,1)}, bf16[2,384,768]{2,1,0:T(8,128)(2,1)}, u32[]{:S(2)}, u32[]{:S(2)}) collective-permute-start(bf16[2,384,768]{2,1,0:T(8,128)(2,1)} %get-tuple-element.177), channel_id=1, source_target_pairs={{0,0},{1,1},{4,2},{5,3},{2,4},{3,5},{6,6},{7,7},{8,8},{9,9},{12,10... | collective-permute-start | bytes 3538952 | tf_op jit(solution)/shard_map/ppermute | solution.py:1289
  328.7 1.8 add_convert_fusion.12
  330.6 2.4 collective-permute-start.34
  337.1 1.4 pad_maximum_fusion.1
  338.5 3.0 slice_bitcast_fusion
  341.5 4.9 %finish.4 = f32[3072,768]{1,0:T(8,128)} custom-call(s32[3]{0:T(128)S(1)} %broadcast_1_where.2.where, bf16[4,4,192,384]{3,2,1,0:T(8,128)(2,1)S(1)} %get-tuple-element.204.mine, bf16[4,4,192,384]{3,2,1,0:T(8,128)(2,1)S(1)} %get-tuple-element.203.other), custom_call_target="tpu_custom_call" | custom-call | flops 4000000000 | bytes 1048576 | tf_op jit(solution)/shard_map/finish/pallas_call | solution.py:1122
  347.7 8.0 %collective-permute-done.33 = bf16[4,160,384]{2,1,0:T(8,128)(2,1)S(1)} collective-permute-done((bf16[4,160,384]{2,1,0:T(8,128)(2,1)}, bf16[4,160,384]{2,1,0:T(8,128)(2,1)S(1)}, u32[]{:S(2)}, u32[]{:S(2)}) %collective-permute-start.33) | collective-permute-done | bytes 491552 | tf_op jit(solution)/shard_map/ppermute | solution.py:1177
  357.4 1.7 collective-permute-start.36
  360.5 2.3 collective-permute-done.35
  362.7 7.0 %collective-permute-done.36 = bf16[160,384]{1,0:T(8,128)(2,1)S(1)} collective-permute-done((bf16[160,384]{1,0:T(8,128)(2,1)S(1)}, bf16[160,384]{1,0:T(8,128)(2,1)S(1)}, u32[]{:S(2)}, u32[]{:S(2)}) %collective-permute-start.36) | collective-permute-done | bytes 122912 | tf_op jit(solution)/shard_map/ppermute | solution.py:1177
  369.8 2.0 collective-permute-start.38
  374.3 1.8 collective-permute-done.38
  376.1 8.0 %collective-permute-done.39 = bf16[160,384]{1,0:T(8,128)(2,1)S(1)} collective-permute-done((bf16[160,384]{1,0:T(8,128)(2,1)S(1)}, bf16[160,384]{1,0:T(8,128)(2,1)S(1)}, u32[]{:S(2)}, u32[]{:S(2)}) %collective-permute-start.39) | collective-permute-done | bytes 122912 | tf_op jit(solution)/shard_map/ppermute | solution.py:1177
  384.3 1.5 collective-permute-start.43
  386.3 1.6 collective-permute-start.45
  387.9 1.9 collective-permute-start.41
  389.9 1.8 copy-done
  391.7 2.1 finish.6
  393.8 4.7 %finish.5 = f32[768,3072]{1,0:T(8,128)} custom-call(s32[3]{0:T(128)S(1)} %get-tuple-element.197.where, bf16[4,4,240,384]{3,2,1,0:T(8,128)(2,1)S(1)} %bitcast.107, bf16[4,4,240,384]{3,2,1,0:T(8,128)(2,1)S(1)} %collective-permute-done.42.other), custom_call_target="tpu_custom_call" | custom-call | flops 4000000000 | bytes 1048576 | tf_op jit(solution)/shard_map/finish/pallas_call | solution.py:1122
  398.5 4.6 %collective-permute-done.41 = bf16[384,768]{1,0:T(8,128)(2,1)S(1)} collective-permute-done((bf16[384,768]{1,0:T(8,128)(2,1)S(1)}, bf16[384,768]{1,0:T(8,128)(2,1)S(1)}, u32[]{:S(2)}, u32[]{:S(2)}) %collective-permute-start.41) | collective-permute-done | bytes 589856 | tf_op jit(solution)/shard_map/ppermute | solution.py:1289
  403.1 6.6 %collective-permute-done.44 = bf16[4,160,384]{2,1,0:T(8,128)(2,1)S(1)} collective-permute-done((bf16[4,160,384]{2,1,0:T(8,128)(2,1)S(1)}, bf16[4,160,384]{2,1,0:T(8,128)(2,1)S(1)}, u32[]{:S(2)}, u32[]{:S(2)}) %collective-permute-start.44) | collective-permute-done | bytes 491552 | tf_op jit(solution)/shard_map/ppermute | solution.py:1177
  411.4 2.1 maximum_convert_fusion
  414.0 4.0 finish.7
  (214 shorter events, 35.6 us)
Async XLA Ops:
  7.2 331.4 %all-gather.5.cloned.1.call-start = ((), (), s32[]{:S(2)}) async-start(), calls=%async_computation | async-start | bytes 4866048 | tf_op jit(solution)/shard_map/all_gather | solution.py:1240
  10.8 10.8 %collective-permute-start = (bf16[2,384,768]{2,1,0:T(8,128)(2,1)}, bf16[2,384,768]{2,1,0:T(8,128)(2,1)S(1)}, u32[]{:S(2)}, u32[]{:S(2)}) collective-permute-start(bf16[2,384,768]{2,1,0:T(8,128)(2,1)} %get-tuple-element.106), channel_id=1, source_target_pairs={{0,0},{1,1},{2,4},{3,5},{4,2},{5,3},{6,6},{7,7},{8,8},{9,9},{10,12... | collective-permute-start | bytes 3538952 | tf_op jit(solution)/shard_map/ppermute | solution.py:1281
  12.7 17.3 %collective-permute-start.1 = (bf16[384,768]{1,0:T(8,128)(2,1)}, bf16[384,768]{1,0:T(8,128)(2,1)S(1)}, u32[]{:S(2)}, u32[]{:S(2)}) collective-permute-start(bf16[384,768]{1,0:T(8,128)(2,1)} %get-tuple-element.107), channel_id=1, source_target_pairs={{0,1},{1,0},{2,5},{3,4},{4,3},{5,2},{6,7},{7,6},{8,9},{9,8},{10,13... | collective-permute-start | bytes 1769480 | tf_op jit(solution)/shard_map/ppermute | solution.py:1281
  21.6 13.4 %copy-start.15 = (bf16[768,2304]{1,0:T(8,128)(2,1)}, bf16[768,2304]{1,0:T(8,128)(2,1)S(1)}, u32[]{:S(2)}) copy-start(bf16[768,2304]{1,0:T(8,128)(2,1)S(1)} %get-tuple-element.114.w_in) | copy-start | bytes 10616836
  30.0 77.9 %copy-start.11 = (bf16[384,768]{1,0:T(8,128)(2,1)}, bf16[384,768]{1,0:T(8,128)(2,1)S(1)}, u32[]{:S(2)}) copy-start(bf16[384,768]{1,0:T(8,128)(2,1)S(1)} %collective-permute-done.1.x2_in.x2) | copy-start | bytes 1769476
  30.0 25.9 %copy-start.58 = (s32[3]{0:T(128)S(1)}, s32[3]{0:T(128)}, u32[]{:S(2)}) copy-start(s32[3]{0:T(128)} %constant.58.clone) | copy-start | bytes 40
  30.0 25.9 %copy-start.59 = (s32[3]{0:T(128)S(1)}, s32[3]{0:T(128)}, u32[]{:S(2)}) copy-start(s32[3]{0:T(128)} %constant.59.clone) | copy-start | bytes 40
  35.0 58.7 %copy-start.20 = (bf16[768,768]{1,0:T(8,128)(2,1)}, bf16[768,768]{1,0:T(8,128)(2,1)S(1)}, u32[]{:S(2)}) copy-start(bf16[768,768]{1,0:T(8,128)(2,1)S(1)} %get-tuple-element.155.refs_0_.refs_1_) | copy-start | bytes 3538948
  35.0 34.8 %collective-permute-start.2 = (bf16[2,768,768]{2,1,0:T(8,128)(2,1)}, bf16[2,768,768]{2,1,0:T(8,128)(2,1)}, u32[]{:S(2)}, u32[]{:S(2)}) collective-permute-start(bf16[2,768,768]{2,1,0:T(8,128)(2,1)} %get-tuple-element.116.refs_1_.refs_5_), channel_id=1, source_target_pairs={{0,4},{4,0},{8,12},{12,8},{16,20},{20,16},{24,28},{28,24},{1,5},{5... | collective-permute-start | bytes 7077896 | tf_op jit(solution)/shard_map/ppermute | solution.py:1177
  56.0 136.7 %copy-start.2 = (s32[3]{0:T(128)}, s32[3]{0:T(128)S(1)}, u32[]{:S(2)}) copy-start(s32[3]{0:T(128)S(1)} %get-tuple-element.198.where.refs_0_) | copy-start | bytes 40
  56.0 39.1 %collective-permute-start.3 = (bf16[384,768]{1,0:T(8,128)(2,1)}, bf16[384,768]{1,0:T(8,128)(2,1)S(1)}, u32[]{:S(2)}, u32[]{:S(2)}) collective-permute-start(bf16[384,768]{1,0:T(8,128)(2,1)} %slice_bitcast_fusion.2), channel_id=1, source_target_pairs={{0,1},{1,0},{2,3},{3,2},{4,5},{6,7},{8,9},{9,8},{10,11},{11,10},{1... | collective-permute-start | bytes 1769480 | tf_op jit(solution)/shard_map/ppermute | solution.py:1166
  64.1 31.0 %collective-permute-start.4 = (bf16[384,768]{1,0:T(8,128)(2,1)}, bf16[384,768]{1,0:T(8,128)(2,1)S(1)}, u32[]{:S(2)}, u32[]{:S(2)}) collective-permute-start(bf16[384,768]{1,0:T(8,128)(2,1)} %slice_bitcast_fusion.2), channel_id=1, source_target_pairs={{0,4},{1,5},{2,6},{3,7},{4,0},{6,2},{8,12},{9,13},{10,14},{11,15},... | collective-permute-start | bytes 1769480 | tf_op jit(solution)/shard_map/ppermute | solution.py:1166
  66.0 29.0 %collective-permute-start.5 = (bf16[384,768]{1,0:T(8,128)(2,1)}, bf16[384,768]{1,0:T(8,128)(2,1)S(1)}, u32[]{:S(2)}, u32[]{:S(2)}) collective-permute-start(bf16[384,768]{1,0:T(8,128)(2,1)} %slice_bitcast_fusion.2), channel_id=1, source_target_pairs={{0,5},{1,4},{2,7},{3,6},{4,1},{6,3},{8,13},{9,12},{10,15},{11,14},... | collective-permute-start | bytes 1769480 | tf_op jit(solution)/shard_map/ppermute | solution.py:1166
  67.4 40.6 %collective-permute-start.6 = (bf16[2,384,768]{2,1,0:T(8,128)(2,1)}, bf16[2,384,768]{2,1,0:T(8,128)(2,1)S(1)}, u32[]{:S(2)}, u32[]{:S(2)}) collective-permute-start(bf16[2,384,768]{2,1,0:T(8,128)(2,1)} %get-tuple-element.125), channel_id=1, source_target_pairs={{0,0},{1,1},{2,4},{3,5},{4,2},{5,3},{6,6},{7,7},{8,8},{9,9},{10,12... | collective-permute-start | bytes 3538952 | tf_op jit(solution)/shard_map/ppermute | solution.py:1281
  69.8 38.1 %collective-permute-start.7 = (bf16[384,768]{1,0:T(8,128)(2,1)}, bf16[384,768]{1,0:T(8,128)(2,1)S(1)}, u32[]{:S(2)}, u32[]{:S(2)}) collective-permute-start(bf16[384,768]{1,0:T(8,128)(2,1)} %get-tuple-element.126), channel_id=1, source_target_pairs={{0,1},{1,0},{2,5},{3,4},{4,3},{5,2},{6,7},{7,6},{8,9},{9,8},{10,13... | collective-permute-start | bytes 1769480 | tf_op jit(solution)/shard_map/ppermute | solution.py:1281
  72.6 22.5 %copy-start.16 = (bf16[768,2304]{1,0:T(8,128)(2,1)S(1)}, bf16[768,2304]{1,0:T(8,128)(2,1)}, u32[]{:S(2)}) copy-start(bf16[768,2304]{1,0:T(8,128)(2,1)} %copy-done.15) | copy-start | bytes 10616836
  142.3 14.1 %copy-start.44 = (f32[1,3072]{1,0:T(1,128)}, f32[1,3072]{1,0:T(1,128)S(1)}, u32[]{:S(2)}) copy-start(f32[1,3072]{1,0:T(1,128)S(1)} %get-tuple-element.168.gb1) | copy-start | bytes 36868
  142.3 11.8 %collective-permute-start.9 = (bf16[16,192,384]{2,1,0:T(8,128)(2,1)}, bf16[16,192,384]{2,1,0:T(8,128)(2,1)S(1)}, u32[]{:S(2)}, u32[]{:S(2)}) collective-permute-start(bf16[16,192,384]{2,1,0:T(8,128)(2,1)} %get-tuple-element.133), channel_id=1, source_target_pairs={{0,4},{4,0},{8,12},{12,8},{16,20},{20,16},{24,28},{28,24},{1,5},{5... | collective-permute-start | bytes 7077896 | tf_op jit(solution)/shard_map/ppermute | solution.py:1177
  149.7 36.3 %collective-permute-start.8 = (bf16[2,384,768]{2,1,0:T(8,128)(2,1)S(1)}, bf16[2,384,768]{2,1,0:T(8,128)(2,1)S(1)}, u32[]{:S(2)}, u32[]{:S(2)}) collective-permute-start(bf16[2,384,768]{2,1,0:T(8,128)(2,1)S(1)} %get-tuple-element.130), channel_id=1, source_target_pairs={{0,0},{1,1},{4,2},{5,3},{2,4},{3,5},{6,6},{7,7},{8,8},{9,9},{12,10... | collective-permute-start | bytes 3538952 | tf_op jit(solution)/shard_map/ppermute | solution.py:1289
  150.5 63.5 %collective-permute-start.10 = (bf16[384,768]{1,0:T(8,128)(2,1)S(1)}, bf16[384,768]{1,0:T(8,128)(2,1)}, u32[]{:S(2)}, u32[]{:S(2)}) collective-permute-start(bf16[384,768]{1,0:T(8,128)(2,1)S(1)} %get-tuple-element.139), channel_id=1, source_target_pairs={{1,0},{0,1},{5,2},{4,3},{3,4},{2,5},{7,6},{6,7},{9,8},{8,9},{13,10... | collective-permute-start | bytes 1769480 | tf_op jit(solution)/shard_map/ppermute | solution.py:1289
  156.4 29.6 %collective-permute-start.11 = (bf16[4,192,384]{2,1,0:T(8,128)(2,1)S(1)}, bf16[4,192,384]{2,1,0:T(8,128)(2,1)S(1)}, u32[]{:S(2)}, u32[]{:S(2)}) collective-permute-start(bf16[4,192,384]{2,1,0:T(8,128)(2,1)S(1)} %get-tuple-element.207), channel_id=1, source_target_pairs={{0,8},{4,12},{8,0},{12,4},{16,24},{20,28},{24,16},{28,20},{1,9},{5... | collective-permute-start | bytes 1769480 | tf_op jit(solution)/shard_map/ppermute | solution.py:1177
  158.0 28.1 %collective-permute-start.12 = (bf16[4,192,384]{2,1,0:T(8,128)(2,1)S(1)}, bf16[4,192,384]{2,1,0:T(8,128)(2,1)S(1)}, u32[]{:S(2)}, u32[]{:S(2)}) collective-permute-start(bf16[4,192,384]{2,1,0:T(8,128)(2,1)S(1)} %get-tuple-element.206), channel_id=1, source_target_pairs={{0,16},{4,20},{8,24},{12,28},{16,0},{20,4},{24,8},{28,12},{1,17},{... | collective-permute-start | bytes 1769480 | tf_op jit(solution)/shard_map/ppermute | solution.py:1177
  159.5 26.6 %collective-permute-start.13 = (bf16[4,192,384]{2,1,0:T(8,128)(2,1)S(1)}, bf16[4,192,384]{2,1,0:T(8,128)(2,1)S(1)}, u32[]{:S(2)}, u32[]{:S(2)}) collective-permute-start(bf16[4,192,384]{2,1,0:T(8,128)(2,1)S(1)} %get-tuple-element.205), channel_id=1, source_target_pairs={{0,24},{4,28},{8,16},{12,20},{16,8},{20,12},{24,0},{28,4},{1,25},{... | collective-permute-start | bytes 1769480 | tf_op jit(solution)/shard_map/ppermute | solution.py:1177
  187.1 26.9 %collective-permute-start.14 = (bf16[192,384]{1,0:T(8,128)(2,1)S(1)}, bf16[192,384]{1,0:T(8,128)(2,1)S(1)}, u32[]{:S(2)}, u32[]{:S(2)}) collective-permute-start(bf16[192,384]{1,0:T(8,128)(2,1)S(1)} %get-tuple-element.226), channel_id=1, source_target_pairs={{0,1},{1,0},{2,3},{3,2},{4,5},{5,4},{6,7},{7,6},{8,9},{9,8},{10,11... | collective-permute-start | bytes 442376 | tf_op jit(solution)/shard_map/ppermute | solution.py:1177
  187.1 26.9 %collective-permute-start.15 = (bf16[192,384]{1,0:T(8,128)(2,1)S(1)}, bf16[192,384]{1,0:T(8,128)(2,1)S(1)}, u32[]{:S(2)}, u32[]{:S(2)}) collective-permute-start(bf16[192,384]{1,0:T(8,128)(2,1)S(1)} %get-tuple-element.225), channel_id=1, source_target_pairs={{0,2},{1,3},{2,0},{3,1},{4,6},{5,7},{6,4},{7,5},{8,10},{9,11},{10,... | collective-permute-start | bytes 442376 | tf_op jit(solution)/shard_map/ppermute | solution.py:1177
  192.7 21.2 %collective-permute-start.16 = (bf16[192,384]{1,0:T(8,128)(2,1)S(1)}, bf16[192,384]{1,0:T(8,128)(2,1)S(1)}, u32[]{:S(2)}, u32[]{:S(2)}) collective-permute-start(bf16[192,384]{1,0:T(8,128)(2,1)S(1)} %get-tuple-element.224), channel_id=1, source_target_pairs={{0,3},{1,2},{2,1},{3,0},{4,7},{5,6},{6,5},{7,4},{8,11},{9,10},{10,... | collective-permute-start | bytes 442376 | tf_op jit(solution)/shard_map/ppermute | solution.py:1177
  192.7 23.1 %collective-permute-start.18 = (bf16[16,240,384]{2,1,0:T(8,128)(2,1)}, bf16[16,240,384]{2,1,0:T(8,128)(2,1)}, u32[]{:S(2)}, u32[]{:S(2)}) collective-permute-start(bf16[16,240,384]{2,1,0:T(8,128)(2,1)} %get-tuple-element.153), channel_id=1, source_target_pairs={{0,4},{4,0},{8,12},{12,8},{16,20},{20,16},{24,28},{28,24},{1,5},{5... | collective-permute-start | bytes 8847368 | tf_op jit(solution)/shard_map/ppermute | solution.py:1177
  214.8 5.0 %collective-permute-start.17 = (bf16[2,768,768]{2,1,0:T(8,128)(2,1)}, bf16[2,768,768]{2,1,0:T(8,128)(2,1)}, u32[]{:S(2)}, u32[]{:S(2)}) collective-permute-start(bf16[2,768,768]{2,1,0:T(8,128)(2,1)} %copy-done.7), channel_id=1, source_target_pairs={{0,4},{4,0},{8,12},{12,8},{16,20},{20,16},{24,28},{28,24},{1,5},{5... | collective-permute-start | bytes 7077896 | tf_op jit(solution)/shard_map/ppermute | solution.py:1177
  215.3 168.9 %all-gather.7.cloned.1.call-start = ((), (), s32[]{:S(2)}) async-start(), calls=%async_computation.1 | async-start | bytes 3686400 | tf_op jit(solution)/shard_map/all_gather | solution.py:1367
  215.8 9.9 %copy-start.38 = (f32[768,768]{1,0:T(8,128)S(1)}, f32[768,768]{1,0:T(8,128)}, u32[]{:S(2)}) copy-start(f32[768,768]{1,0:T(8,128)} %copy-done.36) | copy-start | bytes 7077892
  215.8 9.9 %copy-start.41 = (bf16[768,768]{1,0:T(8,128)(2,1)S(1)}, bf16[768,768]{1,0:T(8,128)(2,1)}, u32[]{:S(2)}) copy-start(bf16[768,768]{1,0:T(8,128)(2,1)} %copy-done.40) | copy-start | bytes 3538948
  221.5 42.1 %collective-permute-start.19 = (bf16[2,384,768]{2,1,0:T(8,128)(2,1)S(1)}, bf16[2,384,768]{2,1,0:T(8,128)(2,1)S(1)}, u32[]{:S(2)}, u32[]{:S(2)}) collective-permute-start(bf16[2,384,768]{2,1,0:T(8,128)(2,1)S(1)} %add_convert_fusion), channel_id=1, source_target_pairs={{0,1},{1,0},{2,3},{3,2},{4,5},{5,4},{6,7},{7,6},{8,9},{9,8},{10,11... | collective-permute-start | bytes 3538952 | tf_op jit(solution)/shard_map/ppermute | solution.py:1177
  222.2 41.5 %collective-permute-start.20 = (bf16[4,240,384]{2,1,0:T(8,128)(2,1)S(1)}, bf16[4,240,384]{2,1,0:T(8,128)(2,1)S(1)}, u32[]{:S(2)}, u32[]{:S(2)}) collective-permute-start(bf16[4,240,384]{2,1,0:T(8,128)(2,1)S(1)} %get-tuple-element.201), channel_id=1, source_target_pairs={{0,8},{4,12},{8,0},{12,4},{16,24},{20,28},{24,16},{28,20},{1,9},{5... | collective-permute-start | bytes 2211848 | tf_op jit(solution)/shard_map/ppermute | solution.py:1177
  223.6 40.0 %collective-permute-start.21 = (bf16[4,240,384]{2,1,0:T(8,128)(2,1)S(1)}, bf16[4,240,384]{2,1,0:T(8,128)(2,1)S(1)}, u32[]{:S(2)}, u32[]{:S(2)}) collective-permute-start(bf16[4,240,384]{2,1,0:T(8,128)(2,1)S(1)} %get-tuple-element.200), channel_id=1, source_target_pairs={{0,16},{4,20},{8,24},{12,28},{16,0},{20,4},{24,8},{28,12},{1,17},{... | collective-permute-start | bytes 2211848 | tf_op jit(solution)/shard_map/ppermute | solution.py:1177
  225.2 38.5 %collective-permute-start.22 = (bf16[4,240,384]{2,1,0:T(8,128)(2,1)S(1)}, bf16[4,240,384]{2,1,0:T(8,128)(2,1)S(1)}, u32[]{:S(2)}, u32[]{:S(2)}) collective-permute-start(bf16[4,240,384]{2,1,0:T(8,128)(2,1)S(1)} %get-tuple-element.199), channel_id=1, source_target_pairs={{0,24},{4,28},{8,16},{12,20},{16,8},{20,12},{24,0},{28,4},{1,25},{... | collective-permute-start | bytes 2211848 | tf_op jit(solution)/shard_map/ppermute | solution.py:1177
  265.0 5.5 %collective-permute-start.23 = (bf16[2,768,768]{2,1,0:T(8,128)(2,1)S(1)}, bf16[2,768,768]{2,1,0:T(8,128)(2,1)S(1)}, u32[]{:S(2)}, u32[]{:S(2)}) collective-permute-start(bf16[2,768,768]{2,1,0:T(8,128)(2,1)S(1)} %get-tuple-element.162), channel_id=1, source_target_pairs={{0,4},{4,0},{8,12},{12,8},{16,20},{20,16},{24,28},{28,24},{1,5},{5... | collective-permute-start | bytes 7077896 | tf_op jit(solution)/shard_map/ppermute | solution.py:1177
  265.1 19.6 %collective-permute-start.24 = (bf16[240,384]{1,0:T(8,128)(2,1)S(1)}, bf16[240,384]{1,0:T(8,128)(2,1)S(1)}, u32[]{:S(2)}, u32[]{:S(2)}) collective-permute-start(bf16[240,384]{1,0:T(8,128)(2,1)S(1)} %get-tuple-element.222), channel_id=1, source_target_pairs={{0,1},{1,0},{2,3},{3,2},{4,5},{5,4},{6,7},{7,6},{8,9},{9,8},{10,11... | collective-permute-start | bytes 552968 | tf_op jit(solution)/shard_map/ppermute | solution.py:1177
  266.6 18.1 %collective-permute-start.25 = (bf16[240,384]{1,0:T(8,128)(2,1)S(1)}, bf16[240,384]{1,0:T(8,128)(2,1)S(1)}, u32[]{:S(2)}, u32[]{:S(2)}) collective-permute-start(bf16[240,384]{1,0:T(8,128)(2,1)S(1)} %get-tuple-element.221), channel_id=1, source_target_pairs={{0,2},{1,3},{2,0},{3,1},{4,6},{5,7},{6,4},{7,5},{8,10},{9,11},{10,... | collective-permute-start | bytes 552968 | tf_op jit(solution)/shard_map/ppermute | solution.py:1177
  269.0 24.9 %collective-permute-start.26 = (bf16[240,384]{1,0:T(8,128)(2,1)S(1)}, bf16[240,384]{1,0:T(8,128)(2,1)S(1)}, u32[]{:S(2)}, u32[]{:S(2)}) collective-permute-start(bf16[240,384]{1,0:T(8,128)(2,1)S(1)} %get-tuple-element.220), channel_id=1, source_target_pairs={{0,3},{1,2},{2,1},{3,0},{4,7},{5,6},{6,5},{7,4},{8,11},{9,10},{10,... | collective-permute-start | bytes 552968 | tf_op jit(solution)/shard_map/ppermute | solution.py:1177
  272.1 28.0 %copy-start.6 = (bf16[768,2304]{1,0:T(8,128)(2,1)S(1)}, bf16[768,2304]{1,0:T(8,128)(2,1)}, u32[]{:S(2)}) copy-start(bf16[768,2304]{1,0:T(8,128)(2,1)} %w_in.1) | copy-start | bytes 10616836
  272.1 28.0 %copy-start.22 = (f32[1152,768]{1,0:T(8,128)S(1)}, f32[1152,768]{1,0:T(8,128)}, u32[]{:S(2)}) copy-start(f32[1152,768]{1,0:T(8,128)} %get-tuple-element.137.back_mid) | copy-start | bytes 10616836
  272.1 28.0 %copy-start.43 = (f32[8,768]{1,0:T(8,128)S(1)}, f32[8,768]{1,0:T(8,128)}, u32[]{:S(2)}) copy-start(f32[8,768]{1,0:T(8,128)} %copy-done.42) | copy-start | bytes 73732
  272.1 28.0 %copy-start.45 = (f32[1,3072]{1,0:T(1,128)S(1)}, f32[1,3072]{1,0:T(1,128)}, u32[]{:S(2)}) copy-start(f32[1,3072]{1,0:T(1,128)} %copy-done.44) | copy-start | bytes 36868
  294.0 19.3 %collective-permute-start.27 = (bf16[240,384]{1,0:T(8,128)(2,1)S(1)}, bf16[240,384]{1,0:T(8,128)(2,1)S(1)}, u32[]{:S(2)}, u32[]{:S(2)}) collective-permute-start(bf16[240,384]{1,0:T(8,128)(2,1)S(1)} %add_convert_fusion.16), channel_id=1, source_target_pairs={{0,1},{1,0},{2,3},{3,2},{4,5},{5,4},{6,7},{7,6},{8,9},{9,8},{10,11... | collective-permute-start | bytes 552968 | tf_op jit(solution)/shard_map/ppermute | solution.py:1177
  297.7 16.3 %collective-permute-start.28 = (bf16[240,384]{1,0:T(8,128)(2,1)S(1)}, bf16[240,384]{1,0:T(8,128)(2,1)S(1)}, u32[]{:S(2)}, u32[]{:S(2)}) collective-permute-start(bf16[240,384]{1,0:T(8,128)(2,1)S(1)} %add_convert_fusion.16), channel_id=1, source_target_pairs={{0,2},{1,3},{2,0},{3,1},{4,6},{5,7},{6,4},{7,5},{8,10},{9,11},{10,... | collective-permute-start | bytes 552968 | tf_op jit(solution)/shard_map/ppermute | solution.py:1177
  297.9 16.1 %collective-permute-start.29 = (bf16[240,384]{1,0:T(8,128)(2,1)S(1)}, bf16[240,384]{1,0:T(8,128)(2,1)S(1)}, u32[]{:S(2)}, u32[]{:S(2)}) collective-permute-start(bf16[240,384]{1,0:T(8,128)(2,1)S(1)} %add_convert_fusion.16), channel_id=1, source_target_pairs={{0,3},{1,2},{2,1},{3,0},{4,7},{5,6},{6,5},{7,4},{8,11},{9,10},{10,... | collective-permute-start | bytes 552968 | tf_op jit(solution)/shard_map/ppermute | solution.py:1177
  300.1 28.6 %collective-permute-start.30 = (bf16[16,144,384]{2,1,0:T(8,128)(2,1)}, bf16[16,144,384]{2,1,0:T(8,128)(2,1)}, u32[]{:S(2)}, u32[]{:S(2)}) collective-permute-start(bf16[16,144,384]{2,1,0:T(8,128)(2,1)} %get-tuple-element.173), channel_id=1, source_target_pairs={{0,4},{4,0},{8,12},{12,8},{16,20},{20,16},{24,28},{28,24},{1,5},{5... | collective-permute-start | bytes 5308424 | tf_op jit(solution)/shard_map/ppermute | solution.py:1177
  318.3 28.1 %collective-permute-start.31 = (bf16[2,384,768]{2,1,0:T(8,128)(2,1)}, bf16[2,384,768]{2,1,0:T(8,128)(2,1)}, u32[]{:S(2)}, u32[]{:S(2)}) collective-permute-start(bf16[2,384,768]{2,1,0:T(8,128)(2,1)} %get-tuple-element.177), channel_id=1, source_target_pairs={{0,0},{1,1},{4,2},{5,3},{2,4},{3,5},{6,6},{7,7},{8,8},{9,9},{12,10... | collective-permute-start | bytes 3538952 | tf_op jit(solution)/shard_map/ppermute | solution.py:1289
  330.6 17.1 %collective-permute-start.34 = (bf16[4,160,384]{2,1,0:T(8,128)(2,1)S(1)}, bf16[4,160,384]{2,1,0:T(8,128)(2,1)S(1)}, u32[]{:S(2)}, u32[]{:S(2)}) collective-permute-start(bf16[4,160,384]{2,1,0:T(8,128)(2,1)S(1)} %pad_maximum_fusion.6), channel_id=1, source_target_pairs={{0,24},{4,28},{8,16},{12,20},{16,8},{20,12},{24,0},{28,4},{1,25},{... | collective-permute-start | bytes 1474568 | tf_op jit(solution)/shard_map/ppermute | solution.py:1177
  333.9 21.9 %collective-permute-start.33 = (bf16[4,160,384]{2,1,0:T(8,128)(2,1)}, bf16[4,160,384]{2,1,0:T(8,128)(2,1)S(1)}, u32[]{:S(2)}, u32[]{:S(2)}) collective-permute-start(bf16[4,160,384]{2,1,0:T(8,128)(2,1)} %pad_maximum_fusion.5), channel_id=1, source_target_pairs={{0,16},{4,20},{8,24},{12,28},{16,0},{20,4},{24,8},{28,12},{1,17},{... | collective-permute-start | bytes 1474568 | tf_op jit(solution)/shard_map/ppermute | solution.py:1177
  335.2 20.5 %collective-permute-start.32 = (bf16[4,160,384]{2,1,0:T(8,128)(2,1)}, bf16[4,160,384]{2,1,0:T(8,128)(2,1)S(1)}, u32[]{:S(2)}, u32[]{:S(2)}) collective-permute-start(bf16[4,160,384]{2,1,0:T(8,128)(2,1)} %pad_maximum_fusion.4), channel_id=1, source_target_pairs={{0,8},{4,12},{8,0},{12,4},{16,24},{20,28},{24,16},{28,20},{1,9},{5... | collective-permute-start | bytes 1474568 | tf_op jit(solution)/shard_map/ppermute | solution.py:1177
  356.0 31.9 %copy-start.14 = (bf16[384,768]{1,0:T(8,128)(2,1)S(1)}, bf16[384,768]{1,0:T(8,128)(2,1)}, u32[]{:S(2)}) copy-start(bf16[384,768]{1,0:T(8,128)(2,1)} %copy-done.13) | copy-start | bytes 1769476
  356.0 6.7 %collective-permute-start.35 = (bf16[160,384]{1,0:T(8,128)(2,1)S(1)}, bf16[160,384]{1,0:T(8,128)(2,1)S(1)}, u32[]{:S(2)}, u32[]{:S(2)}) collective-permute-start(bf16[160,384]{1,0:T(8,128)(2,1)S(1)} %get-tuple-element.227), channel_id=1, source_target_pairs={{0,1},{1,0},{2,3},{3,2},{4,5},{5,4},{6,7},{7,6},{8,9},{9,8},{10,11... | collective-permute-start | bytes 368648 | tf_op jit(solution)/shard_map/ppermute | solution.py:1177
  357.4 12.4 %collective-permute-start.36 = (bf16[160,384]{1,0:T(8,128)(2,1)S(1)}, bf16[160,384]{1,0:T(8,128)(2,1)S(1)}, u32[]{:S(2)}, u32[]{:S(2)}) collective-permute-start(bf16[160,384]{1,0:T(8,128)(2,1)S(1)} %get-tuple-element.229), channel_id=1, source_target_pairs={{0,2},{1,3},{2,0},{3,1},{4,6},{5,7},{6,4},{7,5},{8,10},{9,11},{10,... | collective-permute-start | bytes 368648 | tf_op jit(solution)/shard_map/ppermute | solution.py:1177
  359.1 10.6 %collective-permute-start.37 = (bf16[160,384]{1,0:T(8,128)(2,1)S(1)}, bf16[160,384]{1,0:T(8,128)(2,1)S(1)}, u32[]{:S(2)}, u32[]{:S(2)}) collective-permute-start(bf16[160,384]{1,0:T(8,128)(2,1)S(1)} %get-tuple-element.228), channel_id=1, source_target_pairs={{0,3},{1,2},{2,1},{3,0},{4,7},{5,6},{6,5},{7,4},{8,11},{9,10},{10,... | collective-permute-start | bytes 368648 | tf_op jit(solution)/shard_map/ppermute | solution.py:1177
  369.8 6.3 %collective-permute-start.38 = (bf16[160,384]{1,0:T(8,128)(2,1)S(1)}, bf16[160,384]{1,0:T(8,128)(2,1)S(1)}, u32[]{:S(2)}, u32[]{:S(2)}) collective-permute-start(bf16[160,384]{1,0:T(8,128)(2,1)S(1)} %fusion.14), channel_id=1, source_target_pairs={{0,1},{1,0},{2,3},{3,2},{4,5},{5,4},{6,7},{7,6},{8,9},{9,8},{10,11... | collective-permute-start | bytes 368648 | tf_op jit(solution)/shard_map/ppermute | solution.py:1177
  371.8 12.4 %collective-permute-start.39 = (bf16[160,384]{1,0:T(8,128)(2,1)S(1)}, bf16[160,384]{1,0:T(8,128)(2,1)S(1)}, u32[]{:S(2)}, u32[]{:S(2)}) collective-permute-start(bf16[160,384]{1,0:T(8,128)(2,1)S(1)} %fusion.14), channel_id=1, source_target_pairs={{0,2},{1,3},{2,0},{3,1},{4,6},{5,7},{6,4},{7,5},{8,10},{9,11},{10,... | collective-permute-start | bytes 368648 | tf_op jit(solution)/shard_map/ppermute | solution.py:1177
  372.9 11.2 %collective-permute-start.40 = (bf16[160,384]{1,0:T(8,128)(2,1)S(1)}, bf16[160,384]{1,0:T(8,128)(2,1)S(1)}, u32[]{:S(2)}, u32[]{:S(2)}) collective-permute-start(bf16[160,384]{1,0:T(8,128)(2,1)S(1)} %fusion.14), channel_id=1, source_target_pairs={{0,3},{1,2},{2,1},{3,0},{4,7},{5,6},{6,5},{7,4},{8,11},{9,10},{10,... | collective-permute-start | bytes 368648 | tf_op jit(solution)/shard_map/ppermute | solution.py:1177
  384.2 5.7 %collective-permute-start.42 = (bf16[4,4,240,384]{3,2,1,0:T(8,128)(2,1)}, bf16[4,4,240,384]{3,2,1,0:T(8,128)(2,1)S(1)}, u32[]{:S(2)}, u32[]{:S(2)}) collective-permute-start(bf16[4,4,240,384]{3,2,1,0:T(8,128)(2,1)} %bitcast.105), channel_id=1, source_target_pairs={{0,4},{4,0},{8,12},{12,8},{16,20},{20,16},{24,28},{28,24},{1,5},{5... | collective-permute-start | bytes 8847368 | tf_op jit(solution)/shard_map/ppermute | solution.py:1177
  384.3 18.7 %collective-permute-start.43 = (bf16[4,160,384]{2,1,0:T(8,128)(2,1)S(1)}, bf16[4,160,384]{2,1,0:T(8,128)(2,1)S(1)}, u32[]{:S(2)}, u32[]{:S(2)}) collective-permute-start(bf16[4,160,384]{2,1,0:T(8,128)(2,1)S(1)} %pad_maximum_fusion.7), channel_id=1, source_target_pairs={{0,8},{4,12},{8,0},{12,4},{16,24},{20,28},{24,16},{28,20},{1,9},{5... | collective-permute-start | bytes 1474568 | tf_op jit(solution)/shard_map/ppermute | solution.py:1177
  385.8 23.8 %collective-permute-start.44 = (bf16[4,160,384]{2,1,0:T(8,128)(2,1)S(1)}, bf16[4,160,384]{2,1,0:T(8,128)(2,1)S(1)}, u32[]{:S(2)}, u32[]{:S(2)}) collective-permute-start(bf16[4,160,384]{2,1,0:T(8,128)(2,1)S(1)} %pad_maximum_fusion.7), channel_id=1, source_target_pairs={{0,16},{4,20},{8,24},{12,28},{16,0},{20,4},{24,8},{28,12},{1,17},{... | collective-permute-start | bytes 1474568 | tf_op jit(solution)/shard_map/ppermute | solution.py:1177
  386.3 23.4 %collective-permute-start.45 = (bf16[4,160,384]{2,1,0:T(8,128)(2,1)S(1)}, bf16[4,160,384]{2,1,0:T(8,128)(2,1)S(1)}, u32[]{:S(2)}, u32[]{:S(2)}) collective-permute-start(bf16[4,160,384]{2,1,0:T(8,128)(2,1)S(1)} %pad_maximum_fusion.7), channel_id=1, source_target_pairs={{0,24},{4,28},{8,16},{12,20},{16,8},{20,12},{24,0},{28,4},{1,25},{... | collective-permute-start | bytes 1474568 | tf_op jit(solution)/shard_map/ppermute | solution.py:1177
  387.9 15.2 %collective-permute-start.41 = (bf16[384,768]{1,0:T(8,128)(2,1)S(1)}, bf16[384,768]{1,0:T(8,128)(2,1)S(1)}, u32[]{:S(2)}, u32[]{:S(2)}) collective-permute-start(bf16[384,768]{1,0:T(8,128)(2,1)S(1)} %copy-done.14), channel_id=1, source_target_pairs={{1,0},{0,1},{5,2},{4,3},{3,4},{2,5},{7,6},{6,7},{9,8},{8,9},{13,10... | collective-permute-start | bytes 1769480 | tf_op jit(solution)/shard_map/ppermute | solution.py:1289
  410.0 4.0 collective-permute-start.46
  (45 other events, 218.7 us)
Sparse Core Ops, SparseCore 0:
  215.4 81.2 all-gather.4
  315.2 59.1 all-gather.6

commit v2 on v1

--- a/solution.py
+++ b/solution.py
@@ -699,7 +699,7 @@
         grid=(count,),
         in_specs=[SMEM, block, back_block, block, block] + wide,
         out_specs=[out] + out_wide,
-        compiler_params=limits(28),
+        compiler_params=limits(56),
         cost_estimate=lasting(n * keys * count // 180000),
         name="attend_back",
     )(where, q, do, o, t, *kvs)
@@ -830,7 +830,7 @@
             pltpu.VMEM((n, tile), BF16),
             pltpu.SemaphoreType.DMA((8,)),
         ],
-        compiler_params=limits(48),
+        compiler_params=limits(40),
         cost_estimate=lasting(36),
         name="feed",
     )(where, att_full, att_short, *xs, *cots, w_out, vecs, w1, b1, w2)
@@ -928,7 +928,7 @@
             pltpu.VMEM(v.shape, v.dtype) for v in (att_full, att_short, *cots, mid)
         ]
         + [pltpu.SemaphoreType.DMA((5,))],
-        compiler_params=limits(44),
+        compiler_params=limits(38),
         cost_estimate=lasting(26),
         name="feed_back",
     )(where, att_full, att_short, *cots, w_out, vecs, mid, normed, hidden_low, w1)

time: 430 us -> 423 us (0.984)
  local copies, waits for them, and re-layouts: 24.9 us -> 14.5 us
  waiting for transfers between devices: 63.5 us -> 72.9 us
    unnamed x120 -> x94, local copies, waits for them, and re-layouts: 20.1 us -> 9.7 us
    ppermute x36, waiting for transfers between devices: 51.4 us -> 60.3 us  [swap(): return lax.ppermute(array, axis, flip_pairs(8 if axis == 'dp' else 4, mask))]
    ppermute x4, starting transfers between devices: 13.1 us -> 4.7 us  [give(): lax.ppermute(piece, ('dp', 'blk'), [pair[::-1] for pair in column_pairs(t...]
    ppermute x36, starting transfers between devices: 69.7 us -> 75.7 us  [swap(): return lax.ppermute(array, axis, flip_pairs(8 if axis == 'dp' else 4, mask))]
  transfers between devices with their start and end apart: 49 -> 49, of which waited for: 17 -> 16; matrix products, arithmetic and copies ran while one was open for 6% -> 6% of each run, Pallas kernels for 35% -> 35%
where the time goes in v2:
time: 423 us; the launch traced here: 419 us
  Pallas kernels  192 us (45%)
  starting transfers between devices  102 us (24%)
  waiting for transfers between devices  72.9 us (17%)
  other arithmetic  18.9 us (4%)
  between operations  18 us (4%)
  local copies, waits for them, and re-layouts  14.5 us (3%)
    ppermute x36, starting transfers between devices, swap(): return lax.ppermute(array, axis, flip_pairs(8 if axis == 'dp' else 4, mask))  75.7 us
    ppermute x36, waiting for transfers between devices, swap(): return lax.ppermute(array, axis, flip_pairs(8 if axis == 'dp' else 4, mask))  60.3 us
    pallas_call x2, Pallas kernels, attend_back(): pl.pallas_call(functools.partial(attend_back_kernel, pieces=len(kvs), val...  53.5 us
    pallas_call x1, Pallas kernels, feed(): pl.pallas_call(functools.partial(feed_kernel, steps=steps, tile=tile), gr...  34 us
    pallas_call x2, Pallas kernels, attend(): pl.pallas_call(functools.partial(attend_kernel, pieces=len(kvs), valid=va...  29.6 us
    pallas_call x1, Pallas kernels, feed_back(): pl.pallas_call(functools.partial(feed_back_kernel, steps=steps), grid=(st...  23.7 us
    pallas_call x4, Pallas kernels, finish(): pl.pallas_call(functools.partial(finish_kernel, with_lines=with_lines), g...  15.7 us
    ppermute x3, starting transfers between devices, exchange_short(): return tuple((lax.ppermute(block, ('dp', 'blk'), p) for p in pairs))  11.3 us
  transfers between devices with their start and end apart: 49, of which 16 were waited for; matrix products, arithmetic and copies ran while one was open for 6% of the time, Pallas kernels for 35%

profile of v2, /device:TPU:0, one launch (start us, length us, event | category | flops | bytes accessed | tf_op | source)
XLA Modules:
  0.0 418.9 jit_solution(75427693337255945)
XLA Ops:
  7.3 3.5 leave.2
  10.8 1.9 collective-permute-start
  12.7 3.0 collective-permute-start.1
  16.0 3.3 leave.3
  19.3 2.0 copy-done.5
  22.6 7.5 %collective-permute-done.1.x2_in.x2 = bf16[384,768]{1,0:T(8,128)(2,1)S(1)} collective-permute-done((bf16[384,768]{1,0:T(8,128)(2,1)}, bf16[384,768]{1,0:T(8,128)(2,1)S(1)}, u32[]{:S(2)}, u32[]{:S(2)}) %collective-permute-start.1) | collective-permute-done | bytes 589856 | tf_op jit(solution)/shard_map/ppermute | solution.py:1281
  30.0 5.0 %project.1 = (bf16[768,768]{1,0:T(8,128)(2,1)S(1)}, bf16[2,768,768]{2,1,0:T(8,128)(2,1)}) custom-call(bf16[2,384,768]{2,1,0:T(8,128)(2,1)S(1)} %collective-permute-done.x13_in.x13, bf16[384,768]{1,0:T(8,128)(2,1)S(1)} %collective-permute-done.1.x2_in.x2, f32[4,768]{1,0:T(4,128)S(1)} %get-tuple-element.235.vecs, bf16[768,2304]{1,0:T(8,128)(2,1)S(1)} %get-tuple-element.114.w_in), custom_call_target="tpu_custom_call" | custom-call | flops 4000000000 | bytes 1048576 | tf_op jit(solution)/shard_map/project/pallas_call | solution.py:461
  35.0 20.9 %collective-permute-start.2 = (bf16[2,768,768]{2,1,0:T(8,128)(2,1)}, bf16[2,768,768]{2,1,0:T(8,128)(2,1)}, u32[]{:S(2)}, u32[]{:S(2)}) collective-permute-start(bf16[2,768,768]{2,1,0:T(8,128)(2,1)} %get-tuple-element.116.refs_1_.refs_5_), channel_id=1, source_target_pairs={{0,4},{4,0},{8,12},{12,8},{16,20},{20,16},{24,28},{28,24},{1,5},{5... | collective-permute-start | bytes 7077896 | tf_op jit(solution)/shard_map/ppermute | solution.py:1177
  56.0 8.1 %collective-permute-start.3 = (bf16[384,768]{1,0:T(8,128)(2,1)}, bf16[384,768]{1,0:T(8,128)(2,1)S(1)}, u32[]{:S(2)}, u32[]{:S(2)}) collective-permute-start(bf16[384,768]{1,0:T(8,128)(2,1)} %slice_bitcast_fusion.2), channel_id=1, source_target_pairs={{0,1},{1,0},{2,3},{3,2},{4,5},{6,7},{8,9},{9,8},{10,11},{11,10},{1... | collective-permute-start | bytes 1769480 | tf_op jit(solution)/shard_map/ppermute | solution.py:1166
  64.1 1.9 collective-permute-start.4
  67.4 2.4 collective-permute-start.6
  69.8 2.8 collective-permute-start.7
  72.6 21.1 %attend.2 = (f32[768,768]{1,0:T(8,128)S(1)}, bf16[768,768]{1,0:T(8,128)(2,1)S(1)}) custom-call(bf16[768,768]{1,0:T(8,128)(2,1)S(1)} %get-tuple-element.155.refs_0_.refs_1_, bf16[2,768,768]{2,1,0:T(8,128)(2,1)} %get-tuple-element.116.refs_1_.refs_5_, bf16[2,768,768]{2,1,0:T(8,128)(2,1)} %collective-permute-done.2.refs_2_.refs_6_), custom_call_target="tpu_custom_call" | custom-call | flops 24999999488 | bytes 1048576 | tf_op jit(solution)/shard_map/attend/pallas_call | solution.py:605
  93.8 4.3 %project_short.1 = (bf16[384,768]{1,0:T(8,128)(2,1)S(1)}, bf16[2,768,768]{2,1,0:T(8,128)(2,1)S(1)}, bf16[2,128,768]{2,1,0:T(8,128)(2,1)S(1)}) custom-call(s32[3]{0:T(128)S(1)} %get-tuple-element.198.where.refs_0_, bf16[2,384,768]{2,1,0:T(8,128)(2,1)S(1)} %collective-permute-done.x13_in.x13, bf16[384,768]{1,0:T(8,128)(2,1)S(1)} %collective-permute-done.3.near, ...), custom_call_target="tpu_custom_call" | custom-call | flops 4000000000 | bytes 1048576 | tf_op jit(solution)/shard_map/project_short/pallas_call | solution.py:496
  98.1 8.5 %attend.3 = (f32[384,768]{1,0:T(8,128)S(1)}, bf16[384,768]{1,0:T(8,128)(2,1)S(1)}) custom-call(bf16[384,768]{1,0:T(8,128)(2,1)S(1)} %get-tuple-element.141.refs_0_.refs_1_, bf16[2,768,768]{2,1,0:T(8,128)(2,1)S(1)} %get-tuple-element.122.refs_1_.refs_5_, bf16[2,128,768]{2,1,0:T(8,128)(2,1)S(1)} %get-tuple-element.123.refs_2_.refs_6_), custom_call_target="tpu_custom_call" | custom-call | flops 7000000000 | bytes 1048576 | tf_op jit(solution)/shard_map/attend/pallas_call | solution.py:605
  106.7 34.0 %feed.1 = (bf16[2,384,768]{2,1,0:T(8,128)(2,1)S(1)}, bf16[384,768]{1,0:T(8,128)(2,1)S(1)}, f32[1152,768]{1,0:T(8,128)}, bf16[1152,768]{1,0:T(8,128)(2,1)S(1)}, b...) custom-call(s32[3]{0:T(128)S(1)} %get-tuple-element.198.where.refs_0, ...), custom_call_target="tpu_custom_call" | custom-call | flops 35999997952 | bytes 1048576 | tf_op jit(solution)/shard_map/feed/pallas_call | solution.py:804
  140.7 8.3 %collective-permute-start.9 = (bf16[16,192,384]{2,1,0:T(8,128)(2,1)S(1)}, bf16[16,192,384]{2,1,0:T(8,128)(2,1)S(1)}, u32[]{:S(2)}, u32[]{:S(2)}) collective-permute-start(bf16[16,192,384]{2,1,0:T(8,128)(2,1)S(1)} %get-tuple-element.133), channel_id=1, source_target_pairs={{0,4},{4,0},{8,12},{12,8},{16,20},{20,16},{24,28},{28,24},{1,5},{5... | collective-permute-start | bytes 7077896 | tf_op jit(solution)/shard_map/ppermute | solution.py:1177
  149.8 3.4 collective-permute-done.9
  153.8 1.6 collective-permute-start.11
  155.4 1.5 collective-permute-start.12
  157.4 23.7 %feed_back.1 = (bf16[1152,768]{1,0:T(8,128)(2,1)S(1)}, f32[1152,768]{1,0:T(8,128)}, bf16[16,240,384]{2,1,0:T(8,128)(2,1)}, bf16[16,240,384]{2,1,0:T(8,128)(2,1)S(1)}, f32[8,768]{1,0:T(8,128)S(1)}) custom-call(s32[3]{0:T(128)S(1)} %get-tuple-element.198.where.refs_0_, f32[768,768]{1,0:T(8,128)S(1)} %copy-done.27, ...), custom_call_target="tpu_custom_call" | custom-call | flops 25999998976 | bytes 1048576 | tf_op jit(solution)/shard_map/feed_back/pallas_call | solution.py:903
  182.7 9.7 %collective-permute-start.15 = (bf16[192,384]{1,0:T(8,128)(2,1)S(1)}, bf16[192,384]{1,0:T(8,128)(2,1)S(1)}, u32[]{:S(2)}, u32[]{:S(2)}) collective-permute-start(bf16[192,384]{1,0:T(8,128)(2,1)S(1)} %get-tuple-element.225), channel_id=1, source_target_pairs={{0,2},{1,3},{2,0},{3,1},{4,6},{5,7},{6,4},{7,5},{8,10},{9,11},{10,... | collective-permute-start | bytes 442376 | tf_op jit(solution)/shard_map/ppermute | solution.py:1177
  192.4 16.0 %attend_back.2 = (bf16[384,768]{1,0:T(8,128)(2,1)}, bf16[2,768,768]{2,1,0:T(8,128)(2,1)}, bf16[2,768,768]{2,1,0:T(8,128)(2,1)}) custom-call(s32[3]{0:T(128)} %copy-done.3, bf16[384,768]{1,0:T(8,128)(2,1)} %copy-done.18, bf16[1152,768]{1,0:T(8,128)(2,1)} %copy-done.23, f32[384,768]{1,0:T(8,128)} %copy-done.21, bf16[384,768]{1,0:T(8,128)(2,1)} %copy-done.24, ...), custom_call_target="tpu_custom_call" | custom-call | flops 11000000512 | bytes 1048576 | tf_op jit(solution)/shard_map/attend_back/pallas_call | solution.py:693
  210.9 3.8 add_convert_fusion.2
  214.9 1.6 add_convert_fusion
  217.1 1.5 collective-permute-start.20
  218.6 1.6 collective-permute-start.21
  220.6 37.5 %attend_back.3 = (bf16[768,768]{1,0:T(8,128)(2,1)}, bf16[2,768,768]{2,1,0:T(8,128)(2,1)}, bf16[2,768,768]{2,1,0:T(8,128)(2,1)}) custom-call(s32[3]{0:T(128)} %copy-done.3, bf16[768,768]{1,0:T(8,128)(2,1)} %copy-done.16, bf16[1152,768]{1,0:T(8,128)(2,1)} %copy-done.23, f32[768,768]{1,0:T(8,128)} %copy-done.26, bf16[768,768]{1,0:T(8,128)(2,1)} %copy-done.28, ...), custom_call_target="tpu_custom_call" | custom-call | flops 38999998464 | bytes 1048576 | tf_op jit(solution)/shard_map/attend_back/pallas_call | solution.py:693
  258.8 1.5 collective-permute-start.24
  260.3 2.4 collective-permute-start.25
  262.8 1.4 collective-permute-start.26
  265.5 10.8 %project_back.1 = (bf16[16,144,384]{2,1,0:T(8,128)(2,1)}, bf16[16,144,384]{2,1,0:T(8,128)(2,1)S(1)}, bf16[3,1152,768]{2,1,0:T(8,128)(2,1)}) custom-call(s32[3]{0:T(128)S(1)} %copy-done.4, bf16[2,384,768]{2,1,0:T(8,128)(2,1)S(1)} %copy-done.2, bf16[384,768]{1,0:T(8,128)(2,1)S(1)} %copy-done.9, f32[4,768]{1,0:T(4,128)S(1)} %get-tuple-element.235.vecs, ...), custom_call_target="tpu_custom_call" | custom-call | flops 11000000512 | bytes 1048576 | tf_op jit(solution)/shard_map/project_back/pallas_call | solution.py:984
  277.3 11.5 %collective-permute-done.26 = bf16[240,384]{1,0:T(8,128)(2,1)S(1)} collective-permute-done((bf16[240,384]{1,0:T(8,128)(2,1)S(1)}, bf16[240,384]{1,0:T(8,128)(2,1)S(1)}, u32[]{:S(2)}, u32[]{:S(2)}) %collective-permute-start.26) | collective-permute-done | bytes 184352 | tf_op jit(solution)/shard_map/ppermute | solution.py:1177
  288.9 4.0 collective-permute-start.27
  292.9 2.4 collective-permute-start.29
  295.4 2.5 copy-done.15
  297.9 8.9 %input_back.1 = (bf16[2,384,768]{2,1,0:T(8,128)(2,1)S(1)}, bf16[384,768]{1,0:T(8,128)(2,1)S(1)}, bf16[16,16,384]{2,1,0:T(8,128)(2,1)S(1)}) custom-call(s32[3]{0:T(128)S(1)} %copy-done.4, bf16[2,384,768]{2,1,0:T(8,128)(2,1)S(1)} %copy-done.2, bf16[384,768]{1,0:T(8,128)(2,1)S(1)} %copy-done.9, f32[4,768]{1,0:T(4,128)S(1)} %get-tuple-element.235.vecs, ...), custom_call_target="tpu_custom_call" | custom-call | flops 8999999488 | bytes 1048576 | tf_op jit(solution)/shard_map/input_back/pallas_call | solution.py:1054
  307.6 1.4 collective-permute-done.28
  313.3 1.7 collective-permute-start.31
  315.0 1.9 add_convert_fusion.12
  317.0 2.6 collective-permute-start.34
  323.2 1.4 pad_maximum_fusion.1
  324.6 3.0 slice_bitcast_fusion
  327.6 4.9 %finish.4 = f32[3072,768]{1,0:T(8,128)} custom-call(s32[3]{0:T(128)S(1)} %broadcast_1_where.2.where, bf16[4,4,192,384]{3,2,1,0:T(8,128)(2,1)S(1)} %get-tuple-element.204.mine, bf16[4,4,192,384]{3,2,1,0:T(8,128)(2,1)S(1)} %get-tuple-element.203.other), custom_call_target="tpu_custom_call" | custom-call | flops 4000000000 | bytes 1048576 | tf_op jit(solution)/shard_map/finish/pallas_call | solution.py:1122
  332.5 6.1 %collective-permute-done.34 = bf16[4,160,384]{2,1,0:T(8,128)(2,1)S(1)} collective-permute-done((bf16[4,160,384]{2,1,0:T(8,128)(2,1)S(1)}, bf16[4,160,384]{2,1,0:T(8,128)(2,1)S(1)}, u32[]{:S(2)}, u32[]{:S(2)}) %collective-permute-start.34) | collective-permute-done | bytes 491552 | tf_op jit(solution)/shard_map/ppermute | solution.py:1177
  338.6 11.5 %collective-permute-done.33 = bf16[4,160,384]{2,1,0:T(8,128)(2,1)S(1)} collective-permute-done((bf16[4,160,384]{2,1,0:T(8,128)(2,1)}, bf16[4,160,384]{2,1,0:T(8,128)(2,1)S(1)}, u32[]{:S(2)}, u32[]{:S(2)}) %collective-permute-start.33) | collective-permute-done | bytes 491552 | tf_op jit(solution)/shard_map/ppermute | solution.py:1177
  350.4 2.2 collective-permute-start.35
  352.6 2.4 collective-permute-start.37
  356.3 7.8 %collective-permute-done.36 = bf16[160,384]{1,0:T(8,128)(2,1)S(1)} collective-permute-done((bf16[160,384]{1,0:T(8,128)(2,1)S(1)}, bf16[160,384]{1,0:T(8,128)(2,1)S(1)}, u32[]{:S(2)}, u32[]{:S(2)}) %collective-permute-start.36) | collective-permute-done | bytes 122912 | tf_op jit(solution)/shard_map/ppermute | solution.py:1177
  364.2 2.4 collective-permute-start.38
  366.7 2.4 collective-permute-start.40
  369.1 1.3 collective-permute-done.38
  370.5 7.6 %collective-permute-done.39 = bf16[160,384]{1,0:T(8,128)(2,1)S(1)} collective-permute-done((bf16[160,384]{1,0:T(8,128)(2,1)S(1)}, bf16[160,384]{1,0:T(8,128)(2,1)S(1)}, u32[]{:S(2)}, u32[]{:S(2)}) %collective-permute-start.39) | collective-permute-done | bytes 122912 | tf_op jit(solution)/shard_map/ppermute | solution.py:1177
  378.2 1.4 collective-permute-start.43
  380.2 1.6 collective-permute-start.45
  381.8 2.2 collective-permute-start.41
  384.0 1.8 copy-done
  385.8 2.1 finish.6
  387.9 4.7 %finish.5 = f32[768,3072]{1,0:T(8,128)} custom-call(s32[3]{0:T(128)S(1)} %get-tuple-element.197.where, bf16[4,4,240,384]{3,2,1,0:T(8,128)(2,1)S(1)} %bitcast.107, bf16[4,4,240,384]{3,2,1,0:T(8,128)(2,1)S(1)} %collective-permute-done.42.other), custom_call_target="tpu_custom_call" | custom-call | flops 4000000000 | bytes 1048576 | tf_op jit(solution)/shard_map/finish/pallas_call | solution.py:1122
  392.6 5.1 %collective-permute-done.41 = bf16[384,768]{1,0:T(8,128)(2,1)S(1)} collective-permute-done((bf16[384,768]{1,0:T(8,128)(2,1)S(1)}, bf16[384,768]{1,0:T(8,128)(2,1)S(1)}, u32[]{:S(2)}, u32[]{:S(2)}) %collective-permute-start.41) | collective-permute-done | bytes 589856 | tf_op jit(solution)/shard_map/ppermute | solution.py:1289
  397.7 5.8 %collective-permute-done.44 = bf16[4,160,384]{2,1,0:T(8,128)(2,1)S(1)} collective-permute-done((bf16[4,160,384]{2,1,0:T(8,128)(2,1)S(1)}, bf16[4,160,384]{2,1,0:T(8,128)(2,1)S(1)}, u32[]{:S(2)}, u32[]{:S(2)}) %collective-permute-start.44) | collective-permute-done | bytes 491552 | tf_op jit(solution)/shard_map/ppermute | solution.py:1177
  403.9 1.4 fusion.1
  405.3 2.1 maximum_convert_fusion
  407.8 4.0 finish.7
  (188 shorter events, 22.5 us)
Async XLA Ops:
  7.2 317.4 %all-gather.5.cloned.1.call-start = ((), (), s32[]{:S(2)}) async-start(), calls=%async_computation | async-start | bytes 4866048 | tf_op jit(solution)/shard_map/all_gather | solution.py:1240
  10.8 10.8 %collective-permute-start = (bf16[2,384,768]{2,1,0:T(8,128)(2,1)}, bf16[2,384,768]{2,1,0:T(8,128)(2,1)S(1)}, u32[]{:S(2)}, u32[]{:S(2)}) collective-permute-start(bf16[2,384,768]{2,1,0:T(8,128)(2,1)} %get-tuple-element.106), channel_id=1, source_target_pairs={{0,0},{1,1},{2,4},{3,5},{4,2},{5,3},{6,6},{7,7},{8,8},{9,9},{10,12... | collective-permute-start | bytes 3538952 | tf_op jit(solution)/shard_map/ppermute | solution.py:1281
  12.7 17.3 %collective-permute-start.1 = (bf16[384,768]{1,0:T(8,128)(2,1)}, bf16[384,768]{1,0:T(8,128)(2,1)S(1)}, u32[]{:S(2)}, u32[]{:S(2)}) collective-permute-start(bf16[384,768]{1,0:T(8,128)(2,1)} %get-tuple-element.107), channel_id=1, source_target_pairs={{0,1},{1,0},{2,5},{3,4},{4,3},{5,2},{6,7},{7,6},{8,9},{9,8},{10,13... | collective-permute-start | bytes 1769480 | tf_op jit(solution)/shard_map/ppermute | solution.py:1281
  21.6 13.4 %copy-start.12 = (bf16[768,2304]{1,0:T(8,128)(2,1)}, bf16[768,2304]{1,0:T(8,128)(2,1)S(1)}, u32[]{:S(2)}) copy-start(bf16[768,2304]{1,0:T(8,128)(2,1)S(1)} %get-tuple-element.114.w_in) | copy-start | bytes 10616836
  21.6 85.1 %copy-start.1 = (bf16[2,384,768]{2,1,0:T(8,128)(2,1)}, bf16[2,384,768]{2,1,0:T(8,128)(2,1)S(1)}, u32[]{:S(2)}) copy-start(bf16[2,384,768]{2,1,0:T(8,128)(2,1)S(1)} %collective-permute-done.x13_in.x13) | copy-start | bytes 3538948
  30.0 76.6 %copy-start.8 = (bf16[384,768]{1,0:T(8,128)(2,1)}, bf16[384,768]{1,0:T(8,128)(2,1)S(1)}, u32[]{:S(2)}) copy-start(bf16[384,768]{1,0:T(8,128)(2,1)S(1)} %collective-permute-done.1.x2_in.x2) | copy-start | bytes 1769476
  30.0 25.9 %copy-start.45 = (s32[3]{0:T(128)S(1)}, s32[3]{0:T(128)}, u32[]{:S(2)}) copy-start(s32[3]{0:T(128)} %constant.58.clone) | copy-start | bytes 40
  30.0 25.9 %copy-start.46 = (s32[3]{0:T(128)S(1)}, s32[3]{0:T(128)}, u32[]{:S(2)}) copy-start(s32[3]{0:T(128)} %constant.59.clone) | copy-start | bytes 40
  35.0 58.7 %copy-start.16 = (bf16[768,768]{1,0:T(8,128)(2,1)}, bf16[768,768]{1,0:T(8,128)(2,1)S(1)}, u32[]{:S(2)}) copy-start(bf16[768,768]{1,0:T(8,128)(2,1)S(1)} %get-tuple-element.155.refs_0_.refs_1_) | copy-start | bytes 3538948
  35.0 34.8 %collective-permute-start.2 = (bf16[2,768,768]{2,1,0:T(8,128)(2,1)}, bf16[2,768,768]{2,1,0:T(8,128)(2,1)}, u32[]{:S(2)}, u32[]{:S(2)}) collective-permute-start(bf16[2,768,768]{2,1,0:T(8,128)(2,1)} %get-tuple-element.116.refs_1_.refs_5_), channel_id=1, source_target_pairs={{0,4},{4,0},{8,12},{12,8},{16,20},{20,16},{24,28},{28,24},{1,5},{5... | collective-permute-start | bytes 7077896 | tf_op jit(solution)/shard_map/ppermute | solution.py:1177
  56.0 101.4 %copy-start.3 = (s32[3]{0:T(128)}, s32[3]{0:T(128)S(1)}, u32[]{:S(2)}) copy-start(s32[3]{0:T(128)S(1)} %get-tuple-element.198.where.refs_0_) | copy-start | bytes 40
  56.0 37.7 %collective-permute-start.3 = (bf16[384,768]{1,0:T(8,128)(2,1)}, bf16[384,768]{1,0:T(8,128)(2,1)S(1)}, u32[]{:S(2)}, u32[]{:S(2)}) collective-permute-start(bf16[384,768]{1,0:T(8,128)(2,1)} %slice_bitcast_fusion.2), channel_id=1, source_target_pairs={{0,1},{1,0},{2,3},{3,2},{4,5},{6,7},{8,9},{9,8},{10,11},{11,10},{1... | collective-permute-start | bytes 1769480 | tf_op jit(solution)/shard_map/ppermute | solution.py:1166
  64.1 29.6 %collective-permute-start.4 = (bf16[384,768]{1,0:T(8,128)(2,1)}, bf16[384,768]{1,0:T(8,128)(2,1)S(1)}, u32[]{:S(2)}, u32[]{:S(2)}) collective-permute-start(bf16[384,768]{1,0:T(8,128)(2,1)} %slice_bitcast_fusion.2), channel_id=1, source_target_pairs={{0,4},{1,5},{2,6},{3,7},{4,0},{6,2},{8,12},{9,13},{10,14},{11,15},... | collective-permute-start | bytes 1769480 | tf_op jit(solution)/shard_map/ppermute | solution.py:1166
  66.0 27.7 %collective-permute-start.5 = (bf16[384,768]{1,0:T(8,128)(2,1)}, bf16[384,768]{1,0:T(8,128)(2,1)S(1)}, u32[]{:S(2)}, u32[]{:S(2)}) collective-permute-start(bf16[384,768]{1,0:T(8,128)(2,1)} %slice_bitcast_fusion.2), channel_id=1, source_target_pairs={{0,5},{1,4},{2,7},{3,6},{4,1},{6,3},{8,13},{9,12},{10,15},{11,14},... | collective-permute-start | bytes 1769480 | tf_op jit(solution)/shard_map/ppermute | solution.py:1166
  67.4 39.3 %collective-permute-start.6 = (bf16[2,384,768]{2,1,0:T(8,128)(2,1)}, bf16[2,384,768]{2,1,0:T(8,128)(2,1)S(1)}, u32[]{:S(2)}, u32[]{:S(2)}) collective-permute-start(bf16[2,384,768]{2,1,0:T(8,128)(2,1)} %get-tuple-element.125), channel_id=1, source_target_pairs={{0,0},{1,1},{2,4},{3,5},{4,2},{5,3},{6,6},{7,7},{8,8},{9,9},{10,12... | collective-permute-start | bytes 3538952 | tf_op jit(solution)/shard_map/ppermute | solution.py:1281
  69.8 36.8 %collective-permute-start.7 = (bf16[384,768]{1,0:T(8,128)(2,1)}, bf16[384,768]{1,0:T(8,128)(2,1)S(1)}, u32[]{:S(2)}, u32[]{:S(2)}) collective-permute-start(bf16[384,768]{1,0:T(8,128)(2,1)} %get-tuple-element.126), channel_id=1, source_target_pairs={{0,1},{1,0},{2,5},{3,4},{4,3},{5,2},{6,7},{7,6},{8,9},{9,8},{10,13... | collective-permute-start | bytes 1769480 | tf_op jit(solution)/shard_map/ppermute | solution.py:1281
  72.6 21.2 %copy-start.13 = (bf16[768,2304]{1,0:T(8,128)(2,1)S(1)}, bf16[768,2304]{1,0:T(8,128)(2,1)}, u32[]{:S(2)}) copy-start(bf16[768,2304]{1,0:T(8,128)(2,1)} %copy-done.12) | copy-start | bytes 10616836
  98.1 8.6 %copy-start.7 = (bf16[768,768]{1,0:T(8,128)(2,1)S(1)}, bf16[768,768]{1,0:T(8,128)(2,1)}, u32[]{:S(2)}) copy-start(bf16[768,768]{1,0:T(8,128)(2,1)} %w_out.1) | copy-start | bytes 3538948
  106.6 34.0 %copy-start.24 = (bf16[384,768]{1,0:T(8,128)(2,1)}, bf16[384,768]{1,0:T(8,128)(2,1)S(1)}, u32[]{:S(2)}) copy-start(bf16[384,768]{1,0:T(8,128)(2,1)S(1)} %get-tuple-element.143.refs_4_) | copy-start | bytes 1769476
  106.6 50.8 %copy-start.21 = (f32[384,768]{1,0:T(8,128)}, f32[384,768]{1,0:T(8,128)S(1)}, u32[]{:S(2)}) copy-start(f32[384,768]{1,0:T(8,128)S(1)} %get-tuple-element.124.att_short_in.refs_3_) | copy-start | bytes 3538948
  140.7 12.5 %collective-permute-start.9 = (bf16[16,192,384]{2,1,0:T(8,128)(2,1)S(1)}, bf16[16,192,384]{2,1,0:T(8,128)(2,1)S(1)}, u32[]{:S(2)}, u32[]{:S(2)}) collective-permute-start(bf16[16,192,384]{2,1,0:T(8,128)(2,1)S(1)} %get-tuple-element.133), channel_id=1, source_target_pairs={{0,4},{4,0},{8,12},{12,8},{16,20},{20,16},{24,28},{28,24},{1,5},{5... | collective-permute-start | bytes 7077896 | tf_op jit(solution)/shard_map/ppermute | solution.py:1177
  148.9 32.2 %collective-permute-start.8 = (bf16[2,384,768]{2,1,0:T(8,128)(2,1)S(1)}, bf16[2,384,768]{2,1,0:T(8,128)(2,1)S(1)}, u32[]{:S(2)}, u32[]{:S(2)}) collective-permute-start(bf16[2,384,768]{2,1,0:T(8,128)(2,1)S(1)} %get-tuple-element.130), channel_id=1, source_target_pairs={{0,0},{1,1},{4,2},{5,3},{2,4},{3,5},{6,6},{7,7},{8,8},{9,9},{12,10... | collective-permute-start | bytes 3538952 | tf_op jit(solution)/shard_map/ppermute | solution.py:1289
  149.7 58.7 %collective-permute-start.10 = (bf16[384,768]{1,0:T(8,128)(2,1)S(1)}, bf16[384,768]{1,0:T(8,128)(2,1)S(1)}, u32[]{:S(2)}, u32[]{:S(2)}) collective-permute-start(bf16[384,768]{1,0:T(8,128)(2,1)S(1)} %get-tuple-element.139), channel_id=1, source_target_pairs={{1,0},{0,1},{5,2},{4,3},{3,4},{2,5},{7,6},{6,7},{9,8},{8,9},{13,10... | collective-permute-start | bytes 1769480 | tf_op jit(solution)/shard_map/ppermute | solution.py:1289
  153.8 27.3 %collective-permute-start.11 = (bf16[4,192,384]{2,1,0:T(8,128)(2,1)S(1)}, bf16[4,192,384]{2,1,0:T(8,128)(2,1)S(1)}, u32[]{:S(2)}, u32[]{:S(2)}) collective-permute-start(bf16[4,192,384]{2,1,0:T(8,128)(2,1)S(1)} %get-tuple-element.207), channel_id=1, source_target_pairs={{0,8},{4,12},{8,0},{12,4},{16,24},{20,28},{24,16},{28,20},{1,9},{5... | collective-permute-start | bytes 1769480 | tf_op jit(solution)/shard_map/ppermute | solution.py:1177
  155.4 25.8 %collective-permute-start.12 = (bf16[4,192,384]{2,1,0:T(8,128)(2,1)S(1)}, bf16[4,192,384]{2,1,0:T(8,128)(2,1)S(1)}, u32[]{:S(2)}, u32[]{:S(2)}) collective-permute-start(bf16[4,192,384]{2,1,0:T(8,128)(2,1)S(1)} %get-tuple-element.206), channel_id=1, source_target_pairs={{0,16},{4,20},{8,24},{12,28},{16,0},{20,4},{24,8},{28,12},{1,17},{... | collective-permute-start | bytes 1769480 | tf_op jit(solution)/shard_map/ppermute | solution.py:1177
  156.9 25.1 %collective-permute-start.13 = (bf16[4,192,384]{2,1,0:T(8,128)(2,1)S(1)}, bf16[4,192,384]{2,1,0:T(8,128)(2,1)S(1)}, u32[]{:S(2)}, u32[]{:S(2)}) collective-permute-start(bf16[4,192,384]{2,1,0:T(8,128)(2,1)S(1)} %get-tuple-element.205), channel_id=1, source_target_pairs={{0,24},{4,28},{8,16},{12,20},{16,8},{20,12},{24,0},{28,4},{1,25},{... | collective-permute-start | bytes 1769480 | tf_op jit(solution)/shard_map/ppermute | solution.py:1177
  182.7 26.5 %collective-permute-start.14 = (bf16[192,384]{1,0:T(8,128)(2,1)S(1)}, bf16[192,384]{1,0:T(8,128)(2,1)S(1)}, u32[]{:S(2)}, u32[]{:S(2)}) collective-permute-start(bf16[192,384]{1,0:T(8,128)(2,1)S(1)} %get-tuple-element.226), channel_id=1, source_target_pairs={{0,1},{1,0},{2,3},{3,2},{4,5},{5,4},{6,7},{7,6},{8,9},{9,8},{10,11... | collective-permute-start | bytes 442376 | tf_op jit(solution)/shard_map/ppermute | solution.py:1177
  182.7 26.5 %collective-permute-start.15 = (bf16[192,384]{1,0:T(8,128)(2,1)S(1)}, bf16[192,384]{1,0:T(8,128)(2,1)S(1)}, u32[]{:S(2)}, u32[]{:S(2)}) collective-permute-start(bf16[192,384]{1,0:T(8,128)(2,1)S(1)} %get-tuple-element.225), channel_id=1, source_target_pairs={{0,2},{1,3},{2,0},{3,1},{4,6},{5,7},{6,4},{7,5},{8,10},{9,11},{10,... | collective-permute-start | bytes 442376 | tf_op jit(solution)/shard_map/ppermute | solution.py:1177
  192.4 16.8 %collective-permute-start.16 = (bf16[192,384]{1,0:T(8,128)(2,1)S(1)}, bf16[192,384]{1,0:T(8,128)(2,1)S(1)}, u32[]{:S(2)}, u32[]{:S(2)}) collective-permute-start(bf16[192,384]{1,0:T(8,128)(2,1)S(1)} %get-tuple-element.224), channel_id=1, source_target_pairs={{0,3},{1,2},{2,1},{3,0},{4,7},{5,6},{6,5},{7,4},{8,11},{9,10},{10,... | collective-permute-start | bytes 442376 | tf_op jit(solution)/shard_map/ppermute | solution.py:1177
  192.4 18.5 %collective-permute-start.18 = (bf16[16,240,384]{2,1,0:T(8,128)(2,1)}, bf16[16,240,384]{2,1,0:T(8,128)(2,1)}, u32[]{:S(2)}, u32[]{:S(2)}) collective-permute-start(bf16[16,240,384]{2,1,0:T(8,128)(2,1)} %get-tuple-element.153), channel_id=1, source_target_pairs={{0,4},{4,0},{8,12},{12,8},{16,20},{20,16},{24,28},{28,24},{1,5},{5... | collective-permute-start | bytes 8847368 | tf_op jit(solution)/shard_map/ppermute | solution.py:1177
  209.9 5.0 %collective-permute-start.17 = (bf16[2,768,768]{2,1,0:T(8,128)(2,1)}, bf16[2,768,768]{2,1,0:T(8,128)(2,1)}, u32[]{:S(2)}, u32[]{:S(2)}) collective-permute-start(bf16[2,768,768]{2,1,0:T(8,128)(2,1)} %get-tuple-element.149), channel_id=1, source_target_pairs={{0,4},{4,0},{8,12},{12,8},{16,20},{20,16},{24,28},{28,24},{1,5},{5... | collective-permute-start | bytes 7077896 | tf_op jit(solution)/shard_map/ppermute | solution.py:1177
  210.4 167.7 %all-gather.7.cloned.1.call-start = ((), (), s32[]{:S(2)}) async-start(), calls=%async_computation.1 | async-start | bytes 3686400 | tf_op jit(solution)/shard_map/all_gather | solution.py:1367
  216.5 41.7 %collective-permute-start.19 = (bf16[2,384,768]{2,1,0:T(8,128)(2,1)S(1)}, bf16[2,384,768]{2,1,0:T(8,128)(2,1)S(1)}, u32[]{:S(2)}, u32[]{:S(2)}) collective-permute-start(bf16[2,384,768]{2,1,0:T(8,128)(2,1)S(1)} %add_convert_fusion), channel_id=1, source_target_pairs={{0,1},{1,0},{2,3},{3,2},{4,5},{5,4},{6,7},{7,6},{8,9},{9,8},{10,11... | collective-permute-start | bytes 3538952 | tf_op jit(solution)/shard_map/ppermute | solution.py:1177
  217.1 41.1 %collective-permute-start.20 = (bf16[4,240,384]{2,1,0:T(8,128)(2,1)}, bf16[4,240,384]{2,1,0:T(8,128)(2,1)S(1)}, u32[]{:S(2)}, u32[]{:S(2)}) collective-permute-start(bf16[4,240,384]{2,1,0:T(8,128)(2,1)} %get-tuple-element.201), channel_id=1, source_target_pairs={{0,8},{4,12},{8,0},{12,4},{16,24},{20,28},{24,16},{28,20},{1,9},{5... | collective-permute-start | bytes 2211848 | tf_op jit(solution)/shard_map/ppermute | solution.py:1177
  218.6 39.6 %collective-permute-start.21 = (bf16[4,240,384]{2,1,0:T(8,128)(2,1)}, bf16[4,240,384]{2,1,0:T(8,128)(2,1)S(1)}, u32[]{:S(2)}, u32[]{:S(2)}) collective-permute-start(bf16[4,240,384]{2,1,0:T(8,128)(2,1)} %get-tuple-element.200), channel_id=1, source_target_pairs={{0,16},{4,20},{8,24},{12,28},{16,0},{20,4},{24,8},{28,12},{1,17},{... | collective-permute-start | bytes 2211848 | tf_op jit(solution)/shard_map/ppermute | solution.py:1177
  220.2 38.0 %collective-permute-start.22 = (bf16[4,240,384]{2,1,0:T(8,128)(2,1)}, bf16[4,240,384]{2,1,0:T(8,128)(2,1)S(1)}, u32[]{:S(2)}, u32[]{:S(2)}) collective-permute-start(bf16[4,240,384]{2,1,0:T(8,128)(2,1)} %get-tuple-element.199), channel_id=1, source_target_pairs={{0,24},{4,28},{8,16},{12,20},{16,8},{20,12},{24,0},{28,4},{1,25},{... | collective-permute-start | bytes 2211848 | tf_op jit(solution)/shard_map/ppermute | solution.py:1177
  258.6 5.5 %collective-permute-start.23 = (bf16[2,768,768]{2,1,0:T(8,128)(2,1)}, bf16[2,768,768]{2,1,0:T(8,128)(2,1)S(1)}, u32[]{:S(2)}, u32[]{:S(2)}) collective-permute-start(bf16[2,768,768]{2,1,0:T(8,128)(2,1)} %get-tuple-element.162), channel_id=1, source_target_pairs={{0,4},{4,0},{8,12},{12,8},{16,20},{20,16},{24,28},{28,24},{1,5},{5... | collective-permute-start | bytes 7077896 | tf_op jit(solution)/shard_map/ppermute | solution.py:1177
  258.8 18.5 %collective-permute-start.24 = (bf16[240,384]{1,0:T(8,128)(2,1)S(1)}, bf16[240,384]{1,0:T(8,128)(2,1)S(1)}, u32[]{:S(2)}, u32[]{:S(2)}) collective-permute-start(bf16[240,384]{1,0:T(8,128)(2,1)S(1)} %get-tuple-element.222), channel_id=1, source_target_pairs={{0,1},{1,0},{2,3},{3,2},{4,5},{5,4},{6,7},{7,6},{8,9},{9,8},{10,11... | collective-permute-start | bytes 552968 | tf_op jit(solution)/shard_map/ppermute | solution.py:1177
  260.3 16.9 %collective-permute-start.25 = (bf16[240,384]{1,0:T(8,128)(2,1)S(1)}, bf16[240,384]{1,0:T(8,128)(2,1)S(1)}, u32[]{:S(2)}, u32[]{:S(2)}) collective-permute-start(bf16[240,384]{1,0:T(8,128)(2,1)S(1)} %get-tuple-element.221), channel_id=1, source_target_pairs={{0,2},{1,3},{2,0},{3,1},{4,6},{5,7},{6,4},{7,5},{8,10},{9,11},{10,... | collective-permute-start | bytes 552968 | tf_op jit(solution)/shard_map/ppermute | solution.py:1177
  262.8 26.1 %collective-permute-start.26 = (bf16[240,384]{1,0:T(8,128)(2,1)S(1)}, bf16[240,384]{1,0:T(8,128)(2,1)S(1)}, u32[]{:S(2)}, u32[]{:S(2)}) collective-permute-start(bf16[240,384]{1,0:T(8,128)(2,1)S(1)} %get-tuple-element.220), channel_id=1, source_target_pairs={{0,3},{1,2},{2,1},{3,0},{4,7},{5,6},{6,5},{7,4},{8,11},{9,10},{10,... | collective-permute-start | bytes 552968 | tf_op jit(solution)/shard_map/ppermute | solution.py:1177
  265.5 29.9 %copy-start.6 = (bf16[768,2304]{1,0:T(8,128)(2,1)S(1)}, bf16[768,2304]{1,0:T(8,128)(2,1)}, u32[]{:S(2)}) copy-start(bf16[768,2304]{1,0:T(8,128)(2,1)} %w_in.1) | copy-start | bytes 10616836
  265.5 29.9 %copy-start.17 = (f32[1152,768]{1,0:T(8,128)S(1)}, f32[1152,768]{1,0:T(8,128)}, u32[]{:S(2)}) copy-start(f32[1152,768]{1,0:T(8,128)} %get-tuple-element.137.back_mid) | copy-start | bytes 10616836
  288.9 18.7 %collective-permute-start.27 = (bf16[240,384]{1,0:T(8,128)(2,1)S(1)}, bf16[240,384]{1,0:T(8,128)(2,1)S(1)}, u32[]{:S(2)}, u32[]{:S(2)}) collective-permute-start(bf16[240,384]{1,0:T(8,128)(2,1)S(1)} %add_convert_fusion.16), channel_id=1, source_target_pairs={{0,1},{1,0},{2,3},{3,2},{4,5},{5,4},{6,7},{7,6},{8,9},{9,8},{10,11... | collective-permute-start | bytes 552968 | tf_op jit(solution)/shard_map/ppermute | solution.py:1177
  292.9 16.1 %collective-permute-start.28 = (bf16[240,384]{1,0:T(8,128)(2,1)S(1)}, bf16[240,384]{1,0:T(8,128)(2,1)S(1)}, u32[]{:S(2)}, u32[]{:S(2)}) collective-permute-start(bf16[240,384]{1,0:T(8,128)(2,1)S(1)} %add_convert_fusion.16), channel_id=1, source_target_pairs={{0,2},{1,3},{2,0},{3,1},{4,6},{5,7},{6,4},{7,5},{8,10},{9,11},{10,... | collective-permute-start | bytes 552968 | tf_op jit(solution)/shard_map/ppermute | solution.py:1177
  292.9 16.1 %collective-permute-start.29 = (bf16[240,384]{1,0:T(8,128)(2,1)S(1)}, bf16[240,384]{1,0:T(8,128)(2,1)S(1)}, u32[]{:S(2)}, u32[]{:S(2)}) collective-permute-start(bf16[240,384]{1,0:T(8,128)(2,1)S(1)} %add_convert_fusion.16), channel_id=1, source_target_pairs={{0,3},{1,2},{2,1},{3,0},{4,7},{5,6},{6,5},{7,4},{8,11},{9,10},{10,... | collective-permute-start | bytes 552968 | tf_op jit(solution)/shard_map/ppermute | solution.py:1177
  295.4 19.6 %collective-permute-start.30 = (bf16[16,144,384]{2,1,0:T(8,128)(2,1)}, bf16[16,144,384]{2,1,0:T(8,128)(2,1)}, u32[]{:S(2)}, u32[]{:S(2)}) collective-permute-start(bf16[16,144,384]{2,1,0:T(8,128)(2,1)} %get-tuple-element.173), channel_id=1, source_target_pairs={{0,4},{4,0},{8,12},{12,8},{16,20},{20,16},{24,28},{28,24},{1,5},{5... | collective-permute-start | bytes 5308424 | tf_op jit(solution)/shard_map/ppermute | solution.py:1177
  313.3 19.2 %collective-permute-start.31 = (bf16[2,384,768]{2,1,0:T(8,128)(2,1)S(1)}, bf16[2,384,768]{2,1,0:T(8,128)(2,1)}, u32[]{:S(2)}, u32[]{:S(2)}) collective-permute-start(bf16[2,384,768]{2,1,0:T(8,128)(2,1)S(1)} %get-tuple-element.177), channel_id=1, source_target_pairs={{0,0},{1,1},{4,2},{5,3},{2,4},{3,5},{6,6},{7,7},{8,8},{9,9},{12,10... | collective-permute-start | bytes 3538952 | tf_op jit(solution)/shard_map/ppermute | solution.py:1289
  317.0 21.6 %collective-permute-start.34 = (bf16[4,160,384]{2,1,0:T(8,128)(2,1)S(1)}, bf16[4,160,384]{2,1,0:T(8,128)(2,1)S(1)}, u32[]{:S(2)}, u32[]{:S(2)}) collective-permute-start(bf16[4,160,384]{2,1,0:T(8,128)(2,1)S(1)} %pad_maximum_fusion.6), channel_id=1, source_target_pairs={{0,24},{4,28},{8,16},{12,20},{16,8},{20,12},{24,0},{28,4},{1,25},{... | collective-permute-start | bytes 1474568 | tf_op jit(solution)/shard_map/ppermute | solution.py:1177
  320.4 29.7 %collective-permute-start.33 = (bf16[4,160,384]{2,1,0:T(8,128)(2,1)}, bf16[4,160,384]{2,1,0:T(8,128)(2,1)S(1)}, u32[]{:S(2)}, u32[]{:S(2)}) collective-permute-start(bf16[4,160,384]{2,1,0:T(8,128)(2,1)} %pad_maximum_fusion.5), channel_id=1, source_target_pairs={{0,16},{4,20},{8,24},{12,28},{16,0},{20,4},{24,8},{28,12},{1,17},{... | collective-permute-start | bytes 1474568 | tf_op jit(solution)/shard_map/ppermute | solution.py:1177
  321.9 28.2 %collective-permute-start.32 = (bf16[4,160,384]{2,1,0:T(8,128)(2,1)}, bf16[4,160,384]{2,1,0:T(8,128)(2,1)S(1)}, u32[]{:S(2)}, u32[]{:S(2)}) collective-permute-start(bf16[4,160,384]{2,1,0:T(8,128)(2,1)} %pad_maximum_fusion.4), channel_id=1, source_target_pairs={{0,8},{4,12},{8,0},{12,4},{16,24},{20,28},{24,16},{28,20},{1,9},{5... | collective-permute-start | bytes 1474568 | tf_op jit(solution)/shard_map/ppermute | solution.py:1177
  327.6 22.5 %copy-start.29 = (bf16[4,160,384]{2,1,0:T(8,128)(2,1)S(1)}, bf16[4,160,384]{2,1,0:T(8,128)(2,1)}, u32[]{:S(2)}) copy-start(bf16[4,160,384]{2,1,0:T(8,128)(2,1)} %pad_maximum_fusion.3) | copy-start | bytes 1474564
  350.3 31.5 %copy-start.11 = (bf16[384,768]{1,0:T(8,128)(2,1)S(1)}, bf16[384,768]{1,0:T(8,128)(2,1)}, u32[]{:S(2)}) copy-start(bf16[384,768]{1,0:T(8,128)(2,1)} %copy-done.10) | copy-start | bytes 1769476
  350.4 5.9 %collective-permute-start.35 = (bf16[160,384]{1,0:T(8,128)(2,1)S(1)}, bf16[160,384]{1,0:T(8,128)(2,1)S(1)}, u32[]{:S(2)}, u32[]{:S(2)}) collective-permute-start(bf16[160,384]{1,0:T(8,128)(2,1)S(1)} %get-tuple-element.227), channel_id=1, source_target_pairs={{0,1},{1,0},{2,3},{3,2},{4,5},{5,4},{6,7},{7,6},{8,9},{9,8},{10,11... | collective-permute-start | bytes 368648 | tf_op jit(solution)/shard_map/ppermute | solution.py:1177
  352.6 11.6 %collective-permute-start.36 = (bf16[160,384]{1,0:T(8,128)(2,1)S(1)}, bf16[160,384]{1,0:T(8,128)(2,1)S(1)}, u32[]{:S(2)}, u32[]{:S(2)}) collective-permute-start(bf16[160,384]{1,0:T(8,128)(2,1)S(1)} %get-tuple-element.229), channel_id=1, source_target_pairs={{0,2},{1,3},{2,0},{3,1},{4,6},{5,7},{6,4},{7,5},{8,10},{9,11},{10,... | collective-permute-start | bytes 368648 | tf_op jit(solution)/shard_map/ppermute | solution.py:1177
  352.6 11.6 %collective-permute-start.37 = (bf16[160,384]{1,0:T(8,128)(2,1)S(1)}, bf16[160,384]{1,0:T(8,128)(2,1)S(1)}, u32[]{:S(2)}, u32[]{:S(2)}) collective-permute-start(bf16[160,384]{1,0:T(8,128)(2,1)S(1)} %get-tuple-element.228), channel_id=1, source_target_pairs={{0,3},{1,2},{2,1},{3,0},{4,7},{5,6},{6,5},{7,4},{8,11},{9,10},{10,... | collective-permute-start | bytes 368648 | tf_op jit(solution)/shard_map/ppermute | solution.py:1177
  364.2 6.2 %collective-permute-start.38 = (bf16[160,384]{1,0:T(8,128)(2,1)S(1)}, bf16[160,384]{1,0:T(8,128)(2,1)S(1)}, u32[]{:S(2)}, u32[]{:S(2)}) collective-permute-start(bf16[160,384]{1,0:T(8,128)(2,1)S(1)} %fusion.14), channel_id=1, source_target_pairs={{0,1},{1,0},{2,3},{3,2},{4,5},{5,4},{6,7},{7,6},{8,9},{9,8},{10,11... | collective-permute-start | bytes 368648 | tf_op jit(solution)/shard_map/ppermute | solution.py:1177
  366.7 11.4 %collective-permute-start.39 = (bf16[160,384]{1,0:T(8,128)(2,1)S(1)}, bf16[160,384]{1,0:T(8,128)(2,1)S(1)}, u32[]{:S(2)}, u32[]{:S(2)}) collective-permute-start(bf16[160,384]{1,0:T(8,128)(2,1)S(1)} %fusion.14), channel_id=1, source_target_pairs={{0,2},{1,3},{2,0},{3,1},{4,6},{5,7},{6,4},{7,5},{8,10},{9,11},{10,... | collective-permute-start | bytes 368648 | tf_op jit(solution)/shard_map/ppermute | solution.py:1177
  366.7 11.4 %collective-permute-start.40 = (bf16[160,384]{1,0:T(8,128)(2,1)S(1)}, bf16[160,384]{1,0:T(8,128)(2,1)S(1)}, u32[]{:S(2)}, u32[]{:S(2)}) collective-permute-start(bf16[160,384]{1,0:T(8,128)(2,1)S(1)} %fusion.14), channel_id=1, source_target_pairs={{0,3},{1,2},{2,1},{3,0},{4,7},{5,6},{6,5},{7,4},{8,11},{9,10},{10,... | collective-permute-start | bytes 368648 | tf_op jit(solution)/shard_map/ppermute | solution.py:1177
  378.2 5.8 %collective-permute-start.42 = (bf16[4,4,240,384]{3,2,1,0:T(8,128)(2,1)}, bf16[4,4,240,384]{3,2,1,0:T(8,128)(2,1)S(1)}, u32[]{:S(2)}, u32[]{:S(2)}) collective-permute-start(bf16[4,4,240,384]{3,2,1,0:T(8,128)(2,1)} %bitcast.105), channel_id=1, source_target_pairs={{0,4},{4,0},{8,12},{12,8},{16,20},{20,16},{24,28},{28,24},{1,5},{5... | collective-permute-start | bytes 8847368 | tf_op jit(solution)/shard_map/ppermute | solution.py:1177
  378.2 19.5 %collective-permute-start.43 = (bf16[4,160,384]{2,1,0:T(8,128)(2,1)S(1)}, bf16[4,160,384]{2,1,0:T(8,128)(2,1)S(1)}, u32[]{:S(2)}, u32[]{:S(2)}) collective-permute-start(bf16[4,160,384]{2,1,0:T(8,128)(2,1)S(1)} %pad_maximum_fusion.7), channel_id=1, source_target_pairs={{0,8},{4,12},{8,0},{12,4},{16,24},{20,28},{24,16},{28,20},{1,9},{5... | collective-permute-start | bytes 1474568 | tf_op jit(solution)/shard_map/ppermute | solution.py:1177
  379.7 23.8 %collective-permute-start.44 = (bf16[4,160,384]{2,1,0:T(8,128)(2,1)S(1)}, bf16[4,160,384]{2,1,0:T(8,128)(2,1)S(1)}, u32[]{:S(2)}, u32[]{:S(2)}) collective-permute-start(bf16[4,160,384]{2,1,0:T(8,128)(2,1)S(1)} %pad_maximum_fusion.7), channel_id=1, source_target_pairs={{0,16},{4,20},{8,24},{12,28},{16,0},{20,4},{24,8},{28,12},{1,17},{... | collective-permute-start | bytes 1474568 | tf_op jit(solution)/shard_map/ppermute | solution.py:1177
  380.2 23.3 %collective-permute-start.45 = (bf16[4,160,384]{2,1,0:T(8,128)(2,1)S(1)}, bf16[4,160,384]{2,1,0:T(8,128)(2,1)S(1)}, u32[]{:S(2)}, u32[]{:S(2)}) collective-permute-start(bf16[4,160,384]{2,1,0:T(8,128)(2,1)S(1)} %pad_maximum_fusion.7), channel_id=1, source_target_pairs={{0,24},{4,28},{8,16},{12,20},{16,8},{20,12},{24,0},{28,4},{1,25},{... | collective-permute-start | bytes 1474568 | tf_op jit(solution)/shard_map/ppermute | solution.py:1177
  381.8 15.9 %collective-permute-start.41 = (bf16[384,768]{1,0:T(8,128)(2,1)S(1)}, bf16[384,768]{1,0:T(8,128)(2,1)S(1)}, u32[]{:S(2)}, u32[]{:S(2)}) collective-permute-start(bf16[384,768]{1,0:T(8,128)(2,1)S(1)} %copy-done.11), channel_id=1, source_target_pairs={{1,0},{0,1},{5,2},{4,3},{3,4},{2,5},{7,6},{6,7},{9,8},{8,9},{13,10... | collective-permute-start | bytes 1769480 | tf_op jit(solution)/shard_map/ppermute | solution.py:1289
  403.8 4.0 collective-permute-start.46
  (32 other events, 176.1 us)
Sparse Core Ops, SparseCore 0:
  210.6 82.4 all-gather.4
  310.1 59.5 all-gather.6

commit v3 on v2

--- a/solution.py
+++ b/solution.py
@@ -1076,7 +1076,7 @@
             pltpu.VMEM(w.shape, w.dtype),
             pltpu.SemaphoreType.DMA((1,)),
         ],
-        compiler_params=limits(32),
+        compiler_params=limits(56),
         cost_estimate=lasting(9),
         name="input_back",
     )(where, *xs, vecs, w, back_mid, back, sums, gb1)
@@ -1357,20 +1357,20 @@
     send_c, keep_c, back = project_back(
         where, xs, vecs_one, dq_full, dq_short, own_full, got_full, keep_short, got_pair, got_near
     )
-    part_b = add_low(after(quarter_b[0], keep_c), *line_b)
+    i13, i2, line_sums = input_back(
+        where, xs, vecs_one, w_qkv, back_mid, back, feed_sums, gb1
+    )
+    part_b = add_low(after(quarter_b[0], i2), *line_b)
     got_c = swap(after(send_c, part_b), "dp", 1)
     near_b = over_line([part_b] * 4)
-    i13, i2, line_sums = input_back(
-        where, xs, vecs_one, w_qkv, back_mid, after(back, part_b), feed_sums, gb1
-    )
-    near_b = jnp.stack([after(part_b, i2)] + near_b)
-    half_b = lax.all_gather(near_b, "dp", axis=0, axis_index_groups=CHIPS)
     sums_c = [
         jnp.concatenate([total, line_sums[4 * k : 4 * k + 4]], axis=1)
-        for k, total in enumerate(by_chip(after(keep_c, i2, near_b), got_c))
+        for k, total in enumerate(by_chip(after(keep_c, i2, part_b), got_c))
     ]
+    near_b = jnp.stack([after(part_b, *sums_c)] + near_b)
+    half_b = lax.all_gather(near_b, "dp", axis=0, axis_index_groups=CHIPS)
     chips_c = over_chips(sums_c)
-    (i13_home,) = give((i13, None))[:1]
+    (i13_home,) = give((after(i13, *sums_c), None))[:1]
     output = arrange(after(home, *sums_c))
     all_a = after(all_a, *sums_c)
     halves_a = [all_a[:, c] for c in range(2)]

time: 423 us -> 424 us (level)
    ppermute x36, waiting for transfers between devices: 60.3 us -> 55.4 us  [swap(): return lax.ppermute(array, axis, flip_pairs(8 if axis == 'dp' else 4, mask))]
    pallas_call x1, Pallas kernels: 8.92 us -> 13.2 us  [input_back(): pl.pallas_call(input_back_kernel, grid=(3,), in_specs=[SMEM, pl.BlockSpec...]
    unnamed x94 -> x96, local copies, waits for them, and re-layouts: 9.7 us -> 9.86 us
  transfers between devices with their start and end apart: 49 -> 49, of which waited for: 16 -> 16; matrix products, arithmetic and copies ran while one was open for 6% -> 6% of each run, Pallas kernels for 35% -> 36%
where the time goes in v3:
time: 424 us; the launch traced here: 419 us
  Pallas kernels  195 us (46%)
  starting transfers between devices  103 us (24%)
  waiting for transfers between devices  69 us (16%)
  other arithmetic  18.6 us (4%)
  between operations  18 us (4%)
  local copies, waits for them, and re-layouts  14.6 us (3%)
    ppermute x36, starting transfers between devices, swap(): return lax.ppermute(array, axis, flip_pairs(8 if axis == 'dp' else 4, mask))  75.4 us
    ppermute x36, waiting for transfers between devices, swap(): return lax.ppermute(array, axis, flip_pairs(8 if axis == 'dp' else 4, mask))  55.4 us
    pallas_call x2, Pallas kernels, attend_back(): pl.pallas_call(functools.partial(attend_back_kernel, pieces=len(kvs), val...  53.5 us
    pallas_call x1, Pallas kernels, feed(): pl.pallas_call(functools.partial(feed_kernel, steps=steps, tile=tile), gr...  34 us
    pallas_call x2, Pallas kernels, attend(): pl.pallas_call(functools.partial(attend_kernel, pieces=len(kvs), valid=va...  29.6 us
    pallas_call x1, Pallas kernels, feed_back(): pl.pallas_call(functools.partial(feed_back_kernel, steps=steps), grid=(st...  23.7 us
    pallas_call x4, Pallas kernels, finish(): pl.pallas_call(functools.partial(finish_kernel, with_lines=with_lines), g...  15.7 us
    pallas_call x1, Pallas kernels, input_back(): pl.pallas_call(input_back_kernel, grid=(3,), in_specs=[SMEM, pl.BlockSpec...  13.2 us
  transfers between devices with their start and end apart: 49, of which 16 were waited for; matrix products, arithmetic and copies ran while one was open for 6% of the time, Pallas kernels for 36%

profile of v3, /device:TPU:0, one launch (start us, length us, event | category | flops | bytes accessed | tf_op | source)
XLA Modules:
  0.0 419.0 jit_solution(7519965418360126193)
XLA Ops:
  7.3 3.5 leave.2
  10.8 1.9 collective-permute-start
  12.7 3.0 collective-permute-start.1
  16.0 3.3 leave.3
  19.3 2.0 copy-done.7
  21.7 8.4 %collective-permute-done.1.x2_in.x2 = bf16[384,768]{1,0:T(8,128)(2,1)S(1)} collective-permute-done((bf16[384,768]{1,0:T(8,128)(2,1)}, bf16[384,768]{1,0:T(8,128)(2,1)S(1)}, u32[]{:S(2)}, u32[]{:S(2)}) %collective-permute-start.1) | collective-permute-done | bytes 589856 | tf_op jit(solution)/shard_map/ppermute | solution.py:1281
  30.0 5.0 %project.1 = (bf16[768,768]{1,0:T(8,128)(2,1)S(1)}, bf16[2,768,768]{2,1,0:T(8,128)(2,1)}) custom-call(bf16[2,384,768]{2,1,0:T(8,128)(2,1)S(1)} %collective-permute-done.x13_in.x13, bf16[384,768]{1,0:T(8,128)(2,1)S(1)} %collective-permute-done.1.x2_in.x2, f32[4,768]{1,0:T(4,128)S(1)} %get-tuple-element.235.vecs, bf16[768,2304]{1,0:T(8,128)(2,1)S(1)} %get-tuple-element.114.w_in), custom_call_target="tpu_custom_call" | custom-call | flops 4000000000 | bytes 1048576 | tf_op jit(solution)/shard_map/project/pallas_call | solution.py:461
  36.1 20.0 %collective-permute-start.2 = (bf16[2,768,768]{2,1,0:T(8,128)(2,1)}, bf16[2,768,768]{2,1,0:T(8,128)(2,1)}, u32[]{:S(2)}, u32[]{:S(2)}) collective-permute-start(bf16[2,768,768]{2,1,0:T(8,128)(2,1)} %get-tuple-element.116.refs_1_.refs_5_), channel_id=1, source_target_pairs={{0,4},{4,0},{8,12},{12,8},{16,20},{20,16},{24,28},{28,24},{1,5},{5... | collective-permute-start | bytes 7077896 | tf_op jit(solution)/shard_map/ppermute | solution.py:1177
  56.2 8.9 %collective-permute-start.3 = (bf16[384,768]{1,0:T(8,128)(2,1)S(1)}, bf16[384,768]{1,0:T(8,128)(2,1)S(1)}, u32[]{:S(2)}, u32[]{:S(2)}) collective-permute-start(bf16[384,768]{1,0:T(8,128)(2,1)S(1)} %slice_bitcast_fusion.2), channel_id=1, source_target_pairs={{0,1},{1,0},{2,3},{3,2},{4,5},{6,7},{8,9},{9,8},{10,11},{11,10},{1... | collective-permute-start | bytes 1769480 | tf_op jit(solution)/shard_map/ppermute | solution.py:1166
  65.1 1.9 collective-permute-start.4
  67.0 1.3 collective-permute-start.5
  68.4 2.4 collective-permute-start.6
  70.8 2.8 collective-permute-start.7
  74.9 21.1 %attend.2 = (f32[768,768]{1,0:T(8,128)S(1)}, bf16[768,768]{1,0:T(8,128)(2,1)S(1)}) custom-call(bf16[768,768]{1,0:T(8,128)(2,1)S(1)} %copy-done.17, bf16[2,768,768]{2,1,0:T(8,128)(2,1)} %get-tuple-element.116.refs_1_.refs_5_, bf16[2,768,768]{2,1,0:T(8,128)(2,1)} %collective-permute-done.2.refs_2_.refs_6_), custom_call_target="tpu_custom_call" | custom-call | flops 24999999488 | bytes 1048576 | tf_op jit(solution)/shard_map/attend/pallas_call | solution.py:605
  96.0 4.3 %project_short.1 = (bf16[384,768]{1,0:T(8,128)(2,1)S(1)}, bf16[2,768,768]{2,1,0:T(8,128)(2,1)S(1)}, bf16[2,128,768]{2,1,0:T(8,128)(2,1)S(1)}) custom-call(s32[3]{0:T(128)S(1)} %get-tuple-element.198.where.refs_0_, bf16[2,384,768]{2,1,0:T(8,128)(2,1)S(1)} %collective-permute-done.x13_in.x13, bf16[384,768]{1,0:T(8,128)(2,1)S(1)} %collective-permute-done.3.near, ...), custom_call_target="tpu_custom_call" | custom-call | flops 4000000000 | bytes 1048576 | tf_op jit(solution)/shard_map/project_short/pallas_call | solution.py:496
  100.3 8.5 %attend.3 = (f32[384,768]{1,0:T(8,128)S(1)}, bf16[384,768]{1,0:T(8,128)(2,1)S(1)}) custom-call(bf16[384,768]{1,0:T(8,128)(2,1)S(1)} %get-tuple-element.141.refs_0_.refs_1_, bf16[2,768,768]{2,1,0:T(8,128)(2,1)S(1)} %get-tuple-element.122.refs_1_.refs_5_, bf16[2,128,768]{2,1,0:T(8,128)(2,1)S(1)} %get-tuple-element.123.refs_2_.refs_6_), custom_call_target="tpu_custom_call" | custom-call | flops 7000000000 | bytes 1048576 | tf_op jit(solution)/shard_map/attend/pallas_call | solution.py:605
  108.9 34.0 %feed.1 = (bf16[2,384,768]{2,1,0:T(8,128)(2,1)S(1)}, bf16[384,768]{1,0:T(8,128)(2,1)S(1)}, f32[1152,768]{1,0:T(8,128)}, bf16[1152,768]{1,0:T(8,128)(2,1)S(1)}, b...) custom-call(s32[3]{0:T(128)S(1)} %get-tuple-element.198.where.refs_0, ...), custom_call_target="tpu_custom_call" | custom-call | flops 35999997952 | bytes 1048576 | tf_op jit(solution)/shard_map/feed/pallas_call | solution.py:804
  142.9 6.6 %collective-permute-start.9 = (bf16[16,192,384]{2,1,0:T(8,128)(2,1)S(1)}, bf16[16,192,384]{2,1,0:T(8,128)(2,1)S(1)}, u32[]{:S(2)}, u32[]{:S(2)}) collective-permute-start(bf16[16,192,384]{2,1,0:T(8,128)(2,1)S(1)} %get-tuple-element.133), channel_id=1, source_target_pairs={{0,4},{4,0},{8,12},{12,8},{16,20},{20,16},{24,28},{28,24},{1,5},{5... | collective-permute-start | bytes 7077896 | tf_op jit(solution)/shard_map/ppermute | solution.py:1177
  150.4 3.4 collective-permute-done.9
  154.4 1.6 collective-permute-start.11
  156.0 1.5 collective-permute-start.12
  158.0 23.7 %feed_back.1 = (bf16[1152,768]{1,0:T(8,128)(2,1)S(1)}, f32[1152,768]{1,0:T(8,128)}, bf16[16,240,384]{2,1,0:T(8,128)(2,1)}, bf16[16,240,384]{2,1,0:T(8,128)(2,1)S(1)}, f32[8,768]{1,0:T(8,128)S(1)}) custom-call(s32[3]{0:T(128)S(1)} %get-tuple-element.198.where.refs_0_, f32[768,768]{1,0:T(8,128)S(1)} %copy-done.27, ...), custom_call_target="tpu_custom_call" | custom-call | flops 25999998976 | bytes 1048576 | tf_op jit(solution)/shard_map/feed_back/pallas_call | solution.py:903
  183.3 9.8 %collective-permute-start.15 = (bf16[192,384]{1,0:T(8,128)(2,1)S(1)}, bf16[192,384]{1,0:T(8,128)(2,1)S(1)}, u32[]{:S(2)}, u32[]{:S(2)}) collective-permute-start(bf16[192,384]{1,0:T(8,128)(2,1)S(1)} %get-tuple-element.225), channel_id=1, source_target_pairs={{0,2},{1,3},{2,0},{3,1},{4,6},{5,7},{6,4},{7,5},{8,10},{9,11},{10,... | collective-permute-start | bytes 442376 | tf_op jit(solution)/shard_map/ppermute | solution.py:1177
  193.1 16.0 %attend_back.2 = (bf16[384,768]{1,0:T(8,128)(2,1)}, bf16[2,768,768]{2,1,0:T(8,128)(2,1)}, bf16[2,768,768]{2,1,0:T(8,128)(2,1)}) custom-call(s32[3]{0:T(128)} %copy-done.4, bf16[384,768]{1,0:T(8,128)(2,1)} %copy-done.18, bf16[1152,768]{1,0:T(8,128)(2,1)} %copy-done.23, f32[384,768]{1,0:T(8,128)} %copy-done.21, bf16[384,768]{1,0:T(8,128)(2,1)} %copy-done.24, ...), custom_call_target="tpu_custom_call" | custom-call | flops 11000000512 | bytes 1048576 | tf_op jit(solution)/shard_map/attend_back/pallas_call | solution.py:693
  210.8 3.8 add_convert_fusion.2
  214.8 1.6 add_convert_fusion
  217.0 1.5 collective-permute-start.20
  218.5 1.6 collective-permute-start.21
  220.5 37.5 %attend_back.3 = (bf16[768,768]{1,0:T(8,128)(2,1)}, bf16[2,768,768]{2,1,0:T(8,128)(2,1)}, bf16[2,768,768]{2,1,0:T(8,128)(2,1)}) custom-call(s32[3]{0:T(128)} %copy-done.4, bf16[768,768]{1,0:T(8,128)(2,1)} %copy-done.16, bf16[1152,768]{1,0:T(8,128)(2,1)} %copy-done.23, f32[768,768]{1,0:T(8,128)} %copy-done.26, bf16[768,768]{1,0:T(8,128)(2,1)} %copy-done.28, ...), custom_call_target="tpu_custom_call" | custom-call | flops 38999998464 | bytes 1048576 | tf_op jit(solution)/shard_map/attend_back/pallas_call | solution.py:693
  259.1 1.5 collective-permute-start.24
  260.7 2.4 collective-permute-start.25
  263.1 1.4 collective-permute-start.26
  267.1 9.6 %project_back.1 = (bf16[16,144,384]{2,1,0:T(8,128)(2,1)S(1)}, bf16[16,144,384]{2,1,0:T(8,128)(2,1)S(1)}, bf16[3,1152,768]{2,1,0:T(8,128)(2,1)}) custom-call(s32[3]{0:T(128)S(1)} %copy-done.5, bf16[2,384,768]{2,1,0:T(8,128)(2,1)S(1)} %copy-done.2, bf16[384,768]{1,0:T(8,128)(2,1)S(1)} %copy-done.12, f32[4,768]{1,0:T(4,128)S(1)} %get-tuple-element.235.vecs, ...), custom_call_target="tpu_custom_call" | custom-call | flops 11000000512 | bytes 1048576 | tf_op jit(solution)/shard_map/project_back/pallas_call | solution.py:984
  276.6 13.2 %input_back.1 = (bf16[2,384,768]{2,1,0:T(8,128)(2,1)}, bf16[384,768]{1,0:T(8,128)(2,1)}, bf16[16,16,384]{2,1,0:T(8,128)(2,1)}) custom-call(s32[3]{0:T(128)} %copy-done.4, bf16[2,384,768]{2,1,0:T(8,128)(2,1)} %copy-done.1, bf16[384,768]{1,0:T(8,128)(2,1)} %copy-done.11, f32[4,768]{1,0:T(4,128)} %copy-done.3, bf16[768,2304]{1,0:T(8,128)(2,1)} %w_in.1, ...), custom_call_target="tpu_custom_call" | custom-call | flops 8999999488 | bytes 1048576 | tf_op jit(solution)/shard_map/input_back/pallas_call | solution.py:1054
  290.1 2.8 collective-permute-start.39
  292.9 1.5 collective-permute-start.40
  294.4 1.5 collective-permute-start.41
  299.8 1.9 collective-permute-done.39
  301.7 7.5 %collective-permute-done.40 = bf16[240,384]{1,0:T(8,128)(2,1)S(1)} collective-permute-done((bf16[240,384]{1,0:T(8,128)(2,1)S(1)}, bf16[240,384]{1,0:T(8,128)(2,1)S(1)}, u32[]{:S(2)}, u32[]{:S(2)}) %collective-permute-start.40) | collective-permute-done | bytes 184352 | tf_op jit(solution)/shard_map/ppermute | solution.py:1177
  313.4 2.4 collective-permute-start.31
  317.0 1.9 collective-permute-start.28
  318.9 1.3 fusion.7
  320.3 1.4 pad_maximum_fusion.1
  321.7 3.0 slice_bitcast_fusion
  324.6 4.9 %finish.4 = f32[3072,768]{1,0:T(8,128)} custom-call(s32[3]{0:T(128)S(1)} %broadcast_1_where.2.where, bf16[4,4,192,384]{3,2,1,0:T(8,128)(2,1)S(1)} %get-tuple-element.204.mine, bf16[4,4,192,384]{3,2,1,0:T(8,128)(2,1)S(1)} %get-tuple-element.203.other), custom_call_target="tpu_custom_call" | custom-call | flops 4000000000 | bytes 1048576 | tf_op jit(solution)/shard_map/finish/pallas_call | solution.py:1122
  329.5 4.9 %collective-permute-done.31 = bf16[4,160,384]{2,1,0:T(8,128)(2,1)S(1)} collective-permute-done((bf16[4,160,384]{2,1,0:T(8,128)(2,1)}, bf16[4,160,384]{2,1,0:T(8,128)(2,1)S(1)}, u32[]{:S(2)}, u32[]{:S(2)}) %collective-permute-start.31) | collective-permute-done | bytes 491552 | tf_op jit(solution)/shard_map/ppermute | solution.py:1177
  334.5 10.4 %collective-permute-done.30 = bf16[4,160,384]{2,1,0:T(8,128)(2,1)} collective-permute-done((bf16[4,160,384]{2,1,0:T(8,128)(2,1)}, bf16[4,160,384]{2,1,0:T(8,128)(2,1)}, u32[]{:S(2)}, u32[]{:S(2)}) %collective-permute-start.30) | collective-permute-done | bytes 491552 | tf_op jit(solution)/shard_map/ppermute | solution.py:1177
  345.0 1.5 add_convert_fusion.11
  346.5 4.5 %collective-permute-start.32 = (bf16[160,384]{1,0:T(8,128)(2,1)S(1)}, bf16[160,384]{1,0:T(8,128)(2,1)S(1)}, u32[]{:S(2)}, u32[]{:S(2)}) collective-permute-start(bf16[160,384]{1,0:T(8,128)(2,1)S(1)} %get-tuple-element.227), channel_id=1, source_target_pairs={{0,1},{1,0},{2,3},{3,2},{4,5},{5,4},{6,7},{7,6},{8,9},{9,8},{10,11... | collective-permute-start | bytes 368648 | tf_op jit(solution)/shard_map/ppermute | solution.py:1177
  351.0 2.4 collective-permute-start.33
  354.7 8.6 %collective-permute-done.33 = bf16[160,384]{1,0:T(8,128)(2,1)S(1)} collective-permute-done((bf16[160,384]{1,0:T(8,128)(2,1)S(1)}, bf16[160,384]{1,0:T(8,128)(2,1)S(1)}, u32[]{:S(2)}, u32[]{:S(2)}) %collective-permute-start.33) | collective-permute-done | bytes 122912 | tf_op jit(solution)/shard_map/ppermute | solution.py:1177
  363.4 3.0 collective-permute-start.35
  366.6 2.3 collective-permute-start.37
  370.1 7.9 %collective-permute-done.36 = bf16[160,384]{1,0:T(8,128)(2,1)S(1)} collective-permute-done((bf16[160,384]{1,0:T(8,128)(2,1)S(1)}, bf16[160,384]{1,0:T(8,128)(2,1)S(1)}, u32[]{:S(2)}, u32[]{:S(2)}) %collective-permute-start.36) | collective-permute-done | bytes 122912 | tf_op jit(solution)/shard_map/ppermute | solution.py:1177
  378.2 1.5 collective-permute-start.43
  381.8 2.5 collective-permute-start.38
  384.3 1.8 copy-done
  386.1 2.1 finish.6
  388.2 4.7 %finish.5 = f32[768,3072]{1,0:T(8,128)} custom-call(s32[3]{0:T(128)S(1)} %get-tuple-element.197.where, bf16[4,4,240,384]{3,2,1,0:T(8,128)(2,1)S(1)} %bitcast.107, bf16[4,4,240,384]{3,2,1,0:T(8,128)(2,1)S(1)} %collective-permute-done.42.other), custom_call_target="tpu_custom_call" | custom-call | flops 4000000000 | bytes 1048576 | tf_op jit(solution)/shard_map/finish/pallas_call | solution.py:1122
  392.9 5.1 %collective-permute-done.38 = bf16[384,768]{1,0:T(8,128)(2,1)S(1)} collective-permute-done((bf16[384,768]{1,0:T(8,128)(2,1)S(1)}, bf16[384,768]{1,0:T(8,128)(2,1)S(1)}, u32[]{:S(2)}, u32[]{:S(2)}) %collective-permute-start.38) | collective-permute-done | bytes 589856 | tf_op jit(solution)/shard_map/ppermute | solution.py:1289
  398.0 5.5 %collective-permute-done.44 = bf16[4,160,384]{2,1,0:T(8,128)(2,1)S(1)} collective-permute-done((bf16[4,160,384]{2,1,0:T(8,128)(2,1)S(1)}, bf16[4,160,384]{2,1,0:T(8,128)(2,1)S(1)}, u32[]{:S(2)}, u32[]{:S(2)}) %collective-permute-start.44) | collective-permute-done | bytes 491552 | tf_op jit(solution)/shard_map/ppermute | solution.py:1177
  404.1 2.1 maximum_convert_fusion
  406.2 1.7 collective-permute-done.46.other.refs_1_
  407.9 4.0 finish.7
  (190 shorter events, 25.6 us)
Async XLA Ops:
  7.2 314.5 %all-gather.5.cloned.1.call-start = ((), (), s32[]{:S(2)}) async-start(), calls=%async_computation | async-start | bytes 4866048 | tf_op jit(solution)/shard_map/all_gather | solution.py:1240
  10.8 10.8 %collective-permute-start = (bf16[2,384,768]{2,1,0:T(8,128)(2,1)}, bf16[2,384,768]{2,1,0:T(8,128)(2,1)S(1)}, u32[]{:S(2)}, u32[]{:S(2)}) collective-permute-start(bf16[2,384,768]{2,1,0:T(8,128)(2,1)} %get-tuple-element.106), channel_id=1, source_target_pairs={{0,0},{1,1},{2,4},{3,5},{4,2},{5,3},{6,6},{7,7},{8,8},{9,9},{10,12... | collective-permute-start | bytes 3538952 | tf_op jit(solution)/shard_map/ppermute | solution.py:1281
  12.7 17.3 %collective-permute-start.1 = (bf16[384,768]{1,0:T(8,128)(2,1)}, bf16[384,768]{1,0:T(8,128)(2,1)S(1)}, u32[]{:S(2)}, u32[]{:S(2)}) collective-permute-start(bf16[384,768]{1,0:T(8,128)(2,1)} %get-tuple-element.107), channel_id=1, source_target_pairs={{0,1},{1,0},{2,5},{3,4},{4,3},{5,2},{6,7},{7,6},{8,9},{9,8},{10,13... | collective-permute-start | bytes 1769480 | tf_op jit(solution)/shard_map/ppermute | solution.py:1281
  21.6 13.5 %copy-start.13 = (bf16[768,2304]{1,0:T(8,128)(2,1)}, bf16[768,2304]{1,0:T(8,128)(2,1)S(1)}, u32[]{:S(2)}) copy-start(bf16[768,2304]{1,0:T(8,128)(2,1)S(1)} %get-tuple-element.114.w_in) | copy-start | bytes 10616836
  21.6 242.9 %copy-start.3 = (f32[4,768]{1,0:T(4,128)}, f32[4,768]{1,0:T(4,128)S(1)}, u32[]{:S(2)}) copy-start(f32[4,768]{1,0:T(4,128)S(1)} %get-tuple-element.235.vecs) | copy-start | bytes 36868
  21.6 87.3 %copy-start.1 = (bf16[2,384,768]{2,1,0:T(8,128)(2,1)}, bf16[2,384,768]{2,1,0:T(8,128)(2,1)S(1)}, u32[]{:S(2)}) copy-start(bf16[2,384,768]{2,1,0:T(8,128)(2,1)S(1)} %collective-permute-done.x13_in.x13) | copy-start | bytes 3538948
  30.0 78.9 %copy-start.11 = (bf16[384,768]{1,0:T(8,128)(2,1)}, bf16[384,768]{1,0:T(8,128)(2,1)S(1)}, u32[]{:S(2)}) copy-start(bf16[384,768]{1,0:T(8,128)(2,1)S(1)} %collective-permute-done.1.x2_in.x2) | copy-start | bytes 1769476
  30.0 26.1 %copy-start.44 = (s32[3]{0:T(128)S(1)}, s32[3]{0:T(128)}, u32[]{:S(2)}) copy-start(s32[3]{0:T(128)} %constant.58.clone) | copy-start | bytes 40
  30.0 26.1 %copy-start.45 = (s32[3]{0:T(128)S(1)}, s32[3]{0:T(128)}, u32[]{:S(2)}) copy-start(s32[3]{0:T(128)} %constant.59.clone) | copy-start | bytes 40
  30.0 40.8 %copy-start.47 = (bf16[384,768]{1,0:T(8,128)(2,1)S(1)}, bf16[384,768]{1,0:T(8,128)(2,1)}, u32[]{:S(2)}) copy-start(bf16[384,768]{1,0:T(8,128)(2,1)} %get-tuple-element.126) | copy-start | bytes 1769476
  36.1 34.7 %collective-permute-start.2 = (bf16[2,768,768]{2,1,0:T(8,128)(2,1)}, bf16[2,768,768]{2,1,0:T(8,128)(2,1)}, u32[]{:S(2)}, u32[]{:S(2)}) collective-permute-start(bf16[2,768,768]{2,1,0:T(8,128)(2,1)} %get-tuple-element.116.refs_1_.refs_5_), channel_id=1, source_target_pairs={{0,4},{4,0},{8,12},{12,8},{16,20},{20,16},{24,28},{28,24},{1,5},{5... | collective-permute-start | bytes 7077896 | tf_op jit(solution)/shard_map/ppermute | solution.py:1177
  56.2 101.8 %copy-start.4 = (s32[3]{0:T(128)}, s32[3]{0:T(128)S(1)}, u32[]{:S(2)}) copy-start(s32[3]{0:T(128)S(1)} %get-tuple-element.198.where.refs_0_) | copy-start | bytes 40
  56.2 39.8 %collective-permute-start.3 = (bf16[384,768]{1,0:T(8,128)(2,1)S(1)}, bf16[384,768]{1,0:T(8,128)(2,1)S(1)}, u32[]{:S(2)}, u32[]{:S(2)}) collective-permute-start(bf16[384,768]{1,0:T(8,128)(2,1)S(1)} %slice_bitcast_fusion.2), channel_id=1, source_target_pairs={{0,1},{1,0},{2,3},{3,2},{4,5},{6,7},{8,9},{9,8},{10,11},{11,10},{1... | collective-permute-start | bytes 1769480 | tf_op jit(solution)/shard_map/ppermute | solution.py:1166
  65.1 30.9 %collective-permute-start.4 = (bf16[384,768]{1,0:T(8,128)(2,1)S(1)}, bf16[384,768]{1,0:T(8,128)(2,1)S(1)}, u32[]{:S(2)}, u32[]{:S(2)}) collective-permute-start(bf16[384,768]{1,0:T(8,128)(2,1)S(1)} %slice_bitcast_fusion.2), channel_id=1, source_target_pairs={{0,4},{1,5},{2,6},{3,7},{4,0},{6,2},{8,12},{9,13},{10,14},{11,15},... | collective-permute-start | bytes 1769480 | tf_op jit(solution)/shard_map/ppermute | solution.py:1166
  67.0 29.0 %collective-permute-start.5 = (bf16[384,768]{1,0:T(8,128)(2,1)S(1)}, bf16[384,768]{1,0:T(8,128)(2,1)S(1)}, u32[]{:S(2)}, u32[]{:S(2)}) collective-permute-start(bf16[384,768]{1,0:T(8,128)(2,1)S(1)} %slice_bitcast_fusion.2), channel_id=1, source_target_pairs={{0,5},{1,4},{2,7},{3,6},{4,1},{6,3},{8,13},{9,12},{10,15},{11,14},... | collective-permute-start | bytes 1769480 | tf_op jit(solution)/shard_map/ppermute | solution.py:1166
  68.4 40.5 %collective-permute-start.6 = (bf16[2,384,768]{2,1,0:T(8,128)(2,1)}, bf16[2,384,768]{2,1,0:T(8,128)(2,1)S(1)}, u32[]{:S(2)}, u32[]{:S(2)}) collective-permute-start(bf16[2,384,768]{2,1,0:T(8,128)(2,1)} %get-tuple-element.125), channel_id=1, source_target_pairs={{0,0},{1,1},{2,4},{3,5},{4,2},{5,3},{6,6},{7,7},{8,8},{9,9},{10,12... | collective-permute-start | bytes 3538952 | tf_op jit(solution)/shard_map/ppermute | solution.py:1281
  70.8 38.1 %collective-permute-start.7 = (bf16[384,768]{1,0:T(8,128)(2,1)S(1)}, bf16[384,768]{1,0:T(8,128)(2,1)S(1)}, u32[]{:S(2)}, u32[]{:S(2)}) collective-permute-start(bf16[384,768]{1,0:T(8,128)(2,1)S(1)} %copy-done.47), channel_id=1, source_target_pairs={{0,1},{1,0},{2,5},{3,4},{4,3},{5,2},{6,7},{7,6},{8,9},{9,8},{10,13... | collective-permute-start | bytes 1769480 | tf_op jit(solution)/shard_map/ppermute | solution.py:1281
  74.9 21.1 %copy-start.14 = (bf16[768,2304]{1,0:T(8,128)(2,1)S(1)}, bf16[768,2304]{1,0:T(8,128)(2,1)}, u32[]{:S(2)}) copy-start(bf16[768,2304]{1,0:T(8,128)(2,1)} %copy-done.13) | copy-start | bytes 10616836
  108.9 34.0 %copy-start.24 = (bf16[384,768]{1,0:T(8,128)(2,1)}, bf16[384,768]{1,0:T(8,128)(2,1)S(1)}, u32[]{:S(2)}) copy-start(bf16[384,768]{1,0:T(8,128)(2,1)S(1)} %get-tuple-element.143.refs_4_) | copy-start | bytes 1769476
  108.9 49.1 %copy-start.21 = (f32[384,768]{1,0:T(8,128)}, f32[384,768]{1,0:T(8,128)S(1)}, u32[]{:S(2)}) copy-start(f32[384,768]{1,0:T(8,128)S(1)} %get-tuple-element.124.att_short_in.refs_3_) | copy-start | bytes 3538948
  142.9 11.5 %copy-start.30 = (f32[1,3072]{1,0:T(1,128)}, f32[1,3072]{1,0:T(1,128)S(1)}, u32[]{:S(2)}) copy-start(f32[1,3072]{1,0:T(1,128)S(1)} %get-tuple-element.166.gb1) | copy-start | bytes 36868
  142.9 10.8 %collective-permute-start.9 = (bf16[16,192,384]{2,1,0:T(8,128)(2,1)S(1)}, bf16[16,192,384]{2,1,0:T(8,128)(2,1)S(1)}, u32[]{:S(2)}, u32[]{:S(2)}) collective-permute-start(bf16[16,192,384]{2,1,0:T(8,128)(2,1)S(1)} %get-tuple-element.133), channel_id=1, source_target_pairs={{0,4},{4,0},{8,12},{12,8},{16,20},{20,16},{24,28},{28,24},{1,5},{5... | collective-permute-start | bytes 7077896 | tf_op jit(solution)/shard_map/ppermute | solution.py:1177
  149.6 32.1 %collective-permute-start.8 = (bf16[2,384,768]{2,1,0:T(8,128)(2,1)S(1)}, bf16[2,384,768]{2,1,0:T(8,128)(2,1)S(1)}, u32[]{:S(2)}, u32[]{:S(2)}) collective-permute-start(bf16[2,384,768]{2,1,0:T(8,128)(2,1)S(1)} %get-tuple-element.130), channel_id=1, source_target_pairs={{0,0},{1,1},{4,2},{5,3},{2,4},{3,5},{6,6},{7,7},{8,8},{9,9},{12,10... | collective-permute-start | bytes 3538952 | tf_op jit(solution)/shard_map/ppermute | solution.py:1289
  150.3 58.7 %collective-permute-start.10 = (bf16[384,768]{1,0:T(8,128)(2,1)S(1)}, bf16[384,768]{1,0:T(8,128)(2,1)}, u32[]{:S(2)}, u32[]{:S(2)}) collective-permute-start(bf16[384,768]{1,0:T(8,128)(2,1)S(1)} %get-tuple-element.139), channel_id=1, source_target_pairs={{1,0},{0,1},{5,2},{4,3},{3,4},{2,5},{7,6},{6,7},{9,8},{8,9},{13,10... | collective-permute-start | bytes 1769480 | tf_op jit(solution)/shard_map/ppermute | solution.py:1289
  154.4 27.3 %collective-permute-start.11 = (bf16[4,192,384]{2,1,0:T(8,128)(2,1)S(1)}, bf16[4,192,384]{2,1,0:T(8,128)(2,1)S(1)}, u32[]{:S(2)}, u32[]{:S(2)}) collective-permute-start(bf16[4,192,384]{2,1,0:T(8,128)(2,1)S(1)} %get-tuple-element.207), channel_id=1, source_target_pairs={{0,8},{4,12},{8,0},{12,4},{16,24},{20,28},{24,16},{28,20},{1,9},{5... | collective-permute-start | bytes 1769480 | tf_op jit(solution)/shard_map/ppermute | solution.py:1177
  156.0 25.8 %collective-permute-start.12 = (bf16[4,192,384]{2,1,0:T(8,128)(2,1)S(1)}, bf16[4,192,384]{2,1,0:T(8,128)(2,1)S(1)}, u32[]{:S(2)}, u32[]{:S(2)}) collective-permute-start(bf16[4,192,384]{2,1,0:T(8,128)(2,1)S(1)} %get-tuple-element.206), channel_id=1, source_target_pairs={{0,16},{4,20},{8,24},{12,28},{16,0},{20,4},{24,8},{28,12},{1,17},{... | collective-permute-start | bytes 1769480 | tf_op jit(solution)/shard_map/ppermute | solution.py:1177
  157.5 24.9 %collective-permute-start.13 = (bf16[4,192,384]{2,1,0:T(8,128)(2,1)S(1)}, bf16[4,192,384]{2,1,0:T(8,128)(2,1)S(1)}, u32[]{:S(2)}, u32[]{:S(2)}) collective-permute-start(bf16[4,192,384]{2,1,0:T(8,128)(2,1)S(1)} %get-tuple-element.205), channel_id=1, source_target_pairs={{0,24},{4,28},{8,16},{12,20},{16,8},{20,12},{24,0},{28,4},{1,25},{... | collective-permute-start | bytes 1769480 | tf_op jit(solution)/shard_map/ppermute | solution.py:1177
  183.3 25.8 %collective-permute-start.14 = (bf16[192,384]{1,0:T(8,128)(2,1)S(1)}, bf16[192,384]{1,0:T(8,128)(2,1)S(1)}, u32[]{:S(2)}, u32[]{:S(2)}) collective-permute-start(bf16[192,384]{1,0:T(8,128)(2,1)S(1)} %get-tuple-element.226), channel_id=1, source_target_pairs={{0,1},{1,0},{2,3},{3,2},{4,5},{5,4},{6,7},{7,6},{8,9},{9,8},{10,11... | collective-permute-start | bytes 442376 | tf_op jit(solution)/shard_map/ppermute | solution.py:1177
  183.3 25.8 %collective-permute-start.15 = (bf16[192,384]{1,0:T(8,128)(2,1)S(1)}, bf16[192,384]{1,0:T(8,128)(2,1)S(1)}, u32[]{:S(2)}, u32[]{:S(2)}) collective-permute-start(bf16[192,384]{1,0:T(8,128)(2,1)S(1)} %get-tuple-element.225), channel_id=1, source_target_pairs={{0,2},{1,3},{2,0},{3,1},{4,6},{5,7},{6,4},{7,5},{8,10},{9,11},{10,... | collective-permute-start | bytes 442376 | tf_op jit(solution)/shard_map/ppermute | solution.py:1177
  193.1 16.0 %collective-permute-start.16 = (bf16[192,384]{1,0:T(8,128)(2,1)S(1)}, bf16[192,384]{1,0:T(8,128)(2,1)S(1)}, u32[]{:S(2)}, u32[]{:S(2)}) collective-permute-start(bf16[192,384]{1,0:T(8,128)(2,1)S(1)} %get-tuple-element.224), channel_id=1, source_target_pairs={{0,3},{1,2},{2,1},{3,0},{4,7},{5,6},{6,5},{7,4},{8,11},{9,10},{10,... | collective-permute-start | bytes 442376 | tf_op jit(solution)/shard_map/ppermute | solution.py:1177
  193.1 17.7 %collective-permute-start.18 = (bf16[16,240,384]{2,1,0:T(8,128)(2,1)}, bf16[16,240,384]{2,1,0:T(8,128)(2,1)}, u32[]{:S(2)}, u32[]{:S(2)}) collective-permute-start(bf16[16,240,384]{2,1,0:T(8,128)(2,1)} %get-tuple-element.153), channel_id=1, source_target_pairs={{0,4},{4,0},{8,12},{12,8},{16,20},{20,16},{24,28},{28,24},{1,5},{5... | collective-permute-start | bytes 8847368 | tf_op jit(solution)/shard_map/ppermute | solution.py:1177
  209.8 5.0 %collective-permute-start.17 = (bf16[2,768,768]{2,1,0:T(8,128)(2,1)}, bf16[2,768,768]{2,1,0:T(8,128)(2,1)}, u32[]{:S(2)}, u32[]{:S(2)}) collective-permute-start(bf16[2,768,768]{2,1,0:T(8,128)(2,1)} %get-tuple-element.149), channel_id=1, source_target_pairs={{0,4},{4,0},{8,12},{12,8},{16,20},{20,16},{24,28},{28,24},{1,5},{5... | collective-permute-start | bytes 7077896 | tf_op jit(solution)/shard_map/ppermute | solution.py:1177
  210.3 167.8 %all-gather.7.cloned.1.call-start = ((), (), s32[]{:S(2)}) async-start(), calls=%async_computation.1 | async-start | bytes 3686400 | tf_op jit(solution)/shard_map/all_gather | solution.py:1371
  216.4 41.7 %collective-permute-start.19 = (bf16[2,384,768]{2,1,0:T(8,128)(2,1)S(1)}, bf16[2,384,768]{2,1,0:T(8,128)(2,1)S(1)}, u32[]{:S(2)}, u32[]{:S(2)}) collective-permute-start(bf16[2,384,768]{2,1,0:T(8,128)(2,1)S(1)} %add_convert_fusion), channel_id=1, source_target_pairs={{0,1},{1,0},{2,3},{3,2},{4,5},{5,4},{6,7},{7,6},{8,9},{9,8},{10,11... | collective-permute-start | bytes 3538952 | tf_op jit(solution)/shard_map/ppermute | solution.py:1177
  217.0 41.1 %collective-permute-start.20 = (bf16[4,240,384]{2,1,0:T(8,128)(2,1)}, bf16[4,240,384]{2,1,0:T(8,128)(2,1)S(1)}, u32[]{:S(2)}, u32[]{:S(2)}) collective-permute-start(bf16[4,240,384]{2,1,0:T(8,128)(2,1)} %get-tuple-element.201), channel_id=1, source_target_pairs={{0,8},{4,12},{8,0},{12,4},{16,24},{20,28},{24,16},{28,20},{1,9},{5... | collective-permute-start | bytes 2211848 | tf_op jit(solution)/shard_map/ppermute | solution.py:1177
  218.5 39.6 %collective-permute-start.21 = (bf16[4,240,384]{2,1,0:T(8,128)(2,1)}, bf16[4,240,384]{2,1,0:T(8,128)(2,1)S(1)}, u32[]{:S(2)}, u32[]{:S(2)}) collective-permute-start(bf16[4,240,384]{2,1,0:T(8,128)(2,1)} %get-tuple-element.200), channel_id=1, source_target_pairs={{0,16},{4,20},{8,24},{12,28},{16,0},{20,4},{24,8},{28,12},{1,17},{... | collective-permute-start | bytes 2211848 | tf_op jit(solution)/shard_map/ppermute | solution.py:1177
  220.1 38.0 %collective-permute-start.22 = (bf16[4,240,384]{2,1,0:T(8,128)(2,1)}, bf16[4,240,384]{2,1,0:T(8,128)(2,1)S(1)}, u32[]{:S(2)}, u32[]{:S(2)}) collective-permute-start(bf16[4,240,384]{2,1,0:T(8,128)(2,1)} %get-tuple-element.199), channel_id=1, source_target_pairs={{0,24},{4,28},{8,16},{12,20},{16,8},{20,12},{24,0},{28,4},{1,25},{... | collective-permute-start | bytes 2211848 | tf_op jit(solution)/shard_map/ppermute | solution.py:1177
  259.1 5.4 %collective-permute-start.23 = (bf16[2,768,768]{2,1,0:T(8,128)(2,1)}, bf16[2,768,768]{2,1,0:T(8,128)(2,1)S(1)}, u32[]{:S(2)}, u32[]{:S(2)}) collective-permute-start(bf16[2,768,768]{2,1,0:T(8,128)(2,1)} %get-tuple-element.162), channel_id=1, source_target_pairs={{0,4},{4,0},{8,12},{12,8},{16,20},{20,16},{24,28},{28,24},{1,5},{5... | collective-permute-start | bytes 7077896 | tf_op jit(solution)/shard_map/ppermute | solution.py:1177
  259.1 30.7 %collective-permute-start.24 = (bf16[240,384]{1,0:T(8,128)(2,1)S(1)}, bf16[240,384]{1,0:T(8,128)(2,1)S(1)}, u32[]{:S(2)}, u32[]{:S(2)}) collective-permute-start(bf16[240,384]{1,0:T(8,128)(2,1)S(1)} %get-tuple-element.222), channel_id=1, source_target_pairs={{0,1},{1,0},{2,3},{3,2},{4,5},{5,4},{6,7},{7,6},{8,9},{9,8},{10,11... | collective-permute-start | bytes 552968 | tf_op jit(solution)/shard_map/ppermute | solution.py:1177
  260.7 29.2 %collective-permute-start.25 = (bf16[240,384]{1,0:T(8,128)(2,1)S(1)}, bf16[240,384]{1,0:T(8,128)(2,1)S(1)}, u32[]{:S(2)}, u32[]{:S(2)}) collective-permute-start(bf16[240,384]{1,0:T(8,128)(2,1)S(1)} %get-tuple-element.221), channel_id=1, source_target_pairs={{0,2},{1,3},{2,0},{3,1},{4,6},{5,7},{6,4},{7,5},{8,10},{9,11},{10,... | collective-permute-start | bytes 552968 | tf_op jit(solution)/shard_map/ppermute | solution.py:1177
  263.1 26.8 %collective-permute-start.26 = (bf16[240,384]{1,0:T(8,128)(2,1)S(1)}, bf16[240,384]{1,0:T(8,128)(2,1)S(1)}, u32[]{:S(2)}, u32[]{:S(2)}) collective-permute-start(bf16[240,384]{1,0:T(8,128)(2,1)S(1)} %get-tuple-element.220), channel_id=1, source_target_pairs={{0,3},{1,2},{2,1},{3,0},{4,7},{5,6},{6,5},{7,4},{8,11},{9,10},{10,... | collective-permute-start | bytes 552968 | tf_op jit(solution)/shard_map/ppermute | solution.py:1177
  290.0 6.7 %collective-permute-start.27 = (bf16[16,144,384]{2,1,0:T(8,128)(2,1)S(1)}, bf16[16,144,384]{2,1,0:T(8,128)(2,1)S(1)}, u32[]{:S(2)}, u32[]{:S(2)}) collective-permute-start(bf16[16,144,384]{2,1,0:T(8,128)(2,1)S(1)} %get-tuple-element.171), channel_id=1, source_target_pairs={{0,4},{4,0},{8,12},{12,8},{16,20},{20,16},{24,28},{28,24},{1,5},{5... | collective-permute-start | bytes 5308424 | tf_op jit(solution)/shard_map/ppermute | solution.py:1177
  290.1 11.6 %collective-permute-start.39 = (bf16[240,384]{1,0:T(8,128)(2,1)S(1)}, bf16[240,384]{1,0:T(8,128)(2,1)S(1)}, u32[]{:S(2)}, u32[]{:S(2)}) collective-permute-start(bf16[240,384]{1,0:T(8,128)(2,1)S(1)} %add_convert_fusion.16), channel_id=1, source_target_pairs={{0,1},{1,0},{2,3},{3,2},{4,5},{5,4},{6,7},{7,6},{8,9},{9,8},{10,11... | collective-permute-start | bytes 552968 | tf_op jit(solution)/shard_map/ppermute | solution.py:1177
  292.9 16.3 %collective-permute-start.40 = (bf16[240,384]{1,0:T(8,128)(2,1)S(1)}, bf16[240,384]{1,0:T(8,128)(2,1)S(1)}, u32[]{:S(2)}, u32[]{:S(2)}) collective-permute-start(bf16[240,384]{1,0:T(8,128)(2,1)S(1)} %add_convert_fusion.16), channel_id=1, source_target_pairs={{0,2},{1,3},{2,0},{3,1},{4,6},{5,7},{6,4},{7,5},{8,10},{9,11},{10,... | collective-permute-start | bytes 552968 | tf_op jit(solution)/shard_map/ppermute | solution.py:1177
  294.4 14.8 %collective-permute-start.41 = (bf16[240,384]{1,0:T(8,128)(2,1)S(1)}, bf16[240,384]{1,0:T(8,128)(2,1)S(1)}, u32[]{:S(2)}, u32[]{:S(2)}) collective-permute-start(bf16[240,384]{1,0:T(8,128)(2,1)S(1)} %add_convert_fusion.16), channel_id=1, source_target_pairs={{0,3},{1,2},{2,1},{3,0},{4,7},{5,6},{6,5},{7,4},{8,11},{9,10},{10,... | collective-permute-start | bytes 552968 | tf_op jit(solution)/shard_map/ppermute | solution.py:1177
  299.7 10.5 %copy-start.35 = (s32[3]{0:T(128)S(1)}, s32[3]{0:T(128)}, u32[]{:S(2)}) copy-start(s32[3]{0:T(128)} %counts.3) | copy-start | bytes 40
  299.7 19.2 %copy-start.32 = (bf16[2,384,768]{2,1,0:T(8,128)(2,1)S(1)}, bf16[2,384,768]{2,1,0:T(8,128)(2,1)}, u32[]{:S(2)}) copy-start(bf16[2,384,768]{2,1,0:T(8,128)(2,1)} %copy-done.31) | copy-start | bytes 3538948
  313.4 21.0 %collective-permute-start.31 = (bf16[4,160,384]{2,1,0:T(8,128)(2,1)}, bf16[4,160,384]{2,1,0:T(8,128)(2,1)S(1)}, u32[]{:S(2)}, u32[]{:S(2)}) collective-permute-start(bf16[4,160,384]{2,1,0:T(8,128)(2,1)} %pad_maximum_fusion.6), channel_id=1, source_target_pairs={{0,24},{4,28},{8,16},{12,20},{16,8},{20,12},{24,0},{28,4},{1,25},{... | collective-permute-start | bytes 1474568 | tf_op jit(solution)/shard_map/ppermute | solution.py:1177
  315.9 29.0 %collective-permute-start.30 = (bf16[4,160,384]{2,1,0:T(8,128)(2,1)}, bf16[4,160,384]{2,1,0:T(8,128)(2,1)}, u32[]{:S(2)}, u32[]{:S(2)}) collective-permute-start(bf16[4,160,384]{2,1,0:T(8,128)(2,1)} %pad_maximum_fusion.5), channel_id=1, source_target_pairs={{0,16},{4,20},{8,24},{12,28},{16,0},{20,4},{24,8},{28,12},{1,17},{... | collective-permute-start | bytes 1474568 | tf_op jit(solution)/shard_map/ppermute | solution.py:1177
  316.4 28.5 %collective-permute-start.29 = (bf16[4,160,384]{2,1,0:T(8,128)(2,1)}, bf16[4,160,384]{2,1,0:T(8,128)(2,1)}, u32[]{:S(2)}, u32[]{:S(2)}) collective-permute-start(bf16[4,160,384]{2,1,0:T(8,128)(2,1)} %pad_maximum_fusion.4), channel_id=1, source_target_pairs={{0,8},{4,12},{8,0},{12,4},{16,24},{20,28},{24,16},{28,20},{1,9},{5... | collective-permute-start | bytes 1474568 | tf_op jit(solution)/shard_map/ppermute | solution.py:1177
  317.0 12.5 %collective-permute-start.28 = (bf16[2,384,768]{2,1,0:T(8,128)(2,1)}, bf16[2,384,768]{2,1,0:T(8,128)(2,1)S(1)}, u32[]{:S(2)}, u32[]{:S(2)}) collective-permute-start(bf16[2,384,768]{2,1,0:T(8,128)(2,1)} %get-tuple-element.176), channel_id=1, source_target_pairs={{0,0},{1,1},{4,2},{5,3},{2,4},{3,5},{6,6},{7,7},{8,8},{9,9},{12,10... | collective-permute-start | bytes 3538952 | tf_op jit(solution)/shard_map/ppermute | solution.py:1289
  346.5 35.3 %copy-start.46 = (bf16[384,768]{1,0:T(8,128)(2,1)S(1)}, bf16[384,768]{1,0:T(8,128)(2,1)}, u32[]{:S(2)}) copy-start(bf16[384,768]{1,0:T(8,128)(2,1)} %get-tuple-element.180) | copy-start | bytes 1769476
  346.5 8.2 %collective-permute-start.32 = (bf16[160,384]{1,0:T(8,128)(2,1)S(1)}, bf16[160,384]{1,0:T(8,128)(2,1)S(1)}, u32[]{:S(2)}, u32[]{:S(2)}) collective-permute-start(bf16[160,384]{1,0:T(8,128)(2,1)S(1)} %get-tuple-element.227), channel_id=1, source_target_pairs={{0,1},{1,0},{2,3},{3,2},{4,5},{5,4},{6,7},{7,6},{8,9},{9,8},{10,11... | collective-permute-start | bytes 368648 | tf_op jit(solution)/shard_map/ppermute | solution.py:1177
  351.0 12.3 %collective-permute-start.33 = (bf16[160,384]{1,0:T(8,128)(2,1)S(1)}, bf16[160,384]{1,0:T(8,128)(2,1)S(1)}, u32[]{:S(2)}, u32[]{:S(2)}) collective-permute-start(bf16[160,384]{1,0:T(8,128)(2,1)S(1)} %get-tuple-element.229), channel_id=1, source_target_pairs={{0,2},{1,3},{2,0},{3,1},{4,6},{5,7},{6,4},{7,5},{8,10},{9,11},{10,... | collective-permute-start | bytes 368648 | tf_op jit(solution)/shard_map/ppermute | solution.py:1177
  353.4 10.0 %collective-permute-start.34 = (bf16[160,384]{1,0:T(8,128)(2,1)S(1)}, bf16[160,384]{1,0:T(8,128)(2,1)S(1)}, u32[]{:S(2)}, u32[]{:S(2)}) collective-permute-start(bf16[160,384]{1,0:T(8,128)(2,1)S(1)} %get-tuple-element.228), channel_id=1, source_target_pairs={{0,3},{1,2},{2,1},{3,0},{4,7},{5,6},{6,5},{7,4},{8,11},{9,10},{10,... | collective-permute-start | bytes 368648 | tf_op jit(solution)/shard_map/ppermute | solution.py:1177
  363.4 6.7 %collective-permute-start.35 = (bf16[160,384]{1,0:T(8,128)(2,1)S(1)}, bf16[160,384]{1,0:T(8,128)(2,1)S(1)}, u32[]{:S(2)}, u32[]{:S(2)}) collective-permute-start(bf16[160,384]{1,0:T(8,128)(2,1)S(1)} %fusion.14), channel_id=1, source_target_pairs={{0,1},{1,0},{2,3},{3,2},{4,5},{5,4},{6,7},{7,6},{8,9},{9,8},{10,11... | collective-permute-start | bytes 368648 | tf_op jit(solution)/shard_map/ppermute | solution.py:1177
  366.4 11.6 %collective-permute-start.36 = (bf16[160,384]{1,0:T(8,128)(2,1)S(1)}, bf16[160,384]{1,0:T(8,128)(2,1)S(1)}, u32[]{:S(2)}, u32[]{:S(2)}) collective-permute-start(bf16[160,384]{1,0:T(8,128)(2,1)S(1)} %fusion.14), channel_id=1, source_target_pairs={{0,2},{1,3},{2,0},{3,1},{4,6},{5,7},{6,4},{7,5},{8,10},{9,11},{10,... | collective-permute-start | bytes 368648 | tf_op jit(solution)/shard_map/ppermute | solution.py:1177
  366.6 11.5 %collective-permute-start.37 = (bf16[160,384]{1,0:T(8,128)(2,1)S(1)}, bf16[160,384]{1,0:T(8,128)(2,1)S(1)}, u32[]{:S(2)}, u32[]{:S(2)}) collective-permute-start(bf16[160,384]{1,0:T(8,128)(2,1)S(1)} %fusion.14), channel_id=1, source_target_pairs={{0,3},{1,2},{2,1},{3,0},{4,7},{5,6},{6,5},{7,4},{8,11},{9,10},{10,... | collective-permute-start | bytes 368648 | tf_op jit(solution)/shard_map/ppermute | solution.py:1177
  378.1 6.2 %collective-permute-start.42 = (bf16[4,4,240,384]{3,2,1,0:T(8,128)(2,1)}, bf16[4,4,240,384]{3,2,1,0:T(8,128)(2,1)S(1)}, u32[]{:S(2)}, u32[]{:S(2)}) collective-permute-start(bf16[4,4,240,384]{3,2,1,0:T(8,128)(2,1)} %bitcast.105), channel_id=1, source_target_pairs={{0,4},{4,0},{8,12},{12,8},{16,20},{20,16},{24,28},{28,24},{1,5},{5... | collective-permute-start | bytes 8847368 | tf_op jit(solution)/shard_map/ppermute | solution.py:1177
  378.2 19.8 %collective-permute-start.43 = (bf16[4,160,384]{2,1,0:T(8,128)(2,1)S(1)}, bf16[4,160,384]{2,1,0:T(8,128)(2,1)S(1)}, u32[]{:S(2)}, u32[]{:S(2)}) collective-permute-start(bf16[4,160,384]{2,1,0:T(8,128)(2,1)S(1)} %pad_maximum_fusion.7), channel_id=1, source_target_pairs={{0,8},{4,12},{8,0},{12,4},{16,24},{20,28},{24,16},{28,20},{1,9},{5... | collective-permute-start | bytes 1474568 | tf_op jit(solution)/shard_map/ppermute | solution.py:1177
  379.7 23.8 %collective-permute-start.44 = (bf16[4,160,384]{2,1,0:T(8,128)(2,1)S(1)}, bf16[4,160,384]{2,1,0:T(8,128)(2,1)S(1)}, u32[]{:S(2)}, u32[]{:S(2)}) collective-permute-start(bf16[4,160,384]{2,1,0:T(8,128)(2,1)S(1)} %pad_maximum_fusion.7), channel_id=1, source_target_pairs={{0,16},{4,20},{8,24},{12,28},{16,0},{20,4},{24,8},{28,12},{1,17},{... | collective-permute-start | bytes 1474568 | tf_op jit(solution)/shard_map/ppermute | solution.py:1177
  381.0 22.5 %collective-permute-start.45 = (bf16[4,160,384]{2,1,0:T(8,128)(2,1)S(1)}, bf16[4,160,384]{2,1,0:T(8,128)(2,1)S(1)}, u32[]{:S(2)}, u32[]{:S(2)}) collective-permute-start(bf16[4,160,384]{2,1,0:T(8,128)(2,1)S(1)} %pad_maximum_fusion.7), channel_id=1, source_target_pairs={{0,24},{4,28},{8,16},{12,20},{16,8},{20,12},{24,0},{28,4},{1,25},{... | collective-permute-start | bytes 1474568 | tf_op jit(solution)/shard_map/ppermute | solution.py:1177
  381.8 16.2 %collective-permute-start.38 = (bf16[384,768]{1,0:T(8,128)(2,1)S(1)}, bf16[384,768]{1,0:T(8,128)(2,1)S(1)}, u32[]{:S(2)}, u32[]{:S(2)}) collective-permute-start(bf16[384,768]{1,0:T(8,128)(2,1)S(1)} %copy-done.46), channel_id=1, source_target_pairs={{1,0},{0,1},{5,2},{4,3},{3,4},{2,5},{7,6},{6,7},{9,8},{8,9},{13,10... | collective-permute-start | bytes 1769480 | tf_op jit(solution)/shard_map/ppermute | solution.py:1289
  403.9 4.0 collective-permute-start.46
  (33 other events, 177.5 us)
Sparse Core Ops, SparseCore 0:
  210.5 83.8 all-gather.4
  310.3 58.7 all-gather.6
